TPU v7x, 32 devices: a whole 2x2x4 slice. The times are simulated.
32 devices in a mesh: groups: 2 (over y), gx: 8 (over z, x), gy: 2 (over core).
Axes of the slice: x: 2, y: 2, z: 4, core: 2. Of those that a mesh axis runs over, the one named last changes fastest.
Arguments:
- tokens: bfloat16 [2, 384, 8192], P(None, ('groups', 'gx'), 'gy'), parts along dimension 1, may hold values from -6 to 6
- gate_up: bfloat16 [2, 8192, 3328], P(None, ('gx', 'gy')), may hold values from -0.0625 to 0.0625
- down_weight: bfloat16 [3328, 8192], P(('gx', 'gy')), may hold values from -0.109375 to 0.109375
Outputs:
- mixed: bfloat16 [2, 384, 8192], P(None, ('groups', 'gx'), 'gy'), parts along dimension 1
There are 2 independent parts, one for each index of `groups`. A program takes and returns all parts, laid end to end along the dimension named above; an argument that names none is the same for every part. Nothing has to cross between parts.
All inputs are finite; a program needn't handle non-finite values.
Results may differ from a plain program's by a relative error of at most 0.005.
Values may be sent and summed in bfloat16 or wider, within the bound.
No kernel may reach another device: no remote copies, remote signals or barrier semaphores. Data moves between devices by JAX's collectives and lax.ppermute only.
A program may use at most 128 MiB of HBM per device.

v0:
```python
import functools

import jax
import jax.numpy as jnp
from jax import lax
from jax.experimental import pallas as pl
from jax.experimental.pallas import tpu as pltpu
from jax.sharding import PartitionSpec as P

LANES = 128
QUAD = 4
VMEM = 56 * 1024 * 1024


def wire_type(stage, stages):
    return jnp.bfloat16 if stages - stage <= 3 else jnp.float32


def place(relative, order, send, keep, value):
    first = (relative >> order[0]) & 1
    second = (relative >> order[1]) & 1
    group = 0 if send.shape[0] == 1 else relative >> 2

    @pl.when(first == 1)
    def _():
        send[group, second] = value.astype(send.dtype)

    @pl.when(first == 0)
    def _():
        keep[group, second] = value


def project_kernel(block, cuts, place_ref, tokens, own, other, *refs):
    outs, acc = refs[:-1], refs[-1]
    chip, core = place_ref[0], place_ref[1]
    chips, each = tokens.shape[0] // cuts[-1][1], cuts[-1][1]
    depth = own.shape[1]
    low, high = tokens[:, :depth], tokens[:, depth:]
    acc[...] = jnp.dot(
        jnp.where(core == 0, low, high), own[0], preferred_element_type=jnp.float32
    ) + jnp.dot(jnp.where(core == 0, high, low), other[0], preferred_element_type=jnp.float32)
    whole_tiles, rest = block // LANES, block % LANES
    fold = LANES // rest
    for index, (first, last, order) in enumerate(cuts):
        count = chips * (last - first)
        part = count // fold
        lane = lax.broadcasted_iota(jnp.int32, (count, LANES), 1)

        def tile(at):
            lanes = slice(at * LANES, (at + 1) * LANES)
            if count == tokens.shape[0]:
                return acc[:, lanes]
            return jnp.concatenate(
                [acc[chip * each + first : chip * each + last, lanes] for chip in range(chips)]
            )

        for q in range(QUAD):
            base = q * block
            shift = base % LANES
            pieces = []
            for piece in range(whole_tiles):
                at = base // LANES + piece
                value = tile(at)
                if shift:
                    value = jnp.where(lane < shift, tile(at + 1), value)
                    value = pltpu.roll(value, LANES - shift, 1)
                pieces.append(value)
            tail = base + whole_tiles * LANES
            rests = tile(tail // LANES)
            packed = None
            for k in range(fold):
                value = rests[k * part : (k + 1) * part]
                turn = (k * rest - tail % LANES) % LANES
                if turn:
                    value = pltpu.roll(value, turn, 1)
                packed = value if k == 0 else jnp.where(lane[:part] < k * rest, packed, value)
            pieces.append(packed)
            place(
                q ^ (chip & (QUAD - 1)),
                order,
                outs[2 * index],
                outs[2 * index + 1],
                jnp.concatenate(pieces),
            )


def project(spot, tokens, own, other, count_x, cuts, stages):
    block = own.shape[2] // count_x
    rows, depth = tokens.shape[0], own.shape[1]
    wide = QUAD * block
    groups = count_x // QUAD
    shapes, specs = [], []
    for first, last, _ in cuts:
        lines = count_x * (last - first) * block // LANES
        for kind in (wire_type(0, stages), jnp.float32):
            shapes.append(jax.ShapeDtypeStruct((groups, 2, 2, lines, LANES), kind))
            specs.append(
                pl.BlockSpec((1, 2, None, lines, LANES), lambda g, h, s: (g ^ (s[0] >> 2), 0, h, 0, 0))
            )
    weights = pl.BlockSpec((1, depth, wide), lambda g, h, s: (h, 0, g))
    return pl.pallas_call(
        functools.partial(project_kernel, block, cuts),
        out_shape=shapes,
        grid_spec=pltpu.PrefetchScalarGridSpec(
            num_scalar_prefetch=1,
            grid=(groups, 2),
            in_specs=[pl.BlockSpec(tokens.shape, lambda g, h, s: (0, 0)), weights, weights],
            out_specs=specs,
            scratch_shapes=[pltpu.VMEM((rows, wide), jnp.float32)],
        ),
        compiler_params=pltpu.CompilerParams(vmem_limit_bytes=VMEM),
        cost_estimate=pl.CostEstimate(
            flops=8 * rows * depth * own.shape[2], bytes_accessed=4 * own.size, transcendentals=0
        ),
    )(spot, tokens, own, other)


def down_kernel(block, count, order, place_ref, keep_in, recv_in, down, send, keep, hidden):
    chip = place_ref[0]
    whole_tiles, rest = block // LANES, block % LANES
    fold = LANES // rest

    @pl.when(pl.program_id(0) == 0)
    def _():
        gate = keep_in[0] + recv_in[0].astype(jnp.float32)
        upper = keep_in[1] + recv_in[1].astype(jnp.float32)
        value = gate / (1.0 + jnp.exp(-gate)) * upper
        for piece in range(whole_tiles):
            hidden[:, piece * LANES : (piece + 1) * LANES] = value[
                piece * count : (piece + 1) * count
            ].astype(jnp.bfloat16)
        packed = value[whole_tiles * count :]
        part = count // fold
        for k in range(fold):
            turned = pltpu.roll(packed, (LANES - k * rest) % LANES, 1) if k else packed
            hidden[k * part : (k + 1) * part, whole_tiles * LANES :] = turned[:, :rest].astype(jnp.bfloat16)

    product = jnp.dot(hidden[...], down[...], preferred_element_type=jnp.float32)
    chips = 4 * send.shape[0]
    each = count // chips
    for owner in range(chips):
        place(owner ^ chip, order, send, keep, product[owner * each : (owner + 1) * each])


def down_project(spot, keep, recv, down, count, order, count_x, stages, span=(0, 1), wide=2048):
    block, features = down.shape
    part, parts = span
    features = features // parts
    wide = min(wide, features)
    groups = count_x // QUAD
    each = count // count_x
    whole = pl.BlockSpec(keep.shape, lambda c, s: (0, 0, 0))
    out = pl.BlockSpec((groups, 2, each, wide), lambda c, s: (0, 0, 0, c))
    return pl.pallas_call(
        functools.partial(down_kernel, block, count, order),
        out_shape=[
            jax.ShapeDtypeStruct((groups, 2, each, features), kind)
            for kind in (wire_type(0, stages), jnp.float32)
        ],
        grid_spec=pltpu.PrefetchScalarGridSpec(
            num_scalar_prefetch=1,
            grid=(features // wide,),
            in_specs=[
                whole,
                whole,
                pl.BlockSpec((block, wide), lambda c, s: (0, part * (features // wide) + c)),
            ],
            out_specs=[out, out],
            scratch_shapes=[pltpu.VMEM((count, block), jnp.bfloat16)],
        ),
        compiler_params=pltpu.CompilerParams(vmem_limit_bytes=VMEM),
        cost_estimate=pl.CostEstimate(
            flops=2 * count * block * features, bytes_accessed=2 * block * features, transcendentals=0
        ),
    )(spot, keep, recv, down)


def swap(value, bit):
    count = lax.axis_size("gx")
    return lax.ppermute(value, "gx", [(i, i ^ (1 << bit)) for i in range(count)])


def swap_cores(value):
    return lax.ppermute(value, "gy", [(0, 1), (1, 0)])


def after(value, done):
    return value if done is None else lax.optimization_barrier((value, done))[0]


def halving(send, keep, order, stages, done, narrow_last=True):
    recv = swap(send, order[0])
    done = yield send
    for stage in range(1, stages):
        acc = keep + after(recv, done).astype(jnp.float32)
        kind = wire_type(stage, stages)
        if stage == stages - 1 and not narrow_last:
            kind = jnp.float32
        if stage == 1:
            send, keep, bit = acc[:, 1].astype(kind), acc[:, 0], order[1]
        else:
            half = acc.shape[0] // 2
            send, keep, bit = acc[half:].astype(kind), acc[:half], 1 + half.bit_length()
        recv = swap(send, bit)
        done = yield send
    return keep[0], after(recv, done)[0]


def chunk_steps(spot, parts, down, cut, count_x, stages, narrow_last):
    first, last, order = cut
    core = spot[1]
    keep, recv = yield from halving(parts[0], parts[1], order, stages, None, narrow_last)
    count = count_x * (last - first)
    send, keep = down_project(spot, keep, recv, down, count, order, count_x, stages)
    keep, recv = yield from halving(send, keep, order, stages, None)
    mixed = (keep + recv.astype(jnp.float32)).astype(jnp.bfloat16)
    halves = mixed.reshape(mixed.shape[0], 2, -1)
    mine = lax.dynamic_index_in_dim(halves, core, 1, False)
    send = lax.dynamic_index_in_dim(halves, 1 - core, 1, False)
    theirs = swap_cores(send)
    yield send
    return jnp.where(core == 0, jnp.stack([mine, theirs]), jnp.stack([theirs, mine]))


def local(tokens, gate_up, down_weight):
    count_x = lax.axis_size("gx")
    stages = count_x.bit_length() - 1
    chip, core = lax.axis_index("gx"), lax.axis_index("gy")
    spot = jnp.stack([chip, core]).astype(jnp.int32)
    each = tokens.shape[1]
    depth = gate_up.shape[1]

    mine = lax.dynamic_index_in_dim(tokens, core, 0, False)
    theirs = swap_cores(lax.dynamic_index_in_dim(tokens, 1 - core, 0, False))
    other = swap_cores(after(gate_up, theirs))
    down_other = swap_cores(after(down_weight, theirs))
    rows = jnp.where(core == 0, jnp.stack([mine, theirs]), jnp.stack([theirs, mine]))
    rows = rows.reshape(2, each, count_x // 2, 2 * depth).transpose(0, 2, 1, 3)
    rows = rows.reshape(count_x, each, 2 * depth)
    rows = lax.all_to_all(rows, "gx", 0, 0).reshape(count_x * each, 2 * depth)

    step = 8 if each % 8 == 0 else each
    cuts = tuple((a, a + step, (0, 1)) for a in range(0, each, step))
    down = jnp.where(
        core == 0,
        jnp.concatenate([down_weight, down_other]),
        jnp.concatenate([down_other, down_weight]),
    )
    parts = project(spot, rows, gate_up, other, count_x, cuts, stages)
    chunks = [
        chunk_steps(spot, parts[2 * i : 2 * i + 2], down, cut, count_x, stages, i == 0)
        for i, cut in enumerate(cuts)
    ]
    turns = sorted((turn + 1.6 * i, i) for i in range(len(cuts)) for turn in range(2 * stages + 2))
    done, results = None, {}
    for _, i in turns:
        try:
            done = chunks[i].send(done if i in results else None)
            results[i] = None
        except StopIteration as end:
            results[i] = end.value
    return jnp.concatenate([results[i] for i in range(len(cuts))], axis=1)


def solution(mesh):
    return jax.shard_map(
        local,
        mesh=mesh,
        in_specs=(
            P(None, ("groups", "gx"), "gy"),
            P(None, ("gx", "gy"), None),
            P(("gx", "gy"), None),
        ),
        out_specs=P(None, ("groups", "gx"), "gy"),
        check_vma=False,
    )
```

profile of v0, /device:TPU:0, one launch (start us, length us, event | category | flops | bytes accessed | tf_op | source)
XLA Modules:
  0.0 150.3 jit_solution(8944241436408879080)
XLA Ops:
  0.0 1.7 %constant_dynamic-slice_fusion = (bf16[1,24,4096]{2,1,0:T(8,128)(2,1)}, bf16[24,4096]{1,0:T(8,128)(2,1)S(1)}) fusion(bf16[2,24,4096]{2,1,0:T(8,128)(2,1)} %param.3, s32[]{:T(128)S(6)} %select_n.48, s32[]{:T(128)S(6)} %select_n.49), kind=kLoop, calls=%fused_computation.57 | loop fusion | bytes 786440 | tf_op jit(solution)/shard_map/jit(dynamic_index_in_dim)/dynamic_slice | solution.py:233
  1.7 0.5 collective-permute-start
  2.2 1.1 collective-permute-done
  3.2 0.7 copy-done.6
  3.9 0.4 collective-permute-start.1
  4.3 0.1 collective-permute-start.6
  4.4 1.3 maximum_select_fusion.1
  5.8 0.8 pad_maximum_fusion
  6.5 7.2 %all-to-all-start = ((bf16[8,24,1024]{2,1,0:T(8,128)(2,1)}), bf16[8,24,1024]{2,1,0:T(8,128)(2,1)}, u32[]{:S(2)}, u32[]{:S(2)}) async-start(bf16[8,24,1024]{2,1,0:T(8,128)(2,1)} %bitcast.72), calls=%async_computation | async-start | bytes 786432 | tf_op jit(solution)/shard_map/all_to_all | solution.py:240
  13.7 0.6 pad_add_fusion.place_ref
  14.3 11.5 %all-to-all-done = bf16[8,24,1024]{2,1,0:T(8,128)(2,1)} async-done(((bf16[8,24,1024]{2,1,0:T(8,128)(2,1)}), bf16[8,24,1024]{2,1,0:T(8,128)(2,1)}, u32[]{:S(2)}, u32[]{:S(2)}) %all-to-all-start) | async-done | bytes 393248 | tf_op jit(solution)/shard_map/all_to_all | solution.py:240
  25.8 12.5 %shard_map.37 = (bf16[2,2,2,208,128]{4,3,2,1,0:T(8,128)(2,1)}, f32[2,2,2,208,128]{4,3,2,1,0:T(8,128)}, bf16[2,2,2,208,128]{4,3,2,1,0:T(8,128)(2,1)}, f32[2,2,2,2...) custom-call(s32[2]{0:T(128)} %pad_add_fusion.place_ref, ...), custom_call_target="tpu_custom_call" | custom-call | flops 2617245696 | bytes 13631488 | tf_op jit(solution)/shard_map/pallas_call | solution.py:101
  38.3 1.0 copy.4
  39.3 1.5 collective-permute-start.2
  40.8 1.0 copy.6
  41.8 0.7 collective-permute-start.5
  42.5 9.6 %collective-permute-done.2 = bf16[2,2,2,208,128]{4,3,2,0,1:T(8,128)(2,1)S(1)} collective-permute-done((bf16[2,2,2,208,128]{4,3,2,0,1:T(8,128)(2,1)S(1)}, bf16[2,2,2,208,128]{4,3,2,0,1:T(8,128)(2,1)S(1)}, u32[]{:S(2)}, u32[]{:S(2)}) %collective-permute-start.2) | collective-permute-done | bytes 426016 | tf_op jit(solution)/shard_map/ppermute | solution.py:180
  52.1 1.2 copy_add_fusion.2
  53.4 1.0 collective-permute-start.3
  54.4 0.0 collective-permute-done.6
  54.4 4.2 %maximum_select_fusion.down = bf16[416,8192]{1,0:T(8,128)(2,1)} fusion(bf16[208,8192]{1,0:T(8,128)(2,1)S(1)} %collective-permute-done.6, bf16[208,8192]{1,0:T(8,128)(2,1)S(1)} %copy-done, pred[]{:T(512)S(6)} %eq.2), kind=kLoop, calls=%fused_computation | loop fusion | flops 30670848 | bytes 13631489 | tf_op jit(solution)/shard_map/jit(_where)/select_n | solution.py:244
  58.6 2.1 %collective-permute-done.3 = bf16[2,2,208,128]{3,2,1,0:T(8,128)(2,1)S(1)} collective-permute-done((bf16[2,2,208,128]{3,2,1,0:T(8,128)(2,1)S(1)}, bf16[2,2,208,128]{3,2,1,0:T(8,128)(2,1)S(1)}, u32[]{:S(2)}, u32[]{:S(2)}) %collective-permute-start.3) | collective-permute-done | bytes 213024 | tf_op jit(solution)/shard_map/ppermute | solution.py:180
  60.8 0.1 collective-permute-start.4
  60.9 0.1 copy_add_fusion.1
  61.0 0.3 collective-permute-start.8
  61.3 0.7 slice_bitcast_fusion.8.keep_in
  62.0 4.9 %collective-permute-done.4 = bf16[1,2,208,128]{3,2,1,0:T(8,128)(2,1)S(1)} collective-permute-done((bf16[1,2,208,128]{3,2,1,0:T(8,128)(2,1)S(1)}, bf16[1,2,208,128]{3,2,1,0:T(8,128)(2,1)S(1)}, u32[]{:S(2)}, u32[]{:S(2)}) %collective-permute-start.4) | collective-permute-done | bytes 106528 | tf_op jit(solution)/shard_map/ppermute | solution.py:180
  66.9 0.6 copy-done.7
  67.5 6.5 %shard_map.38 = (bf16[2,2,8,8192]{3,2,1,0:T(8,128)(2,1)}, f32[2,2,8,8192]{3,2,1,0:T(8,128)}) custom-call(s32[2]{0:T(128)} %pad_add_fusion.place_ref, f32[2,208,128]{2,1,0:T(8,128)} %slice_bitcast_fusion.8.keep_in, bf16[2,208,128]{2,1,0:T(8,128)(2,1)} %bitcast.79, bf16[416,8192]{1,0:T(8,128)(2,1)} %maximum_select_fusion.down), custom_call_target="tpu_custom_call" | custom-call | flops 436207616 | bytes 6815744 | tf_op jit(solution)/shard_map/pallas_call | solution.py:154
  74.0 1.1 collective-permute-start.7
  75.1 1.0 collective-permute-start.11
  76.2 0.7 slice_bitcast_fusion.7
  76.9 9.3 %collective-permute-done.7 = bf16[2,2,8,8192]{3,2,1,0:T(8,128)(2,1)S(1)} collective-permute-done((bf16[2,2,8,8192]{3,2,1,0:T(8,128)(2,1)}, bf16[2,2,8,8192]{3,2,1,0:T(8,128)(2,1)S(1)}, u32[]{:S(2)}, u32[]{:S(2)}) %collective-permute-start.7) | collective-permute-done | bytes 524320 | tf_op jit(solution)/shard_map/ppermute | solution.py:180
  86.2 1.3 convert_add_fusion.2
  87.5 0.6 collective-permute-start.9
  88.1 2.6 %collective-permute-done.11 = bf16[2,2,2,208,128]{4,3,2,0,1:T(8,128)(2,1)S(1)} collective-permute-done((bf16[2,2,2,208,128]{4,3,2,0,1:T(8,128)(2,1)S(1)}, bf16[2,2,2,208,128]{4,3,2,0,1:T(8,128)(2,1)S(1)}, u32[]{:S(2)}, u32[]{:S(2)}) %collective-permute-start.11) | collective-permute-done | bytes 426016 | tf_op jit(solution)/shard_map/ppermute | solution.py:180
  90.7 0.1 copy_add_fusion
  90.8 0.6 collective-permute-start.14
  91.4 0.7 copy-done.5
  92.1 6.5 %shard_map.39 = (bf16[2,2,8,8192]{3,2,1,0:T(8,128)(2,1)}, f32[2,2,8,8192]{3,2,1,0:T(8,128)}) custom-call(s32[2]{0:T(128)} %pad_add_fusion.place_ref, f32[2,208,128]{2,1,0:T(8,128)} %get-tuple-element.71.keep_in, f32[2,208,128]{2,1,0:T(8,128)} %bitcast.77, bf16[416,8192]{1,0:T(8,128)(2,1)} %maximum_select_fusion.down), custom_call_target="tpu_custom_call" | custom-call | flops 436207616 | bytes 6815744 | tf_op jit(solution)/shard_map/pallas_call | solution.py:154
  98.6 1.8 %collective-permute-start.13 = (bf16[2,2,8,8192]{3,2,1,0:T(8,128)(2,1)}, bf16[2,2,8,8192]{3,2,1,0:T(8,128)(2,1)S(1)}, u32[]{:S(2)}, u32[]{:S(2)}) collective-permute-start(bf16[2,2,8,8192]{3,2,1,0:T(8,128)(2,1)} %get-tuple-element.55), channel_id=1, source_target_pairs={{0,2},{2,0},{4,6},{6,4},{8,10},{10,8},{12,14},{14,12},{1,3},{3,1},... | collective-permute-start | bytes 1572872 | tf_op jit(solution)/shard_map/ppermute | solution.py:180
  100.4 3.2 %collective-permute-start.12 = (bf16[1,8,8192]{2,1,0:T(8,128)(2,1)S(1)}, bf16[1,8,8192]{2,1,0:T(8,128)(2,1)S(1)}, u32[]{:S(2)}, u32[]{:S(2)}) collective-permute-start(bf16[1,8,8192]{2,1,0:T(8,128)(2,1)S(1)} %slice.198), channel_id=1, source_target_pairs={{0,8},{2,10},{4,12},{6,14},{8,0},{10,2},{12,4},{14,6},{1,9},{3,11}... | collective-permute-start | bytes 393224 | tf_op jit(solution)/shard_map/ppermute | solution.py:180
  103.6 0.7 fusion.15
  104.4 0.0 collective-permute-start.17
  104.4 3.6 %collective-permute-done.13 = bf16[2,2,8,8192]{3,2,1,0:T(8,128)(2,1)S(1)} collective-permute-done((bf16[2,2,8,8192]{3,2,1,0:T(8,128)(2,1)}, bf16[2,2,8,8192]{3,2,1,0:T(8,128)(2,1)S(1)}, u32[]{:S(2)}, u32[]{:S(2)}) %collective-permute-start.13) | collective-permute-done | bytes 524320 | tf_op jit(solution)/shard_map/ppermute | solution.py:180
  108.0 1.3 convert_add_fusion.1
  109.3 1.6 %collective-permute-start.16 = (bf16[2,8,8192]{2,1,0:T(8,128)(2,1)S(1)}, bf16[2,8,8192]{2,1,0:T(8,128)(2,1)S(1)}, u32[]{:S(2)}, u32[]{:S(2)}) collective-permute-start(bf16[2,8,8192]{2,1,0:T(8,128)(2,1)S(1)} %fusion.7), channel_id=1, source_target_pairs={{0,4},{2,6},{4,0},{6,2},{8,12},{10,14},{12,8},{14,10},{1,5},{3,7},... | collective-permute-start | bytes 786440 | tf_op jit(solution)/shard_map/ppermute | solution.py:180
  111.0 0.1 collective-permute-start.15
  111.1 2.9 %collective-permute-done.17 = f32[1,2,208,128]{3,2,1,0:T(8,128)S(1)} collective-permute-done((f32[1,2,208,128]{3,2,1,0:T(8,128)S(1)}, f32[1,2,208,128]{3,2,1,0:T(8,128)S(1)}, u32[]{:S(2)}, u32[]{:S(2)}) %collective-permute-start.17) | collective-permute-done | bytes 213024 | tf_op jit(solution)/shard_map/ppermute | solution.py:180
  114.0 0.7 copy-done.4
  114.7 6.5 %shard_map.40 = (bf16[2,2,8,8192]{3,2,1,0:T(8,128)(2,1)}, f32[2,2,8,8192]{3,2,1,0:T(8,128)}) custom-call(s32[2]{0:T(128)} %pad_add_fusion.place_ref, f32[2,208,128]{2,1,0:T(8,128)} %get-tuple-element.70.keep_in, f32[2,208,128]{2,1,0:T(8,128)} %bitcast.76, bf16[416,8192]{1,0:T(8,128)(2,1)} %maximum_select_fusion.down), custom_call_target="tpu_custom_call" | custom-call | flops 436207616 | bytes 6815744 | tf_op jit(solution)/shard_map/pallas_call | solution.py:154
  121.2 0.5 collective-permute-start.19
  121.8 0.2 collective-permute-start.18
  122.0 10.8 %collective-permute-done.19 = bf16[2,2,8,8192]{3,2,1,0:T(8,128)(2,1)S(1)} collective-permute-done((bf16[2,2,8,8192]{3,2,1,0:T(8,128)(2,1)}, bf16[2,2,8,8192]{3,2,1,0:T(8,128)(2,1)S(1)}, u32[]{:S(2)}, u32[]{:S(2)}) %collective-permute-start.19) | collective-permute-done | bytes 524320 | tf_op jit(solution)/shard_map/ppermute | solution.py:180
  132.8 1.3 convert_add_fusion
  134.1 0.6 collective-permute-start.21
  134.8 5.8 %collective-permute-done.21 = bf16[2,8,8192]{2,1,0:T(8,128)(2,1)S(1)} collective-permute-done((bf16[2,8,8192]{2,1,0:T(8,128)(2,1)S(1)}, bf16[2,8,8192]{2,1,0:T(8,128)(2,1)S(1)}, u32[]{:S(2)}, u32[]{:S(2)}) %collective-permute-start.21) | collective-permute-done | bytes 262176 | tf_op jit(solution)/shard_map/ppermute | solution.py:180
  140.6 0.1 fusion
  140.7 3.6 %collective-permute-start.22 = (bf16[1,8,8192]{2,1,0:T(8,128)(2,1)S(1)}, bf16[1,8,8192]{2,1,0:T(8,128)(2,1)S(1)}, u32[]{:S(2)}, u32[]{:S(2)}) collective-permute-start(bf16[1,8,8192]{2,1,0:T(8,128)(2,1)S(1)} %slice.196), channel_id=1, source_target_pairs={{0,8},{2,10},{4,12},{6,14},{8,0},{10,2},{12,4},{14,6},{1,9},{3,11}... | collective-permute-start | bytes 393224 | tf_op jit(solution)/shard_map/ppermute | solution.py:180
  144.2 0.1 collective-permute-start.20
  144.3 3.8 %collective-permute-done.22 = bf16[1,8,8192]{2,1,0:T(8,128)(2,1)S(1)} collective-permute-done((bf16[1,8,8192]{2,1,0:T(8,128)(2,1)S(1)}, bf16[1,8,8192]{2,1,0:T(8,128)(2,1)S(1)}, u32[]{:S(2)}, u32[]{:S(2)}) %collective-permute-start.22) | collective-permute-done | bytes 131104 | tf_op jit(solution)/shard_map/ppermute | solution.py:180
  148.2 0.1 collective-permute-start.23
  148.3 1.2 collective-permute-done.23
  149.5 0.8 pad_maximum_fusion.1
  (50 shorter events, 0.7 us)
Async XLA Ops:
  1.7 1.5 %collective-permute-start = (bf16[24,4096]{1,0:T(8,128)(2,1)S(1)}, bf16[24,4096]{1,0:T(8,128)(2,1)S(1)}, u32[]{:S(2)}, u32[]{:S(2)}) collective-permute-start(bf16[24,4096]{1,0:T(8,128)(2,1)S(1)} %get-tuple-element.78), channel_id=1, source_target_pairs={{0,1},{1,0},{2,3},{3,2},{4,5},{5,4},{6,7},{7,6},{8,9},{9,8},{10,11... | collective-permute-start | bytes 589832 | tf_op jit(solution)/shard_map/ppermute | solution.py:184
  3.2 0.7 copy-start.6
  3.9 21.9 %collective-permute-start.1 = (bf16[2,512,3328]{2,1,0:T(8,128)(2,1)}, bf16[2,512,3328]{2,1,0:T(8,128)(2,1)}, u32[]{:S(2)}, u32[]{:S(2)}) collective-permute-start(bf16[2,512,3328]{2,1,0:T(8,128)(2,1)} %own.1), channel_id=1, source_target_pairs={{0,1},{1,0},{2,3},{3,2},{4,5},{5,4},{6,7},{7,6},{8,9},{9,8},{10,11... | collective-permute-start | bytes 20447240 | tf_op jit(solution)/shard_map/ppermute | solution.py:184
  4.3 50.1 %collective-permute-start.6 = (bf16[208,8192]{1,0:T(8,128)(2,1)}, bf16[208,8192]{1,0:T(8,128)(2,1)S(1)}, u32[]{:S(2)}, u32[]{:S(2)}) collective-permute-start(bf16[208,8192]{1,0:T(8,128)(2,1)} %param.5), channel_id=1, source_target_pairs={{0,1},{1,0},{2,3},{3,2},{4,5},{5,4},{6,7},{7,6},{8,9},{9,8},{10,11... | collective-permute-start | bytes 10223624 | tf_op jit(solution)/shard_map/ppermute | solution.py:184
  6.5 19.3 %all-to-all-start = ((bf16[8,24,1024]{2,1,0:T(8,128)(2,1)}), bf16[8,24,1024]{2,1,0:T(8,128)(2,1)}, u32[]{:S(2)}, u32[]{:S(2)}) async-start(bf16[8,24,1024]{2,1,0:T(8,128)(2,1)} %bitcast.72), calls=%async_computation | async-start | bytes 786432 | tf_op jit(solution)/shard_map/all_to_all | solution.py:240
  25.8 28.6 %copy-start = (bf16[208,8192]{1,0:T(8,128)(2,1)S(1)}, bf16[208,8192]{1,0:T(8,128)(2,1)}, u32[]{:S(2)}) copy-start(bf16[208,8192]{1,0:T(8,128)(2,1)} %param.5) | copy-start | bytes 10223620
  39.3 12.8 %collective-permute-start.2 = (bf16[2,2,2,208,128]{4,3,2,0,1:T(8,128)(2,1)S(1)}, bf16[2,2,2,208,128]{4,3,2,0,1:T(8,128)(2,1)S(1)}, u32[]{:S(2)}, u32[]{:S(2)}) collective-permute-start(bf16[2,2,2,208,128]{4,3,2,0,1:T(8,128)(2,1)S(1)} %copy.4), channel_id=1, source_target_pairs={{0,2},{2,0},{4,6},{6,4},{8,10},{10,8},{12,14},{14,12},{1,3},{3,1},... | collective-permute-start | bytes 1277960 | tf_op jit(solution)/shard_map/ppermute | solution.py:180
  41.8 19.0 %collective-permute-start.5 = (bf16[2,2,2,208,128]{4,3,2,0,1:T(8,128)(2,1)S(1)}, bf16[2,2,2,208,128]{4,3,2,0,1:T(8,128)(2,1)S(1)}, u32[]{:S(2)}, u32[]{:S(2)}) collective-permute-start(bf16[2,2,2,208,128]{4,3,2,0,1:T(8,128)(2,1)S(1)} %copy.6), channel_id=1, source_target_pairs={{0,2},{2,0},{4,6},{6,4},{8,10},{10,8},{12,14},{14,12},{1,3},{3,1},... | collective-permute-start | bytes 1277960 | tf_op jit(solution)/shard_map/ppermute | solution.py:180
  53.4 7.5 %copy-start.2 = (f32[2,2,2,208,128]{4,3,2,1,0:T(8,128)S(1)}, f32[2,2,2,208,128]{4,3,2,1,0:T(8,128)}, u32[]{:S(2)}) copy-start(f32[2,2,2,208,128]{4,3,2,1,0:T(8,128)} %get-tuple-element.43) | copy-start | bytes 2555908
  53.4 7.3 %collective-permute-start.3 = (bf16[2,2,208,128]{3,2,1,0:T(8,128)(2,1)S(1)}, bf16[2,2,208,128]{3,2,1,0:T(8,128)(2,1)S(1)}, u32[]{:S(2)}, u32[]{:S(2)}) collective-permute-start(bf16[2,2,208,128]{3,2,1,0:T(8,128)(2,1)S(1)} %fusion.12), channel_id=1, source_target_pairs={{0,4},{2,6},{4,0},{6,2},{8,12},{10,14},{12,8},{14,10},{1,5},{3,7},... | collective-permute-start | bytes 638984 | tf_op jit(solution)/shard_map/ppermute | solution.py:180
  58.6 16.5 %copy-start.3 = (bf16[2,2,2,208,128]{4,3,2,1,0:T(8,128)(2,1)S(1)}, bf16[2,2,2,208,128]{4,3,2,1,0:T(8,128)(2,1)}, u32[]{:S(2)}) copy-start(bf16[2,2,2,208,128]{4,3,2,1,0:T(8,128)(2,1)} %get-tuple-element.49) | copy-start | bytes 1277956
  60.8 6.1 %collective-permute-start.4 = (bf16[1,2,208,128]{3,2,1,0:T(8,128)(2,1)S(1)}, bf16[1,2,208,128]{3,2,1,0:T(8,128)(2,1)S(1)}, u32[]{:S(2)}, u32[]{:S(2)}) collective-permute-start(bf16[1,2,208,128]{3,2,1,0:T(8,128)(2,1)S(1)} %slice.199), channel_id=1, source_target_pairs={{0,8},{2,10},{4,12},{6,14},{8,0},{10,2},{12,4},{14,6},{1,9},{3,11}... | collective-permute-start | bytes 319496 | tf_op jit(solution)/shard_map/ppermute | solution.py:180
  61.0 29.7 %copy-start.1 = (f32[2,2,2,208,128]{4,3,2,1,0:T(8,128)S(1)}, f32[2,2,2,208,128]{4,3,2,1,0:T(8,128)}, u32[]{:S(2)}) copy-start(f32[2,2,2,208,128]{4,3,2,1,0:T(8,128)} %get-tuple-element.52) | copy-start | bytes 2555908
  61.0 15.1 %collective-permute-start.8 = (bf16[2,2,208,128]{3,2,1,0:T(8,128)(2,1)S(1)}, bf16[2,2,208,128]{3,2,1,0:T(8,128)(2,1)S(1)}, u32[]{:S(2)}, u32[]{:S(2)}) collective-permute-start(bf16[2,2,208,128]{3,2,1,0:T(8,128)(2,1)S(1)} %fusion.13), channel_id=1, source_target_pairs={{0,4},{2,6},{4,0},{6,2},{8,12},{10,14},{12,8},{14,10},{1,5},{3,7},... | collective-permute-start | bytes 638984 | tf_op jit(solution)/shard_map/ppermute | solution.py:180
  66.9 0.6 copy-start.7
  74.0 12.2 %collective-permute-start.7 = (bf16[2,2,8,8192]{3,2,1,0:T(8,128)(2,1)}, bf16[2,2,8,8192]{3,2,1,0:T(8,128)(2,1)S(1)}, u32[]{:S(2)}, u32[]{:S(2)}) collective-permute-start(bf16[2,2,8,8192]{3,2,1,0:T(8,128)(2,1)} %get-tuple-element.48), channel_id=1, source_target_pairs={{0,2},{2,0},{4,6},{6,4},{8,10},{10,8},{12,14},{14,12},{1,3},{3,1},... | collective-permute-start | bytes 1572872 | tf_op jit(solution)/shard_map/ppermute | solution.py:180
  75.1 15.6 %collective-permute-start.11 = (bf16[2,2,2,208,128]{4,3,2,0,1:T(8,128)(2,1)S(1)}, bf16[2,2,2,208,128]{4,3,2,0,1:T(8,128)(2,1)S(1)}, u32[]{:S(2)}, u32[]{:S(2)}) collective-permute-start(bf16[2,2,2,208,128]{4,3,2,0,1:T(8,128)(2,1)S(1)} %copy.9), channel_id=1, source_target_pairs={{0,2},{2,0},{4,6},{6,4},{8,10},{10,8},{12,14},{14,12},{1,3},{3,1},... | collective-permute-start | bytes 1277960 | tf_op jit(solution)/shard_map/ppermute | solution.py:180
  76.9 14.5 %collective-permute-start.10 = (f32[1,2,208,128]{3,2,1,0:T(8,128)S(1)}, f32[1,2,208,128]{3,2,1,0:T(8,128)S(1)}, u32[]{:S(2)}, u32[]{:S(2)}) collective-permute-start(f32[1,2,208,128]{3,2,1,0:T(8,128)S(1)} %get-tuple-element.72), channel_id=1, source_target_pairs={{0,8},{2,10},{4,12},{6,14},{8,0},{10,2},{12,4},{14,6},{1,9},{3,11}... | collective-permute-start | bytes 638984 | tf_op jit(solution)/shard_map/ppermute | solution.py:180
  87.5 12.8 %collective-permute-start.9 = (bf16[2,8,8192]{2,1,0:T(8,128)(2,1)S(1)}, bf16[2,8,8192]{2,1,0:T(8,128)(2,1)S(1)}, u32[]{:S(2)}, u32[]{:S(2)}) collective-permute-start(bf16[2,8,8192]{2,1,0:T(8,128)(2,1)S(1)} %fusion.6), channel_id=1, source_target_pairs={{0,4},{2,6},{4,0},{6,2},{8,12},{10,14},{12,8},{14,10},{1,5},{3,7},... | collective-permute-start | bytes 786440 | tf_op jit(solution)/shard_map/ppermute | solution.py:180
  90.8 12.8 %collective-permute-start.14 = (bf16[2,2,208,128]{3,2,1,0:T(8,128)(2,1)S(1)}, bf16[2,2,208,128]{3,2,1,0:T(8,128)(2,1)S(1)}, u32[]{:S(2)}, u32[]{:S(2)}) collective-permute-start(bf16[2,2,208,128]{3,2,1,0:T(8,128)(2,1)S(1)} %fusion.14), channel_id=1, source_target_pairs={{0,4},{2,6},{4,0},{6,2},{8,12},{10,14},{12,8},{14,10},{1,5},{3,7},... | collective-permute-start | bytes 638984 | tf_op jit(solution)/shard_map/ppermute | solution.py:180
  91.4 0.7 copy-start.5
  98.6 9.4 %collective-permute-start.13 = (bf16[2,2,8,8192]{3,2,1,0:T(8,128)(2,1)}, bf16[2,2,8,8192]{3,2,1,0:T(8,128)(2,1)S(1)}, u32[]{:S(2)}, u32[]{:S(2)}) collective-permute-start(bf16[2,2,8,8192]{3,2,1,0:T(8,128)(2,1)} %get-tuple-element.55), channel_id=1, source_target_pairs={{0,2},{2,0},{4,6},{6,4},{8,10},{10,8},{12,14},{14,12},{1,3},{3,1},... | collective-permute-start | bytes 1572872 | tf_op jit(solution)/shard_map/ppermute | solution.py:180
  100.4 10.5 %collective-permute-start.12 = (bf16[1,8,8192]{2,1,0:T(8,128)(2,1)S(1)}, bf16[1,8,8192]{2,1,0:T(8,128)(2,1)S(1)}, u32[]{:S(2)}, u32[]{:S(2)}) collective-permute-start(bf16[1,8,8192]{2,1,0:T(8,128)(2,1)S(1)} %slice.198), channel_id=1, source_target_pairs={{0,8},{2,10},{4,12},{6,14},{8,0},{10,2},{12,4},{14,6},{1,9},{3,11}... | collective-permute-start | bytes 393224 | tf_op jit(solution)/shard_map/ppermute | solution.py:180
  104.4 9.6 %collective-permute-start.17 = (f32[1,2,208,128]{3,2,1,0:T(8,128)S(1)}, f32[1,2,208,128]{3,2,1,0:T(8,128)S(1)}, u32[]{:S(2)}, u32[]{:S(2)}) collective-permute-start(f32[1,2,208,128]{3,2,1,0:T(8,128)S(1)} %get-tuple-element.69), channel_id=1, source_target_pairs={{0,8},{2,10},{4,12},{6,14},{8,0},{10,2},{12,4},{14,6},{1,9},{3,11}... | collective-permute-start | bytes 638984 | tf_op jit(solution)/shard_map/ppermute | solution.py:180
  109.3 12.4 %collective-permute-start.16 = (bf16[2,8,8192]{2,1,0:T(8,128)(2,1)S(1)}, bf16[2,8,8192]{2,1,0:T(8,128)(2,1)S(1)}, u32[]{:S(2)}, u32[]{:S(2)}) collective-permute-start(bf16[2,8,8192]{2,1,0:T(8,128)(2,1)S(1)} %fusion.7), channel_id=1, source_target_pairs={{0,4},{2,6},{4,0},{6,2},{8,12},{10,14},{12,8},{14,10},{1,5},{3,7},... | collective-permute-start | bytes 786440 | tf_op jit(solution)/shard_map/ppermute | solution.py:180
  111.0 33.2 %collective-permute-start.15 = (bf16[8,4096]{1,0:T(8,128)(2,1)S(1)}, bf16[8,4096]{1,0:T(8,128)(2,1)S(1)}, u32[]{:S(2)}, u32[]{:S(2)}) collective-permute-start(bf16[8,4096]{1,0:T(8,128)(2,1)S(1)} %get-tuple-element.80), channel_id=1, source_target_pairs={{0,1},{1,0},{2,3},{3,2},{4,5},{5,4},{6,7},{7,6},{8,9},{9,8},{10,11... | collective-permute-start | bytes 196616 | tf_op jit(solution)/shard_map/ppermute | solution.py:184
  114.0 0.7 copy-start.4
  121.2 11.6 %collective-permute-start.19 = (bf16[2,2,8,8192]{3,2,1,0:T(8,128)(2,1)}, bf16[2,2,8,8192]{3,2,1,0:T(8,128)(2,1)S(1)}, u32[]{:S(2)}, u32[]{:S(2)}) collective-permute-start(bf16[2,2,8,8192]{3,2,1,0:T(8,128)(2,1)} %get-tuple-element.62), channel_id=1, source_target_pairs={{0,2},{2,0},{4,6},{6,4},{8,10},{10,8},{12,14},{14,12},{1,3},{3,1},... | collective-permute-start | bytes 1572872 | tf_op jit(solution)/shard_map/ppermute | solution.py:180
  121.8 12.9 %collective-permute-start.18 = (bf16[1,8,8192]{2,1,0:T(8,128)(2,1)S(1)}, bf16[1,8,8192]{2,1,0:T(8,128)(2,1)S(1)}, u32[]{:S(2)}, u32[]{:S(2)}) collective-permute-start(bf16[1,8,8192]{2,1,0:T(8,128)(2,1)S(1)} %slice.197), channel_id=1, source_target_pairs={{0,8},{2,10},{4,12},{6,14},{8,0},{10,2},{12,4},{14,6},{1,9},{3,11}... | collective-permute-start | bytes 393224 | tf_op jit(solution)/shard_map/ppermute | solution.py:180
  134.1 6.4 %collective-permute-start.21 = (bf16[2,8,8192]{2,1,0:T(8,128)(2,1)S(1)}, bf16[2,8,8192]{2,1,0:T(8,128)(2,1)S(1)}, u32[]{:S(2)}, u32[]{:S(2)}) collective-permute-start(bf16[2,8,8192]{2,1,0:T(8,128)(2,1)S(1)} %fusion.8), channel_id=1, source_target_pairs={{0,4},{2,6},{4,0},{6,2},{8,12},{10,14},{12,8},{14,10},{1,5},{3,7},... | collective-permute-start | bytes 786440 | tf_op jit(solution)/shard_map/ppermute | solution.py:180
  140.7 7.5 %collective-permute-start.22 = (bf16[1,8,8192]{2,1,0:T(8,128)(2,1)S(1)}, bf16[1,8,8192]{2,1,0:T(8,128)(2,1)S(1)}, u32[]{:S(2)}, u32[]{:S(2)}) collective-permute-start(bf16[1,8,8192]{2,1,0:T(8,128)(2,1)S(1)} %slice.196), channel_id=1, source_target_pairs={{0,8},{2,10},{4,12},{6,14},{8,0},{10,2},{12,4},{14,6},{1,9},{3,11}... | collective-permute-start | bytes 393224 | tf_op jit(solution)/shard_map/ppermute | solution.py:180
  144.2 4.0 %collective-permute-start.20 = (bf16[8,4096]{1,0:T(8,128)(2,1)S(1)}, bf16[8,4096]{1,0:T(8,128)(2,1)S(1)}, u32[]{:S(2)}, u32[]{:S(2)}) collective-permute-start(bf16[8,4096]{1,0:T(8,128)(2,1)S(1)} %get-tuple-element.82), channel_id=1, source_target_pairs={{0,1},{1,0},{2,3},{3,2},{4,5},{5,4},{6,7},{7,6},{8,9},{9,8},{10,11... | collective-permute-start | bytes 196616 | tf_op jit(solution)/shard_map/ppermute | solution.py:184
  148.2 1.3 collective-permute-start.23
where the time goes:
time: 151 us; the launch traced here: 150 us
  waiting for transfers between devices  69.3 us (46%)
  Pallas kernels  31.9 us (21%)
  starting transfers between devices  26.5 us (18%)
  other arithmetic  13.3 us (9%)
  local copies, waits for them, and re-layouts  8.96 us (6%)
    ppermute x18, waiting for transfers between devices, swap(): return lax.ppermute(value, 'gx', [(i, i ^ 1 << bit) for i in range(count)])  55.5 us
    pallas_call x3, Pallas kernels, down_project(): pl.pallas_call(functools.partial(down_kernel, block, count, order), out_s...  19.4 us
    ppermute x18, starting transfers between devices, swap(): return lax.ppermute(value, 'gx', [(i, i ^ 1 << bit) for i in range(count)])  18.2 us
    pallas_call x1, Pallas kernels, project(): pl.pallas_call(functools.partial(project_kernel, block, cuts), out_shape=...  12.5 us
    all_to_all x1, waiting for transfers between devices, local(): rows = lax.all_to_all(rows, 'gx', 0, 0).reshape(count_x * each, 2 * depth)  11.5 us
    all_to_all x1, starting transfers between devices, local(): rows = lax.all_to_all(rows, 'gx', 0, 0).reshape(count_x * each, 2 * depth)  7.17 us
    add x12, other arithmetic, halving(): acc = keep + after(recv, done).astype(jnp.float32)  5.57 us
    select_n x1, other arithmetic, local(): jnp.where(core == 0, jnp.concatenate([down_weight, down_other]), jnp.conc...  4.21 us
  transfers between devices with their start and end apart: 25, of which 13 were waited for; matrix products, arithmetic and copies ran while one was open for 11% of the time, Pallas kernels for 21%

commit v1 on v0

v1 whole, which is shorter than its diff:
```python
import functools

import jax
import jax.numpy as jnp
from jax import lax
from jax.experimental import pallas as pl
from jax.experimental.pallas import tpu as pltpu
from jax.sharding import PartitionSpec as P

LANES = 128
QUAD = 4
VMEM = 20 * 1024 * 1024


ORDERS = [((0, 1), (0, 1)), ((1, 0), (1, 0)), ((0, 1), (1, 0))]
TURNS = [0, 1, 0, 1, 2, 0, 1, 0, 2, 1, 2, 0, 2, 1, 0, 1, 0, 2, 1, 0, 2, 1, 2, 2]


def wire_type(stage, stages):
    return jnp.bfloat16 if stages - stage <= 3 else jnp.float32


def place(relative, order, send, keep, value):
    first = (relative >> order[0]) & 1
    second = (relative >> order[1]) & 1
    group = 0 if send.shape[0] == 1 else relative >> 2

    @pl.when(first == 1)
    def _():
        send[group, second] = value.astype(send.dtype)

    @pl.when(first == 0)
    def _():
        keep[group, second] = value


def project_kernel(block, cuts, place_ref, tokens, own_in, other_in, *refs):
    outs, (own, other, accs, sems) = refs[:-4], refs[-4:]
    chip, core = place_ref[0], place_ref[1]
    chips, each = tokens.shape[0] // cuts[-1][1], cuts[-1][1]
    halves, depth, wide = own.shape[0], own.shape[1], QUAD * block
    groups = own.shape[2] // wide
    span = wide if groups <= 2 else own.shape[2]
    loads = {}
    for half in range(halves):
        for group in range(own.shape[2] // span):
            lanes = slice(group * span, (group + 1) * span)
            loads[half, group] = [
                pltpu.make_async_copy(source.at[half, :, lanes], target.at[half, :, lanes], sems.at[i, half, group])
                for i, (source, target) in enumerate(((own_in, own), (other_in, other)))
            ]
            for load in loads[half, group]:
                load.start()
    low, high = tokens[:, :depth], tokens[:, depth:]
    first_rows = jnp.where(core == 0, low, high)
    second_rows = jnp.where(core == 0, high, low)
    whole_tiles, rest = block // LANES, block % LANES
    fold = LANES // rest

    def step(half, group, acc):
        at = group * wide
        span = pl.ds(at if isinstance(at, int) else pl.multiple_of(at, LANES), wide)
        acc[...] = jnp.dot(first_rows, own[half, :, span], preferred_element_type=jnp.float32) + jnp.dot(
            second_rows, other[half, :, span], preferred_element_type=jnp.float32
        )
        for index, (first, last, order) in enumerate(cuts):
            count = chips * (last - first)
            part = count // fold
            lane = lax.broadcasted_iota(jnp.int32, (count, LANES), 1)

            def tile(at):
                lanes = slice(at * LANES, (at + 1) * LANES)
                if count == tokens.shape[0]:
                    return acc[:, lanes]
                return jnp.concatenate([acc[c * each + first : c * each + last, lanes] for c in range(chips)])

            for q in range(QUAD):
                base, shift = q * block // LANES, q * block % LANES
                tail = tile(base + whole_tiles)
                head = tile(base)
                pieces = [jnp.where(lane < shift, tail, head) if shift else head]
                pieces += [tile(base + t) for t in range(1, whole_tiles)]
                packed = None
                for k in range(fold):
                    value = tail[k * part : (k + 1) * part]
                    turn = (k * rest - shift) % LANES
                    if turn:
                        value = pltpu.roll(value, turn, 1)
                    packed = value if k == 0 else jnp.where(lane[:part] < k * rest, packed, value)
                pieces.append(packed)
                value = jnp.concatenate(pieces)
                relative = (QUAD * group + q) ^ chip
                outer, a, b = relative >> 2, (relative >> order[0]) & 1, (relative >> order[1]) & 1
                send, keep = outs[2 * index], outs[2 * index + 1]

                @pl.when(a == 1)
                def _():
                    send[outer, b, half] = value.astype(send.dtype)

                @pl.when(a == 0)
                def _():
                    keep[outer, b, half] = value

    for half in range(halves):
        for group in range(own.shape[2] // span):
            for load in loads[half, group]:
                load.wait()
            if groups <= 2:
                step(half, group, accs.at[group % 2])
            else:
                lax.fori_loop(0, groups, lambda g, c: step(half, g, accs.at[0]), None)


def project(spot, tokens, own, other, count_x, cuts, stages):
    block = own.shape[2] // count_x
    rows, depth = tokens.shape[0], own.shape[1]
    groups = count_x // QUAD
    if groups > 2 and own.shape[0] > 1:
        two = [project(spot, tokens, own[h : h + 1], other[h : h + 1], count_x, cuts, stages) for h in range(2)]
        return [jnp.concatenate(pair, axis=2) for pair in zip(*two)]
    shapes = []
    for first, last, _ in cuts:
        lines = count_x * (last - first) * block // LANES
        for kind in (wire_type(0, stages), jnp.float32):
            shapes.append(jax.ShapeDtypeStruct((groups, 2, own.shape[0], lines, LANES), kind))
    inside = pl.BlockSpec(memory_space=pltpu.VMEM)
    scratch = jax.ShapeDtypeStruct((2, rows, QUAD * block), jnp.float32)
    held = sum(t.size * t.dtype.itemsize for t in [tokens, own, other, scratch, *shapes])
    return pl.pallas_call(
        functools.partial(project_kernel, block, cuts),
        out_shape=shapes,
        in_specs=[pl.BlockSpec(memory_space=pltpu.SMEM), inside] + [pl.BlockSpec(memory_space=pltpu.HBM)] * 2,
        out_specs=[inside] * len(shapes),
        scratch_shapes=[
            pltpu.VMEM(own.shape, own.dtype),
            pltpu.VMEM(own.shape, own.dtype),
            pltpu.VMEM(scratch.shape, scratch.dtype),
            pltpu.SemaphoreType.DMA((2, own.shape[0], 2)),
        ],
        compiler_params=pltpu.CompilerParams(vmem_limit_bytes=held + 4 * 1024 * 1024),
        cost_estimate=pl.CostEstimate(
            flops=4 * rows * depth * own.shape[2], bytes_accessed=2 * own.size, transcendentals=0
        ),
    )(spot, tokens, own, other)


def down_kernel(block, count, order, place_ref, keep_in, recv_in, own, other, send, keep, hidden):
    chip, core = place_ref[0], place_ref[1]
    whole_tiles, rest = block // LANES, block % LANES
    fold = LANES // rest

    @pl.when(pl.program_id(0) == 0)
    def _():
        gate = keep_in[0] + recv_in[0].astype(jnp.float32)
        upper = keep_in[1] + recv_in[1].astype(jnp.float32)
        value = gate / (1.0 + jnp.exp(-gate)) * upper
        tiles = jnp.concatenate(
            [value[piece * count : (piece + 1) * count] for piece in range(whole_tiles)], axis=1
        )
        shift = (chip & (QUAD - 1)) * rest
        turned = pltpu.roll(tiles, lax.rem(whole_tiles * LANES - shift, whole_tiles * LANES), 1)
        high = turned.astype(jnp.bfloat16)
        hidden[:count, : whole_tiles * LANES] = high
        hidden[count:, : whole_tiles * LANES] = (turned - high.astype(jnp.float32)).astype(jnp.bfloat16)
        packed = value[whole_tiles * count :]
        part = count // fold
        for k in range(fold):
            turned = pltpu.roll(packed, (LANES - k * rest) % LANES, 1) if k else packed
            turned = turned[:, :rest]
            high = turned.astype(jnp.bfloat16)
            hidden[k * part : (k + 1) * part, whole_tiles * LANES :] = high
            hidden[count + k * part : count + (k + 1) * part, whole_tiles * LANES :] = (
                turned - high.astype(jnp.float32)
            ).astype(jnp.bfloat16)

    low, high = hidden[:, : block // 2], hidden[:, block // 2 :]
    product = jnp.dot(
        jnp.where(core == 0, low, high), own[...], preferred_element_type=jnp.float32
    ) + jnp.dot(jnp.where(core == 0, high, low), other[...], preferred_element_type=jnp.float32)
    product = product[:count] + product[count:]
    chips = 4 * send.shape[0]
    each = count // chips
    for owner in range(chips):
        place(owner ^ chip, order, send, keep, product[owner * each : (owner + 1) * each])


def down_project(spot, keep, recv, own, other, count, order, count_x, stages, span=(0, 1), wide=4096):
    block, features = 2 * own.shape[0], own.shape[1]
    part, parts = span
    features = features // parts
    wide = min(wide, features)
    groups = count_x // QUAD
    each = count // count_x
    whole = pl.BlockSpec(keep.shape, lambda c, s: (0, 0, 0))
    out = pl.BlockSpec((groups, 2, each, wide), lambda c, s: (0, 0, 0, c))
    weights = pl.BlockSpec((block // 2, wide), lambda c, s: (0, part * (features // wide) + c))
    return pl.pallas_call(
        functools.partial(down_kernel, block, count, order),
        out_shape=[
            jax.ShapeDtypeStruct((groups, 2, each, features), kind)
            for kind in (wire_type(0, stages), jnp.float32)
        ],
        grid_spec=pltpu.PrefetchScalarGridSpec(
            num_scalar_prefetch=1,
            grid=(features // wide,),
            in_specs=[
                whole,
                whole,
                weights,
                weights,
            ],
            out_specs=[out, out],
            scratch_shapes=[pltpu.VMEM((2 * count, block), jnp.bfloat16)],
        ),
        compiler_params=pltpu.CompilerParams(vmem_limit_bytes=VMEM),
        cost_estimate=pl.CostEstimate(
            flops=2 * count * block * features, bytes_accessed=2 * block * features, transcendentals=0
        ),
    )(spot, keep, recv, own, other)


def swap(value, bit):
    count = lax.axis_size("gx")
    return lax.ppermute(value, "gx", [(i, i ^ (1 << bit)) for i in range(count)])


def swap_cores(value):
    return lax.ppermute(value, "gy", [(0, 1), (1, 0)])


def after(value, done):
    return value if done is None else lax.optimization_barrier((value, done))[0]


def halving(send, keep, order, stages, done):
    recv = swap(after(send, done), order[0])
    done = yield send
    for stage in range(1, stages):
        acc = keep + after(recv, done).astype(jnp.float32)
        kind = wire_type(stage, stages)
        if stage == 1:
            send, keep, bit = acc[:, 1].astype(kind), acc[:, 0], order[1]
        else:
            half = acc.shape[0] // 2
            send, keep, bit = acc[half:].astype(kind), acc[:half], 1 + half.bit_length()
        recv = swap(send, bit)
        done = yield send
    return keep[0], after(recv, done)[0]


def chunk_steps(spot, parts, downs, count, orders, count_x, stages):
    core = spot[1]
    done = yield
    keep, recv = yield from halving(parts[0], parts[1], orders[0], stages, done)
    send, keep = down_project(spot, keep, recv, *downs, count, orders[1], count_x, stages)
    keep, recv = yield from halving(send, keep, orders[1], stages, None)
    mixed = (keep + recv.astype(jnp.float32)).astype(jnp.bfloat16)
    halves = mixed.reshape(mixed.shape[0], 2, -1)
    mine = lax.dynamic_index_in_dim(halves, core, 1, False)
    send = lax.dynamic_index_in_dim(halves, 1 - core, 1, False)
    theirs = swap_cores(send)
    done = yield send
    theirs = after(theirs, done)
    return jnp.where(core == 0, jnp.stack([mine, theirs]), jnp.stack([theirs, mine]))


def local(tokens, gate_up, down_weight):
    count_x = lax.axis_size("gx")
    stages = count_x.bit_length() - 1
    chip, core = lax.axis_index("gx"), lax.axis_index("gy")
    spot = jnp.stack([chip, core]).astype(jnp.int32)
    each = tokens.shape[1]
    depth = gate_up.shape[1]

    mine = lax.dynamic_index_in_dim(tokens, core, 0, False)
    theirs = swap_cores(lax.dynamic_index_in_dim(tokens, 1 - core, 0, False))
    other = swap_cores(after(gate_up, theirs))
    down_other = swap_cores(after(down_weight, theirs))
    rows = jnp.where(core == 0, jnp.stack([mine, theirs]), jnp.stack([theirs, mine]))
    rows = rows.reshape(2, each, count_x // 2, 2 * depth).transpose(0, 2, 1, 3)
    rows = rows.reshape(count_x, each, 2 * depth)
    rows = lax.all_to_all(rows, "gx", 0, 0).reshape(count_x * each, 2 * depth)

    if stages == 3 and each == 24:
        step, orders, turns = 8, ORDERS, TURNS
    else:
        step, orders = each, [((0, 1), (0, 1))]
        turns = [0] * (2 * stages + 2)
    cuts = tuple((i * step, (i + 1) * step, order[0]) for i, order in enumerate(orders))
    parts = project(spot, rows, gate_up, other, count_x, cuts, stages)
    chunks = [
        chunk_steps(
            spot, parts[2 * i : 2 * i + 2], (down_weight, down_other), count_x * step, order, count_x, stages
        )
        for i, order in enumerate(orders)
    ]
    for chunk in chunks:
        next(chunk)
    done, results = None, {}
    for i in turns:
        try:
            done = chunks[i].send(done)
        except StopIteration as end:
            results[i] = end.value
    return jnp.concatenate([results[i] for i in range(len(cuts))], axis=1)


def solution(mesh):
    return jax.shard_map(
        local,
        mesh=mesh,
        in_specs=(
            P(None, ("groups", "gx"), "gy"),
            P(None, ("gx", "gy"), None),
            P(("gx", "gy"), None),
        ),
        out_specs=P(None, ("groups", "gx"), "gy"),
        check_vma=False,
    )
```

time: 151 us -> 127 us (0.84)
  Pallas kernels: 31.9 us -> 19.2 us
  other arithmetic: 13.3 us -> 3.81 us
  starting transfers between devices: 26.5 us -> 32.6 us
  waiting for transfers between devices: 69.3 us -> 63.6 us
  local copies, waits for them, and re-layouts: 8.96 us -> 5.46 us
    pallas_call x3, Pallas kernels: 19.4 us -> 9.55 us  [down_project(): pl.pallas_call(functools.partial(down_kernel, block, count, order), out_s...]
    ppermute x18, waiting for transfers between devices: 55.5 us -> 49 us  [swap(): return lax.ppermute(value, 'gx', [(i, i ^ 1 << bit) for i in range(count)])]
    ppermute x18, starting transfers between devices: 18.2 us -> 24.2 us  [swap(): return lax.ppermute(value, 'gx', [(i, i ^ 1 << bit) for i in range(count)])]
    add x12, other arithmetic: 5.57 us -> 0.77 us  [halving(): acc = keep + after(recv, done).astype(jnp.float32)]
    select_n x1 -> x0, other arithmetic: 4.21 us -> none  [local(): jnp.where(core == 0, jnp.concatenate([down_weight, down_other]), jnp.conc...]
    pallas_call x1, Pallas kernels: 12.5 us -> 9.65 us  [project(): pl.pallas_call(functools.partial(project_kernel, block, cuts), out_shape=...]
    pallas_call x3 -> x1, local copies, waits for them, and re-layouts: 2.1 us -> 0.03 us  [project(): pl.pallas_call(functools.partial(project_kernel, block, cuts), out_shape=...]
    unnamed x16 -> x6, local copies, waits for them, and re-layouts: 2.69 us -> 3.24 us
  transfers between devices with their start and end apart: 25 -> 25, of which waited for: 13 -> 16; matrix products, arithmetic and copies ran while one was open for 11% -> 3% of each run, Pallas kernels for 21% -> 15%
where the time goes in v1:
time: 127 us; the launch traced here: 125 us
  waiting for transfers between devices  63.6 us (50%)
  starting transfers between devices  32.6 us (26%)
  Pallas kernels  19.2 us (15%)
  local copies, waits for them, and re-layouts  5.46 us (4%)
  other arithmetic  3.81 us (3%)
    ppermute x18, waiting for transfers between devices, swap(): return lax.ppermute(value, 'gx', [(i, i ^ 1 << bit) for i in range(count)])  49 us
    ppermute x18, starting transfers between devices, swap(): return lax.ppermute(value, 'gx', [(i, i ^ 1 << bit) for i in range(count)])  24.2 us
    all_to_all x1, waiting for transfers between devices, local(): rows = lax.all_to_all(rows, 'gx', 0, 0).reshape(count_x * each, 2 * depth)  12.2 us
    pallas_call x1, Pallas kernels, project(): pl.pallas_call(functools.partial(project_kernel, block, cuts), out_shape=...  9.65 us
    pallas_call x3, Pallas kernels, down_project(): pl.pallas_call(functools.partial(down_kernel, block, count, order), out_s...  9.55 us
    all_to_all x1, starting transfers between devices, local(): rows = lax.all_to_all(rows, 'gx', 0, 0).reshape(count_x * each, 2 * depth)  6.95 us
    unnamed x6, local copies, waits for them, and re-layouts  3.24 us
  transfers between devices with their start and end apart: 25, of which 16 were waited for; matrix products, arithmetic and copies ran while one was open for 3% of the time, Pallas kernels for 15%

profile of v1, /device:TPU:0, one launch (start us, length us, event | category | flops | bytes accessed | tf_op | source)
XLA Modules:
  0.0 124.9 jit_solution(6315214595211991050)
XLA Ops:
  0.0 1.7 %constant_dynamic-slice_fusion = (bf16[1,24,4096]{2,1,0:T(8,128)(2,1)}, bf16[24,4096]{1,0:T(8,128)(2,1)S(1)}) fusion(bf16[2,24,4096]{2,1,0:T(8,128)(2,1)} %param.3, s32[]{:T(128)S(6)} %select_n.40, s32[]{:T(128)S(6)} %select_n.41), kind=kLoop, calls=%fused_computation.58 | loop fusion | bytes 786440 | tf_op jit(solution)/shard_map/jit(dynamic_index_in_dim)/dynamic_slice | solution.py:275
  1.7 0.5 collective-permute-start
  2.2 1.1 collective-permute-done
  3.2 0.4 collective-permute-start.1
  3.6 0.3 copy-done.2
  3.9 0.4 collective-permute-start.7
  4.3 1.3 %maximum_select_fusion = bf16[2,24,4096]{2,1,0:T(8,128)(2,1)S(1)} fusion(bf16[1,24,4096]{2,1,0:T(8,128)(2,1)} %bitcast.79, bf16[1,24,4096]{2,1,0:T(8,128)(2,1)} %get-tuple-element.83, pred[]{:T(512)S(6)} %eq.2), kind=kLoop, calls=%fused_computation.24 | loop fusion | flops 589824 | bytes 786433 | tf_op jit(solution)/shard_map/jit(_where)/select_n | solution.py:279
  5.6 0.8 pad_maximum_fusion
  6.4 7.0 %all-to-all-start = ((bf16[8,24,1024]{2,1,0:T(8,128)(2,1)}), bf16[8,24,1024]{2,1,0:T(8,128)(2,1)}, u32[]{:S(2)}, u32[]{:S(2)}) async-start(bf16[8,24,1024]{2,1,0:T(8,128)(2,1)} %bitcast.75), calls=%async_computation | async-start | bytes 786432 | tf_op jit(solution)/shard_map/all_to_all | solution.py:282
  13.3 0.1 pad_add_fusion.place_ref
  13.4 12.2 %all-to-all-done = bf16[8,24,1024]{2,1,0:T(8,128)(2,1)} async-done(((bf16[8,24,1024]{2,1,0:T(8,128)(2,1)}), bf16[8,24,1024]{2,1,0:T(8,128)(2,1)}, u32[]{:S(2)}, u32[]{:S(2)}) %all-to-all-start) | async-done | bytes 393248 | tf_op jit(solution)/shard_map/all_to_all | solution.py:282
  25.7 0.0 collective-permute-done.1.other_in
  25.7 2.9 %copy-done.1 = bf16[2,512,3328]{2,1,0:T(8,128)(2,1)S(1)} copy-done((bf16[2,512,3328]{2,1,0:T(8,128)(2,1)S(1)}, bf16[2,512,3328]{2,1,0:T(8,128)(2,1)}, u32[]{:S(2)}) %copy-start.1) | copy-done | bytes 6815768
  28.6 9.7 %shard_map.37 = (bf16[2,2,2,208,128]{4,3,2,1,0:T(8,128)(2,1)S(1)}, f32[2,2,2,208,128]{4,3,2,1,0:T(8,128)S(1)}, bf16[2,2,2,208,128]{4,3,2,1,0:T(8,128)(2,1)S(1)},...) custom-call(s32[2]{0:T(128)S(1)} %pad_add_fusion.place_ref, ...), custom_call_target="tpu_custom_call" | custom-call | flops 1308622848 | bytes 6815744 | tf_op jit(solution)/shard_map/pallas_call | solution.py:129
  38.3 0.0 copy-start
  38.3 1.5 %collective-permute-start.2 = (bf16[2,2,2,208,128]{4,3,2,0,1:T(8,128)(2,1)S(1)}, bf16[2,2,2,208,128]{4,3,2,0,1:T(8,128)(2,1)S(1)}, u32[]{:S(2)}, u32[]{:S(2)}) collective-permute-start(bf16[2,2,2,208,128]{4,3,2,0,1:T(8,128)(2,1)S(1)} %copy.4), channel_id=1, source_target_pairs={{0,2},{2,0},{4,6},{6,4},{8,10},{10,8},{12,14},{14,12},{1,3},{3,1},... | collective-permute-start | bytes 1277960 | tf_op jit(solution)/shard_map/ppermute | solution.py:224
  39.9 0.1 collective-permute-start.5
  39.9 9.4 %collective-permute-done.2 = bf16[2,2,2,208,128]{4,3,2,0,1:T(8,128)(2,1)S(1)} collective-permute-done((bf16[2,2,2,208,128]{4,3,2,0,1:T(8,128)(2,1)S(1)}, bf16[2,2,2,208,128]{4,3,2,0,1:T(8,128)(2,1)S(1)}, u32[]{:S(2)}, u32[]{:S(2)}) %collective-permute-start.2) | collective-permute-done | bytes 426016 | tf_op jit(solution)/shard_map/ppermute | solution.py:224
  49.3 0.1 copy_add_fusion.2
  49.4 0.1 collective-permute-start.3
  49.5 1.2 collective-permute-done.5
  50.7 0.1 copy_add_fusion.1
  50.8 0.5 collective-permute-start.6
  51.4 1.6 %collective-permute-start.9 = (bf16[2,2,2,208,128]{4,3,2,0,1:T(8,128)(2,1)S(1)}, bf16[2,2,2,208,128]{4,3,2,0,1:T(8,128)(2,1)S(1)}, u32[]{:S(2)}, u32[]{:S(2)}) collective-permute-start(bf16[2,2,2,208,128]{4,3,2,0,1:T(8,128)(2,1)S(1)} %copy.8), channel_id=1, source_target_pairs={{0,2},{2,0},{4,6},{6,4},{8,10},{10,8},{12,14},{14,12},{1,3},{3,1},... | collective-permute-start | bytes 1277960 | tf_op jit(solution)/shard_map/ppermute | solution.py:224
  53.0 2.3 %collective-permute-done.3 = bf16[2,2,208,128]{3,2,1,0:T(8,128)(2,1)S(1)} collective-permute-done((bf16[2,2,208,128]{3,2,1,0:T(8,128)(2,1)S(1)}, bf16[2,2,208,128]{3,2,1,0:T(8,128)(2,1)S(1)}, u32[]{:S(2)}, u32[]{:S(2)}) %collective-permute-start.3) | collective-permute-done | bytes 213024 | tf_op jit(solution)/shard_map/ppermute | solution.py:224
  55.4 1.7 %collective-permute-start.4 = (bf16[1,2,208,128]{3,2,1,0:T(8,128)(2,1)S(1)}, bf16[1,2,208,128]{3,2,1,0:T(8,128)(2,1)S(1)}, u32[]{:S(2)}, u32[]{:S(2)}) collective-permute-start(bf16[1,2,208,128]{3,2,1,0:T(8,128)(2,1)S(1)} %slice.205), channel_id=1, source_target_pairs={{0,8},{2,10},{4,12},{6,14},{8,0},{10,2},{12,4},{14,6},{1,9},{3,11}... | collective-permute-start | bytes 319496 | tf_op jit(solution)/shard_map/ppermute | solution.py:224
  57.1 2.0 %collective-permute-done.6 = bf16[2,2,208,128]{3,2,1,0:T(8,128)(2,1)S(1)} collective-permute-done((bf16[2,2,208,128]{3,2,1,0:T(8,128)(2,1)S(1)}, bf16[2,2,208,128]{3,2,1,0:T(8,128)(2,1)S(1)}, u32[]{:S(2)}, u32[]{:S(2)}) %collective-permute-start.6) | collective-permute-done | bytes 213024 | tf_op jit(solution)/shard_map/ppermute | solution.py:224
  59.2 1.4 %collective-permute-start.11 = (bf16[1,2,208,128]{3,2,1,0:T(8,128)(2,1)S(1)}, bf16[1,2,208,128]{3,2,1,0:T(8,128)(2,1)S(1)}, u32[]{:S(2)}, u32[]{:S(2)}) collective-permute-start(bf16[1,2,208,128]{3,2,1,0:T(8,128)(2,1)S(1)} %slice.204), channel_id=1, source_target_pairs={{0,8},{2,10},{4,12},{6,14},{8,0},{10,2},{12,4},{14,6},{1,9},{3,11}... | collective-permute-start | bytes 319496 | tf_op jit(solution)/shard_map/ppermute | solution.py:224
  60.6 2.6 %collective-permute-done.4 = bf16[1,2,208,128]{3,2,1,0:T(8,128)(2,1)S(1)} collective-permute-done((bf16[1,2,208,128]{3,2,1,0:T(8,128)(2,1)S(1)}, bf16[1,2,208,128]{3,2,1,0:T(8,128)(2,1)S(1)}, u32[]{:S(2)}, u32[]{:S(2)}) %collective-permute-start.4) | collective-permute-done | bytes 106528 | tf_op jit(solution)/shard_map/ppermute | solution.py:224
  63.2 3.2 %shard_map.38 = (bf16[2,2,8,8192]{3,2,1,0:T(8,128)(2,1)S(1)}, f32[2,2,8,8192]{3,2,1,0:T(8,128)S(1)}) custom-call(s32[2]{0:T(128)S(1)} %pad_add_fusion.place_ref, f32[2,208,128]{2,1,0:T(8,128)S(1)} %slice_bitcast_fusion.8.keep_in, bf16[2,208,128]{2,1,0:T(8,128)(2,1)S(1)} %bitcast.73, bf16[208,8192]{1,0:T(8,128)(2,1)S(1)} %copy-done, ...), custom_call_target="tpu_custom_call" | custom-call | flops 436207616 | bytes 6815744 | tf_op jit(solution)/shard_map/pallas_call | solution.py:197
  66.4 0.1 copy_add_fusion
  66.5 0.1 collective-permute-start.10
  66.6 1.9 %collective-permute-start.8 = (bf16[2,2,8,8192]{3,2,1,0:T(8,128)(2,1)S(1)}, bf16[2,2,8,8192]{3,2,1,0:T(8,128)(2,1)S(1)}, u32[]{:S(2)}, u32[]{:S(2)}) collective-permute-start(bf16[2,2,8,8192]{3,2,1,0:T(8,128)(2,1)S(1)} %get-tuple-element.56), channel_id=1, source_target_pairs={{0,2},{2,0},{4,6},{6,4},{8,10},{10,8},{12,14},{14,12},{1,3},{3,1},... | collective-permute-start | bytes 1572872 | tf_op jit(solution)/shard_map/ppermute | solution.py:224
  68.5 0.0 collective-permute-done.11
  68.5 3.2 %shard_map.39 = (bf16[2,2,8,8192]{3,2,1,0:T(8,128)(2,1)S(1)}, f32[2,2,8,8192]{3,2,1,0:T(8,128)S(1)}) custom-call(s32[2]{0:T(128)S(1)} %pad_add_fusion.place_ref, f32[2,208,128]{2,1,0:T(8,128)S(1)} %slice_bitcast_fusion.7.keep_in, bf16[2,208,128]{2,1,0:T(8,128)(2,1)S(1)} %bitcast.72, bf16[208,8192]{1,0:T(8,128)(2,1)S(1)} %copy-done, ...), custom_call_target="tpu_custom_call" | custom-call | flops 436207616 | bytes 6815744 | tf_op jit(solution)/shard_map/pallas_call | solution.py:197
  71.7 2.1 %collective-permute-start.13 = (bf16[2,2,8,8192]{3,2,1,0:T(8,128)(2,1)S(1)}, bf16[2,2,8,8192]{3,2,1,0:T(8,128)(2,1)S(1)}, u32[]{:S(2)}, u32[]{:S(2)}) collective-permute-start(bf16[2,2,8,8192]{3,2,1,0:T(8,128)(2,1)S(1)} %get-tuple-element.61), channel_id=1, source_target_pairs={{0,4},{2,6},{4,0},{6,2},{8,12},{10,14},{12,8},{14,10},{1,5},{3,7},... | collective-permute-start | bytes 1572872 | tf_op jit(solution)/shard_map/ppermute | solution.py:224
  73.7 0.0 collective-permute-done.10
  73.7 0.1 fusion.3
  73.8 1.0 collective-permute-start.14
  74.9 4.7 %collective-permute-done.8 = bf16[2,2,8,8192]{3,2,1,0:T(8,128)(2,1)S(1)} collective-permute-done((bf16[2,2,8,8192]{3,2,1,0:T(8,128)(2,1)S(1)}, bf16[2,2,8,8192]{3,2,1,0:T(8,128)(2,1)S(1)}, u32[]{:S(2)}, u32[]{:S(2)}) %collective-permute-start.8) | collective-permute-done | bytes 524320 | tf_op jit(solution)/shard_map/ppermute | solution.py:224
  79.6 0.1 convert_add_fusion.2
  79.7 0.4 collective-permute-start.12
  80.1 7.1 %collective-permute-done.14 = bf16[1,2,208,128]{3,2,1,0:T(8,128)(2,1)S(1)} collective-permute-done((bf16[1,2,208,128]{3,2,1,0:T(8,128)(2,1)S(1)}, bf16[1,2,208,128]{3,2,1,0:T(8,128)(2,1)S(1)}, u32[]{:S(2)}, u32[]{:S(2)}) %collective-permute-start.14) | collective-permute-done | bytes 106528 | tf_op jit(solution)/shard_map/ppermute | solution.py:224
  87.2 3.2 %shard_map.40 = (bf16[2,2,8,8192]{3,2,1,0:T(8,128)(2,1)S(1)}, f32[2,2,8,8192]{3,2,1,0:T(8,128)S(1)}) custom-call(s32[2]{0:T(128)S(1)} %pad_add_fusion.place_ref, f32[2,208,128]{2,1,0:T(8,128)S(1)} %slice_bitcast_fusion.6.keep_in, bf16[2,208,128]{2,1,0:T(8,128)(2,1)S(1)} %bitcast.74, bf16[208,8192]{1,0:T(8,128)(2,1)S(1)} %copy-done, ...), custom_call_target="tpu_custom_call" | custom-call | flops 436207616 | bytes 6815744 | tf_op jit(solution)/shard_map/pallas_call | solution.py:197
  90.4 4.6 %collective-permute-start.19 = (bf16[2,2,8,8192]{3,2,1,0:T(8,128)(2,1)S(1)}, bf16[2,2,8,8192]{3,2,1,0:T(8,128)(2,1)S(1)}, u32[]{:S(2)}, u32[]{:S(2)}) collective-permute-start(bf16[2,2,8,8192]{3,2,1,0:T(8,128)(2,1)S(1)} %get-tuple-element.66), channel_id=1, source_target_pairs={{0,4},{2,6},{4,0},{6,2},{8,12},{10,14},{12,8},{14,10},{1,5},{3,7},... | collective-permute-start | bytes 1572872 | tf_op jit(solution)/shard_map/ppermute | solution.py:224
  95.0 0.0 collective-permute-done.13
  95.0 0.1 convert_add_fusion.1
  95.1 0.7 collective-permute-start.16
  95.9 1.6 %collective-permute-start.15 = (bf16[1,8,8192]{2,1,0:T(8,128)(2,1)S(1)}, bf16[1,8,8192]{2,1,0:T(8,128)(2,1)S(1)}, u32[]{:S(2)}, u32[]{:S(2)}) collective-permute-start(bf16[1,8,8192]{2,1,0:T(8,128)(2,1)S(1)} %slice.202), channel_id=1, source_target_pairs={{0,8},{2,10},{4,12},{6,14},{8,0},{10,2},{12,4},{14,6},{1,9},{3,11}... | collective-permute-start | bytes 393224 | tf_op jit(solution)/shard_map/ppermute | solution.py:224
  97.5 4.1 %collective-permute-done.16 = bf16[2,8,8192]{2,1,0:T(8,128)(2,1)S(1)} collective-permute-done((bf16[2,8,8192]{2,1,0:T(8,128)(2,1)S(1)}, bf16[2,8,8192]{2,1,0:T(8,128)(2,1)S(1)}, u32[]{:S(2)}, u32[]{:S(2)}) %collective-permute-start.16) | collective-permute-done | bytes 262176 | tf_op jit(solution)/shard_map/ppermute | solution.py:224
  101.6 0.1 collective-permute-start.18
  101.7 5.1 %collective-permute-done.15 = bf16[1,8,8192]{2,1,0:T(8,128)(2,1)S(1)} collective-permute-done((bf16[1,8,8192]{2,1,0:T(8,128)(2,1)S(1)}, bf16[1,8,8192]{2,1,0:T(8,128)(2,1)S(1)}, u32[]{:S(2)}, u32[]{:S(2)}) %collective-permute-start.15) | collective-permute-done | bytes 131104 | tf_op jit(solution)/shard_map/ppermute | solution.py:224
  106.9 0.1 collective-permute-start.17
  107.0 1.7 %collective-permute-done.19 = bf16[2,2,8,8192]{3,2,1,0:T(8,128)(2,1)S(1)} collective-permute-done((bf16[2,2,8,8192]{3,2,1,0:T(8,128)(2,1)S(1)}, bf16[2,2,8,8192]{3,2,1,0:T(8,128)(2,1)S(1)}, u32[]{:S(2)}, u32[]{:S(2)}) %collective-permute-start.19) | collective-permute-done | bytes 524320 | tf_op jit(solution)/shard_map/ppermute | solution.py:224
  108.7 0.1 convert_add_fusion
  108.9 1.5 %collective-permute-start.21 = (bf16[2,8,8192]{2,1,0:T(8,128)(2,1)S(1)}, bf16[2,8,8192]{2,1,0:T(8,128)(2,1)S(1)}, u32[]{:S(2)}, u32[]{:S(2)}) collective-permute-start(bf16[2,8,8192]{2,1,0:T(8,128)(2,1)S(1)} %fusion.8), channel_id=1, source_target_pairs={{0,2},{2,0},{4,6},{6,4},{8,10},{10,8},{12,14},{14,12},{1,3},{3,1},... | collective-permute-start | bytes 786440 | tf_op jit(solution)/shard_map/ppermute | solution.py:224
  110.4 1.9 %collective-permute-done.18 = bf16[1,8,8192]{2,1,0:T(8,128)(2,1)S(1)} collective-permute-done((bf16[1,8,8192]{2,1,0:T(8,128)(2,1)S(1)}, bf16[1,8,8192]{2,1,0:T(8,128)(2,1)S(1)}, u32[]{:S(2)}, u32[]{:S(2)}) %collective-permute-start.18) | collective-permute-done | bytes 131104 | tf_op jit(solution)/shard_map/ppermute | solution.py:224
  112.4 0.1 collective-permute-start.20
  112.5 3.4 %collective-permute-done.21 = bf16[2,8,8192]{2,1,0:T(8,128)(2,1)S(1)} collective-permute-done((bf16[2,8,8192]{2,1,0:T(8,128)(2,1)S(1)}, bf16[2,8,8192]{2,1,0:T(8,128)(2,1)S(1)}, u32[]{:S(2)}, u32[]{:S(2)}) %collective-permute-start.21) | collective-permute-done | bytes 262176 | tf_op jit(solution)/shard_map/ppermute | solution.py:224
  116.0 3.4 %collective-permute-start.22 = (bf16[1,8,8192]{2,1,0:T(8,128)(2,1)S(1)}, bf16[1,8,8192]{2,1,0:T(8,128)(2,1)S(1)}, u32[]{:S(2)}, u32[]{:S(2)}) collective-permute-start(bf16[1,8,8192]{2,1,0:T(8,128)(2,1)S(1)} %slice.200), channel_id=1, source_target_pairs={{0,8},{2,10},{4,12},{6,14},{8,0},{10,2},{12,4},{14,6},{1,9},{3,11}... | collective-permute-start | bytes 393224 | tf_op jit(solution)/shard_map/ppermute | solution.py:224
  119.4 3.3 %collective-permute-done.22 = bf16[1,8,8192]{2,1,0:T(8,128)(2,1)S(1)} collective-permute-done((bf16[1,8,8192]{2,1,0:T(8,128)(2,1)S(1)}, bf16[1,8,8192]{2,1,0:T(8,128)(2,1)S(1)}, u32[]{:S(2)}, u32[]{:S(2)}) %collective-permute-start.22) | collective-permute-done | bytes 131104 | tf_op jit(solution)/shard_map/ppermute | solution.py:224
  122.8 0.1 collective-permute-start.23
  122.9 1.2 collective-permute-done.23
  124.2 0.8 pad_maximum_fusion.1
  (41 shorter events, 0.8 us)
Async XLA Ops:
  1.7 1.5 %collective-permute-start = (bf16[24,4096]{1,0:T(8,128)(2,1)S(1)}, bf16[24,4096]{1,0:T(8,128)(2,1)S(1)}, u32[]{:S(2)}, u32[]{:S(2)}) collective-permute-start(bf16[24,4096]{1,0:T(8,128)(2,1)S(1)} %get-tuple-element.84), channel_id=1, source_target_pairs={{0,1},{1,0},{2,3},{3,2},{4,5},{5,4},{6,7},{7,6},{8,9},{9,8},{10,11... | collective-permute-start | bytes 589832 | tf_op jit(solution)/shard_map/ppermute | solution.py:228
  3.2 0.7 copy-start.2
  3.2 22.4 %collective-permute-start.1 = (bf16[2,512,3328]{2,1,0:T(8,128)(2,1)}, bf16[2,512,3328]{2,1,0:T(8,128)(2,1)}, u32[]{:S(2)}, u32[]{:S(2)}) collective-permute-start(bf16[2,512,3328]{2,1,0:T(8,128)(2,1)} %own_in.1), channel_id=1, source_target_pairs={{0,1},{1,0},{2,3},{3,2},{4,5},{5,4},{6,7},{7,6},{8,9},{9,8},{10,11... | collective-permute-start | bytes 20447240 | tf_op jit(solution)/shard_map/ppermute | solution.py:228
  3.9 59.3 %collective-permute-start.7 = (bf16[208,8192]{1,0:T(8,128)(2,1)}, bf16[208,8192]{1,0:T(8,128)(2,1)S(1)}, u32[]{:S(2)}, u32[]{:S(2)}) collective-permute-start(bf16[208,8192]{1,0:T(8,128)(2,1)} %own.5), channel_id=1, source_target_pairs={{0,1},{1,0},{2,3},{3,2},{4,5},{5,4},{6,7},{7,6},{8,9},{9,8},{10,11... | collective-permute-start | bytes 10223624 | tf_op jit(solution)/shard_map/ppermute | solution.py:228
  6.4 19.3 %all-to-all-start = ((bf16[8,24,1024]{2,1,0:T(8,128)(2,1)}), bf16[8,24,1024]{2,1,0:T(8,128)(2,1)}, u32[]{:S(2)}, u32[]{:S(2)}) async-start(bf16[8,24,1024]{2,1,0:T(8,128)(2,1)} %bitcast.75), calls=%async_computation | async-start | bytes 786432 | tf_op jit(solution)/shard_map/all_to_all | solution.py:282
  25.7 2.9 %copy-start.1 = (bf16[2,512,3328]{2,1,0:T(8,128)(2,1)S(1)}, bf16[2,512,3328]{2,1,0:T(8,128)(2,1)}, u32[]{:S(2)}) copy-start(bf16[2,512,3328]{2,1,0:T(8,128)(2,1)} %own_in.1) | copy-start | bytes 20447236
  38.3 24.9 %copy-start = (bf16[208,8192]{1,0:T(8,128)(2,1)S(1)}, bf16[208,8192]{1,0:T(8,128)(2,1)}, u32[]{:S(2)}) copy-start(bf16[208,8192]{1,0:T(8,128)(2,1)} %own.5) | copy-start | bytes 10223620
  38.3 11.0 %collective-permute-start.2 = (bf16[2,2,2,208,128]{4,3,2,0,1:T(8,128)(2,1)S(1)}, bf16[2,2,2,208,128]{4,3,2,0,1:T(8,128)(2,1)S(1)}, u32[]{:S(2)}, u32[]{:S(2)}) collective-permute-start(bf16[2,2,2,208,128]{4,3,2,0,1:T(8,128)(2,1)S(1)} %copy.4), channel_id=1, source_target_pairs={{0,2},{2,0},{4,6},{6,4},{8,10},{10,8},{12,14},{14,12},{1,3},{3,1},... | collective-permute-start | bytes 1277960 | tf_op jit(solution)/shard_map/ppermute | solution.py:224
  39.9 10.9 %collective-permute-start.5 = (bf16[2,2,2,208,128]{4,3,2,0,1:T(8,128)(2,1)S(1)}, bf16[2,2,2,208,128]{4,3,2,0,1:T(8,128)(2,1)S(1)}, u32[]{:S(2)}, u32[]{:S(2)}) collective-permute-start(bf16[2,2,2,208,128]{4,3,2,0,1:T(8,128)(2,1)S(1)} %copy.6), channel_id=1, source_target_pairs={{0,4},{2,6},{4,0},{6,2},{8,12},{10,14},{12,8},{14,10},{1,5},{3,7},... | collective-permute-start | bytes 1277960 | tf_op jit(solution)/shard_map/ppermute | solution.py:224
  49.4 5.9 %collective-permute-start.3 = (bf16[2,2,208,128]{3,2,1,0:T(8,128)(2,1)S(1)}, bf16[2,2,208,128]{3,2,1,0:T(8,128)(2,1)S(1)}, u32[]{:S(2)}, u32[]{:S(2)}) collective-permute-start(bf16[2,2,208,128]{3,2,1,0:T(8,128)(2,1)S(1)} %fusion.12), channel_id=1, source_target_pairs={{0,4},{2,6},{4,0},{6,2},{8,12},{10,14},{12,8},{14,10},{1,5},{3,7},... | collective-permute-start | bytes 638984 | tf_op jit(solution)/shard_map/ppermute | solution.py:224
  50.8 8.3 %collective-permute-start.6 = (bf16[2,2,208,128]{3,2,1,0:T(8,128)(2,1)S(1)}, bf16[2,2,208,128]{3,2,1,0:T(8,128)(2,1)S(1)}, u32[]{:S(2)}, u32[]{:S(2)}) collective-permute-start(bf16[2,2,208,128]{3,2,1,0:T(8,128)(2,1)S(1)} %fusion.13), channel_id=1, source_target_pairs={{0,2},{2,0},{4,6},{6,4},{8,10},{10,8},{12,14},{14,12},{1,3},{3,1},... | collective-permute-start | bytes 638984 | tf_op jit(solution)/shard_map/ppermute | solution.py:224
  51.4 15.0 %collective-permute-start.9 = (bf16[2,2,2,208,128]{4,3,2,0,1:T(8,128)(2,1)S(1)}, bf16[2,2,2,208,128]{4,3,2,0,1:T(8,128)(2,1)S(1)}, u32[]{:S(2)}, u32[]{:S(2)}) collective-permute-start(bf16[2,2,2,208,128]{4,3,2,0,1:T(8,128)(2,1)S(1)} %copy.8), channel_id=1, source_target_pairs={{0,2},{2,0},{4,6},{6,4},{8,10},{10,8},{12,14},{14,12},{1,3},{3,1},... | collective-permute-start | bytes 1277960 | tf_op jit(solution)/shard_map/ppermute | solution.py:224
  55.4 7.8 %collective-permute-start.4 = (bf16[1,2,208,128]{3,2,1,0:T(8,128)(2,1)S(1)}, bf16[1,2,208,128]{3,2,1,0:T(8,128)(2,1)S(1)}, u32[]{:S(2)}, u32[]{:S(2)}) collective-permute-start(bf16[1,2,208,128]{3,2,1,0:T(8,128)(2,1)S(1)} %slice.205), channel_id=1, source_target_pairs={{0,8},{2,10},{4,12},{6,14},{8,0},{10,2},{12,4},{14,6},{1,9},{3,11}... | collective-permute-start | bytes 319496 | tf_op jit(solution)/shard_map/ppermute | solution.py:224
  59.2 9.3 %collective-permute-start.11 = (bf16[1,2,208,128]{3,2,1,0:T(8,128)(2,1)S(1)}, bf16[1,2,208,128]{3,2,1,0:T(8,128)(2,1)S(1)}, u32[]{:S(2)}, u32[]{:S(2)}) collective-permute-start(bf16[1,2,208,128]{3,2,1,0:T(8,128)(2,1)S(1)} %slice.204), channel_id=1, source_target_pairs={{0,8},{2,10},{4,12},{6,14},{8,0},{10,2},{12,4},{14,6},{1,9},{3,11}... | collective-permute-start | bytes 319496 | tf_op jit(solution)/shard_map/ppermute | solution.py:224
  66.5 7.2 %collective-permute-start.10 = (bf16[2,2,208,128]{3,2,1,0:T(8,128)(2,1)S(1)}, bf16[2,2,208,128]{3,2,1,0:T(8,128)(2,1)S(1)}, u32[]{:S(2)}, u32[]{:S(2)}) collective-permute-start(bf16[2,2,208,128]{3,2,1,0:T(8,128)(2,1)S(1)} %fusion.14), channel_id=1, source_target_pairs={{0,4},{2,6},{4,0},{6,2},{8,12},{10,14},{12,8},{14,10},{1,5},{3,7},... | collective-permute-start | bytes 638984 | tf_op jit(solution)/shard_map/ppermute | solution.py:224
  66.6 12.9 %collective-permute-start.8 = (bf16[2,2,8,8192]{3,2,1,0:T(8,128)(2,1)S(1)}, bf16[2,2,8,8192]{3,2,1,0:T(8,128)(2,1)S(1)}, u32[]{:S(2)}, u32[]{:S(2)}) collective-permute-start(bf16[2,2,8,8192]{3,2,1,0:T(8,128)(2,1)S(1)} %get-tuple-element.56), channel_id=1, source_target_pairs={{0,2},{2,0},{4,6},{6,4},{8,10},{10,8},{12,14},{14,12},{1,3},{3,1},... | collective-permute-start | bytes 1572872 | tf_op jit(solution)/shard_map/ppermute | solution.py:224
  71.7 23.3 %collective-permute-start.13 = (bf16[2,2,8,8192]{3,2,1,0:T(8,128)(2,1)S(1)}, bf16[2,2,8,8192]{3,2,1,0:T(8,128)(2,1)S(1)}, u32[]{:S(2)}, u32[]{:S(2)}) collective-permute-start(bf16[2,2,8,8192]{3,2,1,0:T(8,128)(2,1)S(1)} %get-tuple-element.61), channel_id=1, source_target_pairs={{0,4},{2,6},{4,0},{6,2},{8,12},{10,14},{12,8},{14,10},{1,5},{3,7},... | collective-permute-start | bytes 1572872 | tf_op jit(solution)/shard_map/ppermute | solution.py:224
  73.8 13.4 %collective-permute-start.14 = (bf16[1,2,208,128]{3,2,1,0:T(8,128)(2,1)S(1)}, bf16[1,2,208,128]{3,2,1,0:T(8,128)(2,1)S(1)}, u32[]{:S(2)}, u32[]{:S(2)}) collective-permute-start(bf16[1,2,208,128]{3,2,1,0:T(8,128)(2,1)S(1)} %slice.203), channel_id=1, source_target_pairs={{0,8},{2,10},{4,12},{6,14},{8,0},{10,2},{12,4},{14,6},{1,9},{3,11}... | collective-permute-start | bytes 319496 | tf_op jit(solution)/shard_map/ppermute | solution.py:224
  79.7 16.1 %collective-permute-start.12 = (bf16[2,8,8192]{2,1,0:T(8,128)(2,1)S(1)}, bf16[2,8,8192]{2,1,0:T(8,128)(2,1)S(1)}, u32[]{:S(2)}, u32[]{:S(2)}) collective-permute-start(bf16[2,8,8192]{2,1,0:T(8,128)(2,1)S(1)} %fusion.6), channel_id=1, source_target_pairs={{0,4},{2,6},{4,0},{6,2},{8,12},{10,14},{12,8},{14,10},{1,5},{3,7},... | collective-permute-start | bytes 786440 | tf_op jit(solution)/shard_map/ppermute | solution.py:224
  90.4 18.3 %collective-permute-start.19 = (bf16[2,2,8,8192]{3,2,1,0:T(8,128)(2,1)S(1)}, bf16[2,2,8,8192]{3,2,1,0:T(8,128)(2,1)S(1)}, u32[]{:S(2)}, u32[]{:S(2)}) collective-permute-start(bf16[2,2,8,8192]{3,2,1,0:T(8,128)(2,1)S(1)} %get-tuple-element.66), channel_id=1, source_target_pairs={{0,4},{2,6},{4,0},{6,2},{8,12},{10,14},{12,8},{14,10},{1,5},{3,7},... | collective-permute-start | bytes 1572872 | tf_op jit(solution)/shard_map/ppermute | solution.py:224
  95.1 6.4 %collective-permute-start.16 = (bf16[2,8,8192]{2,1,0:T(8,128)(2,1)S(1)}, bf16[2,8,8192]{2,1,0:T(8,128)(2,1)S(1)}, u32[]{:S(2)}, u32[]{:S(2)}) collective-permute-start(bf16[2,8,8192]{2,1,0:T(8,128)(2,1)S(1)} %fusion.7), channel_id=1, source_target_pairs={{0,2},{2,0},{4,6},{6,4},{8,10},{10,8},{12,14},{14,12},{1,3},{3,1},... | collective-permute-start | bytes 786440 | tf_op jit(solution)/shard_map/ppermute | solution.py:224
  95.9 11.0 %collective-permute-start.15 = (bf16[1,8,8192]{2,1,0:T(8,128)(2,1)S(1)}, bf16[1,8,8192]{2,1,0:T(8,128)(2,1)S(1)}, u32[]{:S(2)}, u32[]{:S(2)}) collective-permute-start(bf16[1,8,8192]{2,1,0:T(8,128)(2,1)S(1)} %slice.202), channel_id=1, source_target_pairs={{0,8},{2,10},{4,12},{6,14},{8,0},{10,2},{12,4},{14,6},{1,9},{3,11}... | collective-permute-start | bytes 393224 | tf_op jit(solution)/shard_map/ppermute | solution.py:224
  101.6 10.7 %collective-permute-start.18 = (bf16[1,8,8192]{2,1,0:T(8,128)(2,1)S(1)}, bf16[1,8,8192]{2,1,0:T(8,128)(2,1)S(1)}, u32[]{:S(2)}, u32[]{:S(2)}) collective-permute-start(bf16[1,8,8192]{2,1,0:T(8,128)(2,1)S(1)} %slice.201), channel_id=1, source_target_pairs={{0,8},{2,10},{4,12},{6,14},{8,0},{10,2},{12,4},{14,6},{1,9},{3,11}... | collective-permute-start | bytes 393224 | tf_op jit(solution)/shard_map/ppermute | solution.py:224
  106.9 5.5 %collective-permute-start.17 = (bf16[8,4096]{1,0:T(8,128)(2,1)S(1)}, bf16[8,4096]{1,0:T(8,128)(2,1)S(1)}, u32[]{:S(2)}, u32[]{:S(2)}) collective-permute-start(bf16[8,4096]{1,0:T(8,128)(2,1)S(1)} %get-tuple-element.86), channel_id=1, source_target_pairs={{0,1},{1,0},{2,3},{3,2},{4,5},{5,4},{6,7},{7,6},{8,9},{9,8},{10,11... | collective-permute-start | bytes 196616 | tf_op jit(solution)/shard_map/ppermute | solution.py:228
  108.9 7.0 %collective-permute-start.21 = (bf16[2,8,8192]{2,1,0:T(8,128)(2,1)S(1)}, bf16[2,8,8192]{2,1,0:T(8,128)(2,1)S(1)}, u32[]{:S(2)}, u32[]{:S(2)}) collective-permute-start(bf16[2,8,8192]{2,1,0:T(8,128)(2,1)S(1)} %fusion.8), channel_id=1, source_target_pairs={{0,2},{2,0},{4,6},{6,4},{8,10},{10,8},{12,14},{14,12},{1,3},{3,1},... | collective-permute-start | bytes 786440 | tf_op jit(solution)/shard_map/ppermute | solution.py:224
  112.4 7.1 %collective-permute-start.20 = (bf16[8,4096]{1,0:T(8,128)(2,1)S(1)}, bf16[8,4096]{1,0:T(8,128)(2,1)S(1)}, u32[]{:S(2)}, u32[]{:S(2)}) collective-permute-start(bf16[8,4096]{1,0:T(8,128)(2,1)S(1)} %get-tuple-element.88), channel_id=1, source_target_pairs={{0,1},{1,0},{2,3},{3,2},{4,5},{5,4},{6,7},{7,6},{8,9},{9,8},{10,11... | collective-permute-start | bytes 196616 | tf_op jit(solution)/shard_map/ppermute | solution.py:228
  116.0 6.8 %collective-permute-start.22 = (bf16[1,8,8192]{2,1,0:T(8,128)(2,1)S(1)}, bf16[1,8,8192]{2,1,0:T(8,128)(2,1)S(1)}, u32[]{:S(2)}, u32[]{:S(2)}) collective-permute-start(bf16[1,8,8192]{2,1,0:T(8,128)(2,1)S(1)} %slice.200), channel_id=1, source_target_pairs={{0,8},{2,10},{4,12},{6,14},{8,0},{10,2},{12,4},{14,6},{1,9},{3,11}... | collective-permute-start | bytes 393224 | tf_op jit(solution)/shard_map/ppermute | solution.py:224
  122.8 1.3 %collective-permute-start.23 = (bf16[8,4096]{1,0:T(8,128)(2,1)S(1)}, bf16[8,4096]{1,0:T(8,128)(2,1)S(1)}, u32[]{:S(2)}, u32[]{:S(2)}) collective-permute-start(bf16[8,4096]{1,0:T(8,128)(2,1)S(1)} %get-tuple-element.90), channel_id=1, source_target_pairs={{0,1},{1,0},{2,3},{3,2},{4,5},{5,4},{6,7},{7,6},{8,9},{9,8},{10,11... | collective-permute-start | bytes 196616 | tf_op jit(solution)/shard_map/ppermute | solution.py:228

commit v2 on v1

--- a/solution.py
+++ b/solution.py
@@ -9,7 +9,6 @@
 
 LANES = 128
 QUAD = 4
-VMEM = 20 * 1024 * 1024
 
 
 ORDERS = [((0, 1), (0, 1)), ((1, 0), (1, 0)), ((0, 1), (1, 0))]
@@ -23,19 +22,39 @@
 def place(relative, order, send, keep, value):
     first = (relative >> order[0]) & 1
     second = (relative >> order[1]) & 1
-    group = 0 if send.shape[0] == 1 else relative >> 2
+    group = 0 if send.shape[1] == 1 else relative >> 2
 
     @pl.when(first == 1)
     def _():
-        send[group, second] = value.astype(send.dtype)
+        send[second, group] = value.astype(send.dtype)
 
     @pl.when(first == 0)
     def _():
-        keep[group, second] = value
-
-
-def project_kernel(block, cuts, place_ref, tokens, own_in, other_in, *refs):
-    outs, (own, other, accs, sems) = refs[:-4], refs[-4:]
+        keep[second, group] = value
+
+
+def deal_kernel(place_ref, tokens, *messages):
+    count, wide = len(messages), messages[0].shape[1]
+    for turn, message in enumerate(messages):
+        target = lax.rem(place_ref[0] + turn, count)
+        message[...] = tokens[:, pl.ds(pl.multiple_of(target * wide, LANES), wide)]
+
+
+def deal(spot, tokens, count):
+    rows, features = tokens.shape
+    inside = pl.BlockSpec(memory_space=pltpu.VMEM)
+    return pl.pallas_call(
+        deal_kernel,
+        out_shape=[jax.ShapeDtypeStruct((rows, features // count), tokens.dtype)] * count,
+        in_specs=[pl.BlockSpec(memory_space=pltpu.SMEM), inside],
+        out_specs=[inside] * count,
+        compiler_params=pltpu.CompilerParams(vmem_limit_bytes=8 * 1024 * 1024),
+    )(spot, tokens)
+
+
+def project_kernel(block, cuts, messages, place_ref, *refs):
+    arrived, own_in, other_in = refs[:messages], refs[messages], refs[messages + 1]
+    outs, (tokens, own, other, accs, sems) = refs[messages + 2 : -5], refs[-5:]
     chip, core = place_ref[0], place_ref[1]
     chips, each = tokens.shape[0] // cuts[-1][1], cuts[-1][1]
     halves, depth, wide = own.shape[0], own.shape[1], QUAD * block
@@ -51,6 +70,10 @@
             ]
             for load in loads[half, group]:
                 load.start()
+    size = arrived[0].shape[0]
+    for turn, message in enumerate(arrived):
+        source = lax.rem(chip + messages - turn, messages) if messages > 1 else 0
+        tokens[pl.ds(pl.multiple_of(source * size, size), size), :] = message[...]
     low, high = tokens[:, :depth], tokens[:, depth:]
     first_rows = jnp.where(core == 0, low, high)
     second_rows = jnp.where(core == 0, high, low)
@@ -95,11 +118,11 @@
 
                 @pl.when(a == 1)
                 def _():
-                    send[outer, b, half] = value.astype(send.dtype)
+                    send[b, outer, half] = value.astype(send.dtype)
 
                 @pl.when(a == 0)
                 def _():
-                    keep[outer, b, half] = value
+                    keep[b, outer, half] = value
 
     for half in range(halves):
         for group in range(own.shape[2] // span):
@@ -111,37 +134,38 @@
                 lax.fori_loop(0, groups, lambda g, c: step(half, g, accs.at[0]), None)
 
 
-def project(spot, tokens, own, other, count_x, cuts, stages):
+def project(spot, arrived, own, other, count_x, cuts, stages):
     block = own.shape[2] // count_x
-    rows, depth = tokens.shape[0], own.shape[1]
+    rows, depth = sum(t.shape[0] for t in arrived), own.shape[1]
     groups = count_x // QUAD
     if groups > 2 and own.shape[0] > 1:
-        two = [project(spot, tokens, own[h : h + 1], other[h : h + 1], count_x, cuts, stages) for h in range(2)]
+        two = [project(spot, arrived, own[h : h + 1], other[h : h + 1], count_x, cuts, stages) for h in range(2)]
         return [jnp.concatenate(pair, axis=2) for pair in zip(*two)]
     shapes = []
     for first, last, _ in cuts:
         lines = count_x * (last - first) * block // LANES
         for kind in (wire_type(0, stages), jnp.float32):
-            shapes.append(jax.ShapeDtypeStruct((groups, 2, own.shape[0], lines, LANES), kind))
+            shapes.append(jax.ShapeDtypeStruct((2, groups, own.shape[0], lines, LANES), kind))
     inside = pl.BlockSpec(memory_space=pltpu.VMEM)
     scratch = jax.ShapeDtypeStruct((2, rows, QUAD * block), jnp.float32)
-    held = sum(t.size * t.dtype.itemsize for t in [tokens, own, other, scratch, *shapes])
+    held = sum(t.size * t.dtype.itemsize for t in [*arrived, *arrived, own, other, scratch, *shapes])
     return pl.pallas_call(
-        functools.partial(project_kernel, block, cuts),
+        functools.partial(project_kernel, block, cuts, len(arrived)),
         out_shape=shapes,
-        in_specs=[pl.BlockSpec(memory_space=pltpu.SMEM), inside] + [pl.BlockSpec(memory_space=pltpu.HBM)] * 2,
+        in_specs=[pl.BlockSpec(memory_space=pltpu.SMEM)] + [inside] * len(arrived) + [pl.BlockSpec(memory_space=pltpu.HBM)] * 2,
         out_specs=[inside] * len(shapes),
         scratch_shapes=[
+            pltpu.VMEM((rows, 2 * depth), arrived[0].dtype),
             pltpu.VMEM(own.shape, own.dtype),
             pltpu.VMEM(own.shape, own.dtype),
             pltpu.VMEM(scratch.shape, scratch.dtype),
             pltpu.SemaphoreType.DMA((2, own.shape[0], 2)),
         ],
-        compiler_params=pltpu.CompilerParams(vmem_limit_bytes=held + 4 * 1024 * 1024),
+        compiler_params=pltpu.CompilerParams(vmem_limit_bytes=max(held + 4 * 1024 * 1024, 44 * 1024 * 1024)),
         cost_estimate=pl.CostEstimate(
             flops=4 * rows * depth * own.shape[2], bytes_accessed=2 * own.size, transcendentals=0
         ),
-    )(spot, tokens, own, other)
+    )(spot, *arrived, own, other)
 
 
 def down_kernel(block, count, order, place_ref, keep_in, recv_in, own, other, send, keep, hidden):
@@ -178,10 +202,10 @@
         jnp.where(core == 0, low, high), own[...], preferred_element_type=jnp.float32
     ) + jnp.dot(jnp.where(core == 0, high, low), other[...], preferred_element_type=jnp.float32)
     product = product[:count] + product[count:]
-    chips = 4 * send.shape[0]
+    chips = 4 * send.shape[1]
     each = count // chips
     for owner in range(chips):
-        place(owner ^ chip, order, send, keep, product[owner * each : (owner + 1) * each])
+        place(owner ^ lax.rem(chip, chips), order, send, keep, product[owner * each : (owner + 1) * each])
 
 
 def down_project(spot, keep, recv, own, other, count, order, count_x, stages, span=(0, 1), wide=4096):
@@ -189,15 +213,15 @@
     part, parts = span
     features = features // parts
     wide = min(wide, features)
-    groups = count_x // QUAD
-    each = count // count_x
+    groups = count_x // 2 // QUAD
+    each = count // (count_x // 2)
     whole = pl.BlockSpec(keep.shape, lambda c, s: (0, 0, 0))
-    out = pl.BlockSpec((groups, 2, each, wide), lambda c, s: (0, 0, 0, c))
+    out = pl.BlockSpec((2, groups, each, wide), lambda c, s: (0, 0, 0, c))
     weights = pl.BlockSpec((block // 2, wide), lambda c, s: (0, part * (features // wide) + c))
     return pl.pallas_call(
         functools.partial(down_kernel, block, count, order),
         out_shape=[
-            jax.ShapeDtypeStruct((groups, 2, each, features), kind)
+            jax.ShapeDtypeStruct((2, groups, each, features), kind)
             for kind in (wire_type(0, stages), jnp.float32)
         ],
         grid_spec=pltpu.PrefetchScalarGridSpec(
@@ -212,7 +236,9 @@
             out_specs=[out, out],
             scratch_shapes=[pltpu.VMEM((2 * count, block), jnp.bfloat16)],
         ),
-        compiler_params=pltpu.CompilerParams(vmem_limit_bytes=VMEM),
+        compiler_params=pltpu.CompilerParams(
+            vmem_limit_bytes=4 * block * wide + 20 * count * wide + 4 * 1024 * 1024
+        ),
         cost_estimate=pl.CostEstimate(
             flops=2 * count * block * features, bytes_accessed=2 * block * features, transcendentals=0
         ),
@@ -232,14 +258,14 @@
     return value if done is None else lax.optimization_barrier((value, done))[0]
 
 
-def halving(send, keep, order, stages, done):
+def halving(send, keep, order, count, stages, done):
     recv = swap(after(send, done), order[0])
     done = yield send
-    for stage in range(1, stages):
+    for stage in range(1, count):
         acc = keep + after(recv, done).astype(jnp.float32)
         kind = wire_type(stage, stages)
         if stage == 1:
-            send, keep, bit = acc[:, 1].astype(kind), acc[:, 0], order[1]
+            send, keep, bit = acc[1].astype(kind), acc[0], order[1]
         else:
             half = acc.shape[0] // 2
             send, keep, bit = acc[half:].astype(kind), acc[:half], 1 + half.bit_length()
@@ -248,20 +274,27 @@
     return keep[0], after(recv, done)[0]
 
 
-def chunk_steps(spot, parts, downs, count, orders, count_x, stages):
-    core = spot[1]
+def move(value, pairs):
+    return lax.ppermute(value, ("gx", "gy"), [(2 * a + b, 2 * c + d) for (a, b), (c, d) in pairs])
+
+
+def chunk_steps(spot, flags, parts, downs, count, orders, count_x, stages):
+    first_core, owner = flags
     done = yield
-    keep, recv = yield from halving(parts[0], parts[1], orders[0], stages, done)
+    keep, recv = yield from halving(parts[0], parts[1], orders[0], stages, stages, done)
     send, keep = down_project(spot, keep, recv, *downs, count, orders[1], count_x, stages)
-    keep, recv = yield from halving(send, keep, orders[1], stages, None)
-    mixed = (keep + recv.astype(jnp.float32)).astype(jnp.bfloat16)
-    halves = mixed.reshape(mixed.shape[0], 2, -1)
-    mine = lax.dynamic_index_in_dim(halves, core, 1, False)
-    send = lax.dynamic_index_in_dim(halves, 1 - core, 1, False)
-    theirs = swap_cores(send)
+    keep, recv = yield from halving(send, keep, orders[1], stages - 1, stages, None)
+    acc = keep + recv.astype(jnp.float32)
+    low, high = jnp.split(acc, 2, axis=1)
+    mine, send = jnp.where(first_core, low, high), jnp.where(first_core, high, low)
+    got = swap_cores(send)
     done = yield send
-    theirs = after(theirs, done)
-    return jnp.where(core == 0, jnp.stack([mine, theirs]), jnp.stack([theirs, mine]))
+    got = after(got, done)
+    send = jnp.where(owner, got, mine).astype(wire_type(stages - 1, stages))
+    recv = swap(send, stages - 1)
+    done = yield send
+    result = (jnp.where(owner, mine, got) + after(recv, done).astype(jnp.float32)).astype(jnp.bfloat16)
+    return result.reshape(2, result.shape[0] // 2, -1)
 
 
 def local(tokens, gate_up, down_weight):
@@ -272,14 +305,20 @@
     each = tokens.shape[1]
     depth = gate_up.shape[1]
 
-    mine = lax.dynamic_index_in_dim(tokens, core, 0, False)
-    theirs = swap_cores(lax.dynamic_index_in_dim(tokens, 1 - core, 0, False))
-    other = swap_cores(after(gate_up, theirs))
-    down_other = swap_cores(after(down_weight, theirs))
-    rows = jnp.where(core == 0, jnp.stack([mine, theirs]), jnp.stack([theirs, mine]))
-    rows = rows.reshape(2, each, count_x // 2, 2 * depth).transpose(0, 2, 1, 3)
-    rows = rows.reshape(count_x, each, 2 * depth)
-    rows = lax.all_to_all(rows, "gx", 0, 0).reshape(count_x * each, 2 * depth)
+    half = count_x // 2
+    other = swap_cores(gate_up)
+    flags = core == 0, core == chip // half
+    tokens, spot, *flags = lax.optimization_barrier((tokens, spot, *flags))
+    dealt = deal(spot, tokens.reshape(2 * each, -1), half)
+    arrived = [
+        move(message, [((i, j), (j * half + (i + turn) % half, i // half)) for i in range(count_x) for j in range(2)])
+        for turn, message in enumerate(dealt)
+    ]
+    down_other = swap_cores(after(down_weight, arrived))
+    if 2 * each % 16:
+        twice = jnp.stack(arrived[::-1] * 2)
+        arrived = lax.dynamic_slice_in_dim(twice, half - 1 - lax.rem(chip, half), half)
+        arrived = [arrived.reshape(half * 2 * each, -1)]
 
     if stages == 3 and each == 24:
         step, orders, turns = 8, ORDERS, TURNS
@@ -287,10 +326,10 @@
         step, orders = each, [((0, 1), (0, 1))]
         turns = [0] * (2 * stages + 2)
     cuts = tuple((i * step, (i + 1) * step, order[0]) for i, order in enumerate(orders))
-    parts = project(spot, rows, gate_up, other, count_x, cuts, stages)
+    parts = project(spot, arrived, gate_up, other, count_x, cuts, stages)
     chunks = [
         chunk_steps(
-            spot, parts[2 * i : 2 * i + 2], (down_weight, down_other), count_x * step, order, count_x, stages
+            spot, flags, parts[2 * i : 2 * i + 2], (down_weight, down_other), count_x * step, order, count_x, stages
         )
         for i, order in enumerate(orders)
     ]

time: 127 us -> 119 us (0.937); the launches traced: 125 us -> 119 us
  waiting for transfers between devices: 63.6 us -> 54.1 us
  starting transfers between devices: 32.6 us -> 41.2 us
  local copies, waits for them, and re-layouts: 5.46 us -> 1.27 us
  other arithmetic: 3.81 us -> 2.16 us
    all_to_all x1 -> x0, waiting for transfers between devices: 12.2 us -> none  [local(): rows = lax.all_to_all(rows, 'gx', 0, 0).reshape(count_x * each, 2 * depth)]
    all_to_all x1 -> x0, starting transfers between devices: 6.95 us -> none  [local(): rows = lax.all_to_all(rows, 'gx', 0, 0).reshape(count_x * each, 2 * depth)]
    ppermute x6 -> x5, starting transfers between devices: 1.41 us -> 7.92 us  [swap_cores(): return lax.ppermute(value, 'gy', [(0, 1), (1, 0)])]
    ppermute x0 -> x4, starting transfers between devices: none -> 6.22 us  [move(): lax.ppermute(value, ('gx', 'gy'), [(2 * a + b, 2 * c + d) for (a, b), (c,...]
    ppermute x0 -> x4, waiting for transfers between devices: none -> 3.74 us  [move(): lax.ppermute(value, ('gx', 'gy'), [(2 * a + b, 2 * c + d) for (a, b), (c,...]
    ppermute x18, starting transfers between devices: 24.2 us -> 27 us  [swap(): return lax.ppermute(value, 'gx', [(i, i ^ 1 << bit) for i in range(count)])]
    ppermute x6 -> x5, waiting for transfers between devices: 2.3 us -> 0.01 us  [swap_cores(): return lax.ppermute(value, 'gy', [(0, 1), (1, 0)])]
    unnamed x6 -> x4, local copies, waits for them, and re-layouts: 3.24 us -> 1 us
  transfers between devices with their start and end apart: 25 -> 27, of which waited for: 16 -> 14; matrix products, arithmetic and copies ran while one was open for 3% -> 1% of each run, Pallas kernels for 15% -> 16%
where the time goes in v2:
time: 119 us
  waiting for transfers between devices  54.1 us (45%)
  starting transfers between devices  41.2 us (35%)
  Pallas kernels  19.5 us (16%)
  other arithmetic  2.16 us (2%)
  local copies, waits for them, and re-layouts  1.27 us (1%)
    ppermute x18, waiting for transfers between devices, swap(): return lax.ppermute(value, 'gx', [(i, i ^ 1 << bit) for i in range(count)])  50.4 us
    ppermute x18, starting transfers between devices, swap(): return lax.ppermute(value, 'gx', [(i, i ^ 1 << bit) for i in range(count)])  27 us
    pallas_call x1, Pallas kernels, project(): pl.pallas_call(functools.partial(project_kernel, block, cuts, len(arrived...  9.58 us
    pallas_call x3, Pallas kernels, down_project(): pl.pallas_call(functools.partial(down_kernel, block, count, order), out_s...  9.33 us
    ppermute x5, starting transfers between devices, swap_cores(): return lax.ppermute(value, 'gy', [(0, 1), (1, 0)])  7.92 us
    ppermute x4, starting transfers between devices, move(): lax.ppermute(value, ('gx', 'gy'), [(2 * a + b, 2 * c + d) for (a, b), (c,...  6.22 us
    ppermute x4, waiting for transfers between devices, move(): lax.ppermute(value, ('gx', 'gy'), [(2 * a + b, 2 * c + d) for (a, b), (c,...  3.74 us
  transfers between devices with their start and end apart: 27, of which 14 were waited for; matrix products, arithmetic and copies ran while one was open for 1% of the time, Pallas kernels for 16%

profile of v2, /device:TPU:0, one launch (start us, length us, event | category | flops | bytes accessed | tf_op | source)
XLA Modules:
  0.0 118.5 jit_solution(8106280182360080718)
XLA Ops:
  0.0 0.5 collective-permute-start.4
  0.5 0.1 pad_add_fusion.place_ref
  0.5 1.0 copy-done.1
  1.5 0.6 shard_map.37
  2.1 0.7 collective-permute-start
  2.8 2.5 %collective-permute-start.1 = (bf16[48,1024]{1,0:T(8,128)(2,1)S(1)}, bf16[48,1024]{1,0:T(8,128)(2,1)S(1)}, u32[]{:S(2)}, u32[]{:S(2)}) collective-permute-start(bf16[48,1024]{1,0:T(8,128)(2,1)S(1)} %get-tuple-element.54), channel_id=1, source_target_pairs={{0,2},{1,10},{2,4},{3,12},{4,6},{5,14},{6,0},{7,8},{8,3},{9,11},{1... | collective-permute-start | bytes 294920 | tf_op jit(solution)/shard_map/ppermute | solution.py:278
  5.3 1.6 %collective-permute-start.2 = (bf16[48,1024]{1,0:T(8,128)(2,1)S(1)}, bf16[48,1024]{1,0:T(8,128)(2,1)S(1)}, u32[]{:S(2)}, u32[]{:S(2)}) collective-permute-start(bf16[48,1024]{1,0:T(8,128)(2,1)S(1)} %get-tuple-element.55), channel_id=1, source_target_pairs={{0,4},{1,12},{2,6},{3,14},{4,0},{5,8},{6,2},{7,10},{8,5},{9,13},{1... | collective-permute-start | bytes 294920 | tf_op jit(solution)/shard_map/ppermute | solution.py:278
  6.9 1.4 %collective-permute-start.3 = (bf16[48,1024]{1,0:T(8,128)(2,1)S(1)}, bf16[48,1024]{1,0:T(8,128)(2,1)S(1)}, u32[]{:S(2)}, u32[]{:S(2)}) collective-permute-start(bf16[48,1024]{1,0:T(8,128)(2,1)S(1)} %get-tuple-element.56), channel_id=1, source_target_pairs={{0,6},{1,14},{2,0},{3,8},{4,2},{5,10},{6,4},{7,12},{8,7},{9,15},{1... | collective-permute-start | bytes 294920 | tf_op jit(solution)/shard_map/ppermute | solution.py:278
  8.3 0.6 collective-permute-done.1.refs_1_
  8.9 2.1 %collective-permute-done.2.refs_2_ = bf16[48,1024]{1,0:T(8,128)(2,1)S(1)} collective-permute-done((bf16[48,1024]{1,0:T(8,128)(2,1)S(1)}, bf16[48,1024]{1,0:T(8,128)(2,1)S(1)}, u32[]{:S(2)}, u32[]{:S(2)}) %collective-permute-start.2) | collective-permute-done | bytes 98336 | tf_op jit(solution)/shard_map/ppermute | solution.py:278
  11.0 1.1 collective-permute-done.3.refs_3_
  12.1 7.3 %collective-permute-start.10 = (bf16[208,8192]{1,0:T(8,128)(2,1)}, bf16[208,8192]{1,0:T(8,128)(2,1)S(1)}, u32[]{:S(2)}, u32[]{:S(2)}) collective-permute-start(bf16[208,8192]{1,0:T(8,128)(2,1)} %own.5), channel_id=1, source_target_pairs={{0,1},{1,0},{2,3},{3,2},{4,5},{5,4},{6,7},{7,6},{8,9},{9,8},{10,11... | collective-permute-start | bytes 10223624 | tf_op jit(solution)/shard_map/ppermute | solution.py:254
  19.3 0.0 collective-permute-done.4.refs_5_
  19.3 9.6 %shard_map.38 = (bf16[2,2,2,208,128]{4,3,2,1,0:T(8,128)(2,1)S(1)}, f32[2,2,2,208,128]{4,3,2,1,0:T(8,128)S(1)}, bf16[2,2,2,208,128]{4,3,2,1,0:T(8,128)(2,1)S(1)},...) custom-call(s32[2]{0:T(128)S(1)} %pad_add_fusion.place_ref, ...), custom_call_target="tpu_custom_call" | custom-call | flops 1308622848 | bytes 6815744 | tf_op jit(solution)/shard_map/pallas_call | solution.py:152
  28.9 0.0 copy-start
  28.9 0.3 collective-permute-start.5
  29.3 1.3 %collective-permute-start.8 = (bf16[2,2,2,208,128]{4,3,2,1,0:T(8,128)(2,1)S(1)}, bf16[2,2,2,208,128]{4,3,2,1,0:T(8,128)(2,1)S(1)}, u32[]{:S(2)}, u32[]{:S(2)}) collective-permute-start(bf16[2,2,2,208,128]{4,3,2,1,0:T(8,128)(2,1)S(1)} %get-tuple-element.64), channel_id=1, source_target_pairs={{0,4},{2,6},{4,0},{6,2},{8,12},{10,14},{12,8},{14,10},{1,5},{3,7},... | collective-permute-start | bytes 1277960 | tf_op jit(solution)/shard_map/ppermute | solution.py:250
  30.6 10.1 %collective-permute-done.5 = bf16[2,2,2,208,128]{4,3,2,1,0:T(8,128)(2,1)S(1)} collective-permute-done((bf16[2,2,2,208,128]{4,3,2,1,0:T(8,128)(2,1)S(1)}, bf16[2,2,2,208,128]{4,3,2,1,0:T(8,128)(2,1)S(1)}, u32[]{:S(2)}, u32[]{:S(2)}) %collective-permute-start.5) | collective-permute-done | bytes 426016 | tf_op jit(solution)/shard_map/ppermute | solution.py:250
  40.7 0.1 convert_add_fusion.5
  40.9 0.1 collective-permute-start.6
  41.0 0.1 convert_add_fusion.4
  41.1 1.6 %collective-permute-start.9 = (bf16[2,2,208,128]{3,2,1,0:T(8,128)(2,1)S(1)}, bf16[2,2,208,128]{3,2,1,0:T(8,128)(2,1)S(1)}, u32[]{:S(2)}, u32[]{:S(2)}) collective-permute-start(bf16[2,2,208,128]{3,2,1,0:T(8,128)(2,1)S(1)} %fusion.10), channel_id=1, source_target_pairs={{0,2},{2,0},{4,6},{6,4},{8,10},{10,8},{12,14},{14,12},{1,3},{3,1},... | collective-permute-start | bytes 638984 | tf_op jit(solution)/shard_map/ppermute | solution.py:250
  42.7 0.5 collective-permute-start.12
  43.2 4.1 %collective-permute-done.6 = bf16[2,2,208,128]{3,2,1,0:T(8,128)(2,1)S(1)} collective-permute-done((bf16[2,2,208,128]{3,2,1,0:T(8,128)(2,1)S(1)}, bf16[2,2,208,128]{3,2,1,0:T(8,128)(2,1)S(1)}, u32[]{:S(2)}, u32[]{:S(2)}) %collective-permute-start.6) | collective-permute-done | bytes 213024 | tf_op jit(solution)/shard_map/ppermute | solution.py:250
  47.3 2.4 %collective-permute-start.7 = (bf16[1,2,208,128]{3,2,1,0:T(8,128)(2,1)S(1)}, bf16[1,2,208,128]{3,2,1,0:T(8,128)(2,1)S(1)}, u32[]{:S(2)}, u32[]{:S(2)}) collective-permute-start(bf16[1,2,208,128]{3,2,1,0:T(8,128)(2,1)S(1)} %slice.143), channel_id=1, source_target_pairs={{0,8},{2,10},{4,12},{6,14},{8,0},{10,2},{12,4},{14,6},{1,9},{3,11}... | collective-permute-start | bytes 319496 | tf_op jit(solution)/shard_map/ppermute | solution.py:250
  49.9 3.2 %collective-permute-start.14 = (bf16[1,2,208,128]{3,2,1,0:T(8,128)(2,1)S(1)}, bf16[1,2,208,128]{3,2,1,0:T(8,128)(2,1)S(1)}, u32[]{:S(2)}, u32[]{:S(2)}) collective-permute-start(bf16[1,2,208,128]{3,2,1,0:T(8,128)(2,1)S(1)} %slice.142), channel_id=1, source_target_pairs={{0,8},{2,10},{4,12},{6,14},{8,0},{10,2},{12,4},{14,6},{1,9},{3,11}... | collective-permute-start | bytes 319496 | tf_op jit(solution)/shard_map/ppermute | solution.py:250
  53.0 4.5 %collective-permute-done.7 = bf16[1,2,208,128]{3,2,1,0:T(8,128)(2,1)S(1)} collective-permute-done((bf16[1,2,208,128]{3,2,1,0:T(8,128)(2,1)S(1)}, bf16[1,2,208,128]{3,2,1,0:T(8,128)(2,1)S(1)}, u32[]{:S(2)}, u32[]{:S(2)}) %collective-permute-start.7) | collective-permute-done | bytes 106528 | tf_op jit(solution)/shard_map/ppermute | solution.py:250
  57.5 3.1 %shard_map.39 = (bf16[2,1,16,8192]{3,2,1,0:T(8,128)(2,1)S(1)}, f32[2,1,16,8192]{3,2,1,0:T(8,128)S(1)}) custom-call(s32[2]{0:T(128)S(1)} %pad_add_fusion.place_ref, f32[2,208,128]{2,1,0:T(8,128)S(1)} %slice_bitcast_fusion.8.keep_in, bf16[2,208,128]{2,1,0:T(8,128)(2,1)S(1)} %bitcast.65, bf16[208,8192]{1,0:T(8,128)(2,1)S(1)} %copy-done, ...), custom_call_target="tpu_custom_call" | custom-call | flops 436207616 | bytes 6815744 | tf_op jit(solution)/shard_map/pallas_call | solution.py:221
  60.6 0.0 collective-permute-done.12
  60.7 0.1 convert_add_fusion.3
  60.8 0.1 collective-permute-start.13
  60.9 0.5 collective-permute-start.11
  61.4 3.1 %shard_map.40 = (bf16[2,1,16,8192]{3,2,1,0:T(8,128)(2,1)S(1)}, f32[2,1,16,8192]{3,2,1,0:T(8,128)S(1)}) custom-call(s32[2]{0:T(128)S(1)} %pad_add_fusion.place_ref, f32[2,208,128]{2,1,0:T(8,128)S(1)} %slice_bitcast_fusion.7.keep_in, bf16[2,208,128]{2,1,0:T(8,128)(2,1)S(1)} %bitcast.64, bf16[208,8192]{1,0:T(8,128)(2,1)S(1)} %copy-done, ...), custom_call_target="tpu_custom_call" | custom-call | flops 436207616 | bytes 6815744 | tf_op jit(solution)/shard_map/pallas_call | solution.py:221
  64.5 2.1 %collective-permute-start.16 = (bf16[2,1,16,8192]{3,2,1,0:T(8,128)(2,1)S(1)}, bf16[2,1,16,8192]{3,2,1,0:T(8,128)(2,1)S(1)}, u32[]{:S(2)}, u32[]{:S(2)}) collective-permute-start(bf16[2,1,16,8192]{3,2,1,0:T(8,128)(2,1)S(1)} %get-tuple-element.75), channel_id=1, source_target_pairs={{0,4},{2,6},{4,0},{6,2},{8,12},{10,14},{12,8},{14,10},{1,5},{3,7},... | collective-permute-start | bytes 1572872 | tf_op jit(solution)/shard_map/ppermute | solution.py:250
  66.6 0.6 collective-permute-done.13
  67.2 2.6 %collective-permute-start.17 = (bf16[1,2,208,128]{3,2,1,0:T(8,128)(2,1)S(1)}, bf16[1,2,208,128]{3,2,1,0:T(8,128)(2,1)S(1)}, u32[]{:S(2)}, u32[]{:S(2)}) collective-permute-start(bf16[1,2,208,128]{3,2,1,0:T(8,128)(2,1)S(1)} %slice.141), channel_id=1, source_target_pairs={{0,8},{2,10},{4,12},{6,14},{8,0},{10,2},{12,4},{14,6},{1,9},{3,11}... | collective-permute-start | bytes 319496 | tf_op jit(solution)/shard_map/ppermute | solution.py:250
  69.9 3.1 %collective-permute-done.11 = bf16[2,1,16,8192]{3,2,1,0:T(8,128)(2,1)S(1)} collective-permute-done((bf16[2,1,16,8192]{3,2,1,0:T(8,128)(2,1)S(1)}, bf16[2,1,16,8192]{3,2,1,0:T(8,128)(2,1)S(1)}, u32[]{:S(2)}, u32[]{:S(2)}) %collective-permute-start.11) | collective-permute-done | bytes 524320 | tf_op jit(solution)/shard_map/ppermute | solution.py:250
  72.9 0.1 convert_add_fusion.2
  73.1 0.4 collective-permute-start.15
  73.5 7.1 %collective-permute-done.17 = bf16[1,2,208,128]{3,2,1,0:T(8,128)(2,1)S(1)} collective-permute-done((bf16[1,2,208,128]{3,2,1,0:T(8,128)(2,1)S(1)}, bf16[1,2,208,128]{3,2,1,0:T(8,128)(2,1)S(1)}, u32[]{:S(2)}, u32[]{:S(2)}) %collective-permute-start.17) | collective-permute-done | bytes 106528 | tf_op jit(solution)/shard_map/ppermute | solution.py:250
  80.5 3.1 %shard_map.41 = (bf16[2,1,16,8192]{3,2,1,0:T(8,128)(2,1)S(1)}, f32[2,1,16,8192]{3,2,1,0:T(8,128)S(1)}) custom-call(s32[2]{0:T(128)S(1)} %pad_add_fusion.place_ref, f32[2,208,128]{2,1,0:T(8,128)S(1)} %slice_bitcast_fusion.6.keep_in, bf16[2,208,128]{2,1,0:T(8,128)(2,1)S(1)} %bitcast.66, bf16[208,8192]{1,0:T(8,128)(2,1)S(1)} %copy-done, ...), custom_call_target="tpu_custom_call" | custom-call | flops 436207616 | bytes 6815744 | tf_op jit(solution)/shard_map/pallas_call | solution.py:221
  83.7 4.6 %collective-permute-start.22 = (bf16[2,1,16,8192]{3,2,1,0:T(8,128)(2,1)S(1)}, bf16[2,1,16,8192]{3,2,1,0:T(8,128)(2,1)S(1)}, u32[]{:S(2)}, u32[]{:S(2)}) collective-permute-start(bf16[2,1,16,8192]{3,2,1,0:T(8,128)(2,1)S(1)} %get-tuple-element.80), channel_id=1, source_target_pairs={{0,4},{2,6},{4,0},{6,2},{8,12},{10,14},{12,8},{14,10},{1,5},{3,7},... | collective-permute-start | bytes 1572872 | tf_op jit(solution)/shard_map/ppermute | solution.py:250
  88.3 0.1 convert_add_fusion.1
  88.4 1.6 %collective-permute-start.19 = (bf16[1,16,8192]{2,1,0:T(8,128)(2,1)S(1)}, bf16[1,16,8192]{2,1,0:T(8,128)(2,1)S(1)}, u32[]{:S(2)}, u32[]{:S(2)}) collective-permute-start(bf16[1,16,8192]{2,1,0:T(8,128)(2,1)S(1)} %fusion.7), channel_id=1, source_target_pairs={{0,2},{2,0},{4,6},{6,4},{8,10},{10,8},{12,14},{14,12},{1,3},{3,1},... | collective-permute-start | bytes 786440 | tf_op jit(solution)/shard_map/ppermute | solution.py:250
  90.0 0.1 fusion.2
  90.1 0.1 collective-permute-start.18
  90.2 4.7 %collective-permute-done.19 = bf16[1,16,8192]{2,1,0:T(8,128)(2,1)S(1)} collective-permute-done((bf16[1,16,8192]{2,1,0:T(8,128)(2,1)S(1)}, bf16[1,16,8192]{2,1,0:T(8,128)(2,1)S(1)}, u32[]{:S(2)}, u32[]{:S(2)}) %collective-permute-start.19) | collective-permute-done | bytes 262176 | tf_op jit(solution)/shard_map/ppermute | solution.py:250
  94.9 0.1 fusion.1
  94.9 0.1 collective-permute-start.21
  95.0 0.1 select_convert_fusion.2
  95.1 0.1 collective-permute-start.20
  95.2 1.9 %collective-permute-done.22 = bf16[2,1,16,8192]{3,2,1,0:T(8,128)(2,1)S(1)} collective-permute-done((bf16[2,1,16,8192]{3,2,1,0:T(8,128)(2,1)S(1)}, bf16[2,1,16,8192]{3,2,1,0:T(8,128)(2,1)S(1)}, u32[]{:S(2)}, u32[]{:S(2)}) %collective-permute-start.22) | collective-permute-done | bytes 524320 | tf_op jit(solution)/shard_map/ppermute | solution.py:250
  97.1 0.1 convert_add_fusion
  97.2 1.1 collective-permute-start.24
  98.4 4.5 %collective-permute-start.23 = (bf16[16,4096]{1,0:T(8,128)(2,1)S(1)}, bf16[16,4096]{1,0:T(8,128)(2,1)S(1)}, u32[]{:S(2)}, u32[]{:S(2)}) collective-permute-start(bf16[16,4096]{1,0:T(8,128)(2,1)S(1)} %select_convert_fusion.1), channel_id=1, source_target_pairs={{0,8},{2,10},{4,12},{6,14},{8,0},{10,2},{12,4},{14,6},{1,9},{3,11}... | collective-permute-start | bytes 393224 | tf_op jit(solution)/shard_map/ppermute | solution.py:250
  102.9 4.7 %collective-permute-done.20 = bf16[16,4096]{1,0:T(8,128)(2,1)S(1)} collective-permute-done((bf16[16,4096]{1,0:T(8,128)(2,1)S(1)}, bf16[16,4096]{1,0:T(8,128)(2,1)S(1)}, u32[]{:S(2)}, u32[]{:S(2)}) %collective-permute-start.20) | collective-permute-done | bytes 131104 | tf_op jit(solution)/shard_map/ppermute | solution.py:250
  107.7 0.1 collective-permute-start.25
  107.7 0.1 fusion.12
  107.8 2.3 %collective-permute-done.23 = bf16[16,4096]{1,0:T(8,128)(2,1)S(1)} collective-permute-done((bf16[16,4096]{1,0:T(8,128)(2,1)S(1)}, bf16[16,4096]{1,0:T(8,128)(2,1)S(1)}, u32[]{:S(2)}, u32[]{:S(2)}) %collective-permute-start.23) | collective-permute-done | bytes 131104 | tf_op jit(solution)/shard_map/ppermute | solution.py:250
  110.2 0.1 collective-permute-start.26
  110.3 0.1 fusion.13
  110.3 7.4 %collective-permute-done.26 = bf16[16,4096]{1,0:T(8,128)(2,1)S(1)} collective-permute-done((bf16[16,4096]{1,0:T(8,128)(2,1)S(1)}, bf16[16,4096]{1,0:T(8,128)(2,1)S(1)}, u32[]{:S(2)}, u32[]{:S(2)}) %collective-permute-start.26) | collective-permute-done | bytes 131104 | tf_op jit(solution)/shard_map/ppermute | solution.py:250
  117.7 0.1 fusion.14
  117.8 0.8 pad_maximum_fusion
  (34 shorter events, 0.6 us)
Async XLA Ops:
  0.0 19.3 %collective-permute-start.4 = (bf16[2,512,3328]{2,1,0:T(8,128)(2,1)}, bf16[2,512,3328]{2,1,0:T(8,128)(2,1)}, u32[]{:S(2)}, u32[]{:S(2)}) collective-permute-start(bf16[2,512,3328]{2,1,0:T(8,128)(2,1)} %refs_4_.1), channel_id=1, source_target_pairs={{0,1},{1,0},{2,3},{3,2},{4,5},{5,4},{6,7},{7,6},{8,9},{9,8},{10,11... | collective-permute-start | bytes 20447240 | tf_op jit(solution)/shard_map/ppermute | solution.py:254
  0.5 1.0 copy-start.1
  2.1 6.2 %collective-permute-start = (bf16[48,1024]{1,0:T(8,128)(2,1)S(1)}, bf16[48,1024]{1,0:T(8,128)(2,1)S(1)}, u32[]{:S(2)}, u32[]{:S(2)}) collective-permute-start(bf16[48,1024]{1,0:T(8,128)(2,1)S(1)} %get-tuple-element.53), channel_id=1, source_target_pairs={{0,0},{1,8},{2,2},{3,10},{4,4},{5,12},{6,6},{7,14},{8,1},{9,9},{10... | collective-permute-start | bytes 294920 | tf_op jit(solution)/shard_map/ppermute | solution.py:278
  2.8 6.2 %collective-permute-start.1 = (bf16[48,1024]{1,0:T(8,128)(2,1)S(1)}, bf16[48,1024]{1,0:T(8,128)(2,1)S(1)}, u32[]{:S(2)}, u32[]{:S(2)}) collective-permute-start(bf16[48,1024]{1,0:T(8,128)(2,1)S(1)} %get-tuple-element.54), channel_id=1, source_target_pairs={{0,2},{1,10},{2,4},{3,12},{4,6},{5,14},{6,0},{7,8},{8,3},{9,11},{1... | collective-permute-start | bytes 294920 | tf_op jit(solution)/shard_map/ppermute | solution.py:278
  5.3 5.7 %collective-permute-start.2 = (bf16[48,1024]{1,0:T(8,128)(2,1)S(1)}, bf16[48,1024]{1,0:T(8,128)(2,1)S(1)}, u32[]{:S(2)}, u32[]{:S(2)}) collective-permute-start(bf16[48,1024]{1,0:T(8,128)(2,1)S(1)} %get-tuple-element.55), channel_id=1, source_target_pairs={{0,4},{1,12},{2,6},{3,14},{4,0},{5,8},{6,2},{7,10},{8,5},{9,13},{1... | collective-permute-start | bytes 294920 | tf_op jit(solution)/shard_map/ppermute | solution.py:278
  6.9 5.2 %collective-permute-start.3 = (bf16[48,1024]{1,0:T(8,128)(2,1)S(1)}, bf16[48,1024]{1,0:T(8,128)(2,1)S(1)}, u32[]{:S(2)}, u32[]{:S(2)}) collective-permute-start(bf16[48,1024]{1,0:T(8,128)(2,1)S(1)} %get-tuple-element.56), channel_id=1, source_target_pairs={{0,6},{1,14},{2,0},{3,8},{4,2},{5,10},{6,4},{7,12},{8,7},{9,15},{1... | collective-permute-start | bytes 294920 | tf_op jit(solution)/shard_map/ppermute | solution.py:278
  12.1 45.4 %collective-permute-start.10 = (bf16[208,8192]{1,0:T(8,128)(2,1)}, bf16[208,8192]{1,0:T(8,128)(2,1)S(1)}, u32[]{:S(2)}, u32[]{:S(2)}) collective-permute-start(bf16[208,8192]{1,0:T(8,128)(2,1)} %own.5), channel_id=1, source_target_pairs={{0,1},{1,0},{2,3},{3,2},{4,5},{5,4},{6,7},{7,6},{8,9},{9,8},{10,11... | collective-permute-start | bytes 10223624 | tf_op jit(solution)/shard_map/ppermute | solution.py:254
  28.9 28.6 %copy-start = (bf16[208,8192]{1,0:T(8,128)(2,1)S(1)}, bf16[208,8192]{1,0:T(8,128)(2,1)}, u32[]{:S(2)}) copy-start(bf16[208,8192]{1,0:T(8,128)(2,1)} %own.5) | copy-start | bytes 10223620
  28.9 11.8 %collective-permute-start.5 = (bf16[2,2,2,208,128]{4,3,2,1,0:T(8,128)(2,1)S(1)}, bf16[2,2,2,208,128]{4,3,2,1,0:T(8,128)(2,1)S(1)}, u32[]{:S(2)}, u32[]{:S(2)}) collective-permute-start(bf16[2,2,2,208,128]{4,3,2,1,0:T(8,128)(2,1)S(1)} %get-tuple-element.58), channel_id=1, source_target_pairs={{0,2},{2,0},{4,6},{6,4},{8,10},{10,8},{12,14},{14,12},{1,3},{3,1},... | collective-permute-start | bytes 1277960 | tf_op jit(solution)/shard_map/ppermute | solution.py:250
  29.3 11.7 %collective-permute-start.8 = (bf16[2,2,2,208,128]{4,3,2,1,0:T(8,128)(2,1)S(1)}, bf16[2,2,2,208,128]{4,3,2,1,0:T(8,128)(2,1)S(1)}, u32[]{:S(2)}, u32[]{:S(2)}) collective-permute-start(bf16[2,2,2,208,128]{4,3,2,1,0:T(8,128)(2,1)S(1)} %get-tuple-element.64), channel_id=1, source_target_pairs={{0,4},{2,6},{4,0},{6,2},{8,12},{10,14},{12,8},{14,10},{1,5},{3,7},... | collective-permute-start | bytes 1277960 | tf_op jit(solution)/shard_map/ppermute | solution.py:250
  40.9 6.4 %collective-permute-start.6 = (bf16[2,2,208,128]{3,2,1,0:T(8,128)(2,1)S(1)}, bf16[2,2,208,128]{3,2,1,0:T(8,128)(2,1)S(1)}, u32[]{:S(2)}, u32[]{:S(2)}) collective-permute-start(bf16[2,2,208,128]{3,2,1,0:T(8,128)(2,1)S(1)} %fusion.9), channel_id=1, source_target_pairs={{0,4},{2,6},{4,0},{6,2},{8,12},{10,14},{12,8},{14,10},{1,5},{3,7},... | collective-permute-start | bytes 638984 | tf_op jit(solution)/shard_map/ppermute | solution.py:250
  41.1 8.7 %collective-permute-start.9 = (bf16[2,2,208,128]{3,2,1,0:T(8,128)(2,1)S(1)}, bf16[2,2,208,128]{3,2,1,0:T(8,128)(2,1)S(1)}, u32[]{:S(2)}, u32[]{:S(2)}) collective-permute-start(bf16[2,2,208,128]{3,2,1,0:T(8,128)(2,1)S(1)} %fusion.10), channel_id=1, source_target_pairs={{0,2},{2,0},{4,6},{6,4},{8,10},{10,8},{12,14},{14,12},{1,3},{3,1},... | collective-permute-start | bytes 638984 | tf_op jit(solution)/shard_map/ppermute | solution.py:250
  42.7 17.9 %collective-permute-start.12 = (bf16[2,2,2,208,128]{4,3,2,1,0:T(8,128)(2,1)S(1)}, bf16[2,2,2,208,128]{4,3,2,1,0:T(8,128)(2,1)S(1)}, u32[]{:S(2)}, u32[]{:S(2)}) collective-permute-start(bf16[2,2,2,208,128]{4,3,2,1,0:T(8,128)(2,1)S(1)} %get-tuple-element.72), channel_id=1, source_target_pairs={{0,2},{2,0},{4,6},{6,4},{8,10},{10,8},{12,14},{14,12},{1,3},{3,1},... | collective-permute-start | bytes 1277960 | tf_op jit(solution)/shard_map/ppermute | solution.py:250
  47.3 10.2 %collective-permute-start.7 = (bf16[1,2,208,128]{3,2,1,0:T(8,128)(2,1)S(1)}, bf16[1,2,208,128]{3,2,1,0:T(8,128)(2,1)S(1)}, u32[]{:S(2)}, u32[]{:S(2)}) collective-permute-start(bf16[1,2,208,128]{3,2,1,0:T(8,128)(2,1)S(1)} %slice.143), channel_id=1, source_target_pairs={{0,8},{2,10},{4,12},{6,14},{8,0},{10,2},{12,4},{14,6},{1,9},{3,11}... | collective-permute-start | bytes 319496 | tf_op jit(solution)/shard_map/ppermute | solution.py:250
  49.9 11.6 %collective-permute-start.14 = (bf16[1,2,208,128]{3,2,1,0:T(8,128)(2,1)S(1)}, bf16[1,2,208,128]{3,2,1,0:T(8,128)(2,1)S(1)}, u32[]{:S(2)}, u32[]{:S(2)}) collective-permute-start(bf16[1,2,208,128]{3,2,1,0:T(8,128)(2,1)S(1)} %slice.142), channel_id=1, source_target_pairs={{0,8},{2,10},{4,12},{6,14},{8,0},{10,2},{12,4},{14,6},{1,9},{3,11}... | collective-permute-start | bytes 319496 | tf_op jit(solution)/shard_map/ppermute | solution.py:250
  60.8 6.4 %collective-permute-start.13 = (bf16[2,2,208,128]{3,2,1,0:T(8,128)(2,1)S(1)}, bf16[2,2,208,128]{3,2,1,0:T(8,128)(2,1)S(1)}, u32[]{:S(2)}, u32[]{:S(2)}) collective-permute-start(bf16[2,2,208,128]{3,2,1,0:T(8,128)(2,1)S(1)} %fusion.11), channel_id=1, source_target_pairs={{0,4},{2,6},{4,0},{6,2},{8,12},{10,14},{12,8},{14,10},{1,5},{3,7},... | collective-permute-start | bytes 638984 | tf_op jit(solution)/shard_map/ppermute | solution.py:250
  60.9 12.1 %collective-permute-start.11 = (bf16[2,1,16,8192]{3,2,1,0:T(8,128)(2,1)S(1)}, bf16[2,1,16,8192]{3,2,1,0:T(8,128)(2,1)S(1)}, u32[]{:S(2)}, u32[]{:S(2)}) collective-permute-start(bf16[2,1,16,8192]{3,2,1,0:T(8,128)(2,1)S(1)} %get-tuple-element.70), channel_id=1, source_target_pairs={{0,2},{2,0},{4,6},{6,4},{8,10},{10,8},{12,14},{14,12},{1,3},{3,1},... | collective-permute-start | bytes 1572872 | tf_op jit(solution)/shard_map/ppermute | solution.py:250
  64.5 23.7 %collective-permute-start.16 = (bf16[2,1,16,8192]{3,2,1,0:T(8,128)(2,1)S(1)}, bf16[2,1,16,8192]{3,2,1,0:T(8,128)(2,1)S(1)}, u32[]{:S(2)}, u32[]{:S(2)}) collective-permute-start(bf16[2,1,16,8192]{3,2,1,0:T(8,128)(2,1)S(1)} %get-tuple-element.75), channel_id=1, source_target_pairs={{0,4},{2,6},{4,0},{6,2},{8,12},{10,14},{12,8},{14,10},{1,5},{3,7},... | collective-permute-start | bytes 1572872 | tf_op jit(solution)/shard_map/ppermute | solution.py:250
  67.2 13.3 %collective-permute-start.17 = (bf16[1,2,208,128]{3,2,1,0:T(8,128)(2,1)S(1)}, bf16[1,2,208,128]{3,2,1,0:T(8,128)(2,1)S(1)}, u32[]{:S(2)}, u32[]{:S(2)}) collective-permute-start(bf16[1,2,208,128]{3,2,1,0:T(8,128)(2,1)S(1)} %slice.141), channel_id=1, source_target_pairs={{0,8},{2,10},{4,12},{6,14},{8,0},{10,2},{12,4},{14,6},{1,9},{3,11}... | collective-permute-start | bytes 319496 | tf_op jit(solution)/shard_map/ppermute | solution.py:250
  73.1 16.9 %collective-permute-start.15 = (bf16[1,16,8192]{2,1,0:T(8,128)(2,1)S(1)}, bf16[1,16,8192]{2,1,0:T(8,128)(2,1)S(1)}, u32[]{:S(2)}, u32[]{:S(2)}) collective-permute-start(bf16[1,16,8192]{2,1,0:T(8,128)(2,1)S(1)} %fusion.6), channel_id=1, source_target_pairs={{0,4},{2,6},{4,0},{6,2},{8,12},{10,14},{12,8},{14,10},{1,5},{3,7},... | collective-permute-start | bytes 786440 | tf_op jit(solution)/shard_map/ppermute | solution.py:250
  83.7 13.4 %collective-permute-start.22 = (bf16[2,1,16,8192]{3,2,1,0:T(8,128)(2,1)S(1)}, bf16[2,1,16,8192]{3,2,1,0:T(8,128)(2,1)S(1)}, u32[]{:S(2)}, u32[]{:S(2)}) collective-permute-start(bf16[2,1,16,8192]{3,2,1,0:T(8,128)(2,1)S(1)} %get-tuple-element.80), channel_id=1, source_target_pairs={{0,4},{2,6},{4,0},{6,2},{8,12},{10,14},{12,8},{14,10},{1,5},{3,7},... | collective-permute-start | bytes 1572872 | tf_op jit(solution)/shard_map/ppermute | solution.py:250
  88.4 6.4 %collective-permute-start.19 = (bf16[1,16,8192]{2,1,0:T(8,128)(2,1)S(1)}, bf16[1,16,8192]{2,1,0:T(8,128)(2,1)S(1)}, u32[]{:S(2)}, u32[]{:S(2)}) collective-permute-start(bf16[1,16,8192]{2,1,0:T(8,128)(2,1)S(1)} %fusion.7), channel_id=1, source_target_pairs={{0,2},{2,0},{4,6},{6,4},{8,10},{10,8},{12,14},{14,12},{1,3},{3,1},... | collective-permute-start | bytes 786440 | tf_op jit(solution)/shard_map/ppermute | solution.py:250
  90.1 4.9 %collective-permute-start.18 = (f32[16,4096]{1,0:T(8,128)S(1)}, f32[16,4096]{1,0:T(8,128)S(1)}, u32[]{:S(2)}, u32[]{:S(2)}) collective-permute-start(f32[16,4096]{1,0:T(8,128)S(1)} %slice_select_fusion.4), channel_id=1, source_target_pairs={{0,1},{1,0},{2,3},{3,2},{4,5},{5,4},{6,7},{7,6},{8,9},{9,8},{10,11... | collective-permute-start | bytes 786440 | tf_op jit(solution)/shard_map/ppermute | solution.py:254
  94.9 3.4 %collective-permute-start.21 = (f32[16,4096]{1,0:T(8,128)S(1)}, f32[16,4096]{1,0:T(8,128)S(1)}, u32[]{:S(2)}, u32[]{:S(2)}) collective-permute-start(f32[16,4096]{1,0:T(8,128)S(1)} %slice_select_fusion.3), channel_id=1, source_target_pairs={{0,1},{1,0},{2,3},{3,2},{4,5},{5,4},{6,7},{7,6},{8,9},{9,8},{10,11... | collective-permute-start | bytes 786440 | tf_op jit(solution)/shard_map/ppermute | solution.py:254
  95.1 12.5 %collective-permute-start.20 = (bf16[16,4096]{1,0:T(8,128)(2,1)S(1)}, bf16[16,4096]{1,0:T(8,128)(2,1)S(1)}, u32[]{:S(2)}, u32[]{:S(2)}) collective-permute-start(bf16[16,4096]{1,0:T(8,128)(2,1)S(1)} %select_convert_fusion.2), channel_id=1, source_target_pairs={{0,8},{2,10},{4,12},{6,14},{8,0},{10,2},{12,4},{14,6},{1,9},{3,11}... | collective-permute-start | bytes 393224 | tf_op jit(solution)/shard_map/ppermute | solution.py:250
  97.2 10.3 %collective-permute-start.24 = (bf16[1,16,8192]{2,1,0:T(8,128)(2,1)S(1)}, bf16[1,16,8192]{2,1,0:T(8,128)(2,1)S(1)}, u32[]{:S(2)}, u32[]{:S(2)}) collective-permute-start(bf16[1,16,8192]{2,1,0:T(8,128)(2,1)S(1)} %fusion.8), channel_id=1, source_target_pairs={{0,2},{2,0},{4,6},{6,4},{8,10},{10,8},{12,14},{14,12},{1,3},{3,1},... | collective-permute-start | bytes 786440 | tf_op jit(solution)/shard_map/ppermute | solution.py:250
  98.4 11.8 %collective-permute-start.23 = (bf16[16,4096]{1,0:T(8,128)(2,1)S(1)}, bf16[16,4096]{1,0:T(8,128)(2,1)S(1)}, u32[]{:S(2)}, u32[]{:S(2)}) collective-permute-start(bf16[16,4096]{1,0:T(8,128)(2,1)S(1)} %select_convert_fusion.1), channel_id=1, source_target_pairs={{0,8},{2,10},{4,12},{6,14},{8,0},{10,2},{12,4},{14,6},{1,9},{3,11}... | collective-permute-start | bytes 393224 | tf_op jit(solution)/shard_map/ppermute | solution.py:250
  107.7 2.5 %collective-permute-start.25 = (f32[16,4096]{1,0:T(8,128)S(1)}, f32[16,4096]{1,0:T(8,128)S(1)}, u32[]{:S(2)}, u32[]{:S(2)}) collective-permute-start(f32[16,4096]{1,0:T(8,128)S(1)} %slice_select_fusion.1), channel_id=1, source_target_pairs={{0,1},{1,0},{2,3},{3,2},{4,5},{5,4},{6,7},{7,6},{8,9},{9,8},{10,11... | collective-permute-start | bytes 786440 | tf_op jit(solution)/shard_map/ppermute | solution.py:254
  110.2 7.5 %collective-permute-start.26 = (bf16[16,4096]{1,0:T(8,128)(2,1)S(1)}, bf16[16,4096]{1,0:T(8,128)(2,1)S(1)}, u32[]{:S(2)}, u32[]{:S(2)}) collective-permute-start(bf16[16,4096]{1,0:T(8,128)(2,1)S(1)} %select_convert_fusion), channel_id=1, source_target_pairs={{0,8},{2,10},{4,12},{6,14},{8,0},{10,2},{12,4},{14,6},{1,9},{3,11}... | collective-permute-start | bytes 393224 | tf_op jit(solution)/shard_map/ppermute | solution.py:250

commit v3 on v2

--- a/solution.py
+++ b/solution.py
@@ -11,8 +11,8 @@
 QUAD = 4
 
 
-ORDERS = [((0, 1), (0, 1)), ((1, 0), (1, 0)), ((0, 1), (1, 0))]
-TURNS = [0, 1, 0, 1, 2, 0, 1, 0, 2, 1, 2, 0, 2, 1, 0, 1, 0, 2, 1, 0, 2, 1, 2, 2]
+ORDERS = [(((0, 1),), ((0, 1), (1, 0))), (((1, 0),), ((0, 1), (1, 0))), (((0, 1), (1, 0)), ((0, 1), (1, 0)))]
+TURNS = [0, 1, 0, 1, 2, 0, 1, 2, 0, 2, 1, 0, 2, 1, 0, 1, 0, 2, 1, 0, 2, 1, 2, 2]
 
 
 def wire_type(stage, stages):
@@ -86,43 +86,38 @@
         acc[...] = jnp.dot(first_rows, own[half, :, span], preferred_element_type=jnp.float32) + jnp.dot(
             second_rows, other[half, :, span], preferred_element_type=jnp.float32
         )
-        for index, (first, last, order) in enumerate(cuts):
+        slot = 0
+        for first, last, orders in cuts:
+            split = len(orders) > 1
+            order = orders[half] if split else orders[0]
+            pair = outs[slot + 2 * half * split :][:2]
+            slot += 2 * len(orders)
             count = chips * (last - first)
             part = count // fold
             lane = lax.broadcasted_iota(jnp.int32, (count, LANES), 1)
 
             def tile(at):
-                lanes = slice(at * LANES, (at + 1) * LANES)
+                lanes = pl.ds(pl.multiple_of(at * LANES, LANES), LANES)
                 if count == tokens.shape[0]:
                     return acc[:, lanes]
                 return jnp.concatenate([acc[c * each + first : c * each + last, lanes] for c in range(chips)])
 
-            for q in range(QUAD):
-                base, shift = q * block // LANES, q * block % LANES
+            for near in range(QUAD):
+                q = near ^ (chip & (QUAD - 1))
+                base, shift = q * whole_tiles, q * rest
                 tail = tile(base + whole_tiles)
-                head = tile(base)
-                pieces = [jnp.where(lane < shift, tail, head) if shift else head]
+                pieces = [jnp.where(lane < shift, tail, tile(base))]
                 pieces += [tile(base + t) for t in range(1, whole_tiles)]
                 packed = None
                 for k in range(fold):
-                    value = tail[k * part : (k + 1) * part]
-                    turn = (k * rest - shift) % LANES
-                    if turn:
-                        value = pltpu.roll(value, turn, 1)
+                    turn = lax.rem(k * rest - shift + LANES, LANES)
+                    value = pltpu.roll(tail[k * part : (k + 1) * part], turn, 1)
                     packed = value if k == 0 else jnp.where(lane[:part] < k * rest, packed, value)
                 pieces.append(packed)
                 value = jnp.concatenate(pieces)
-                relative = (QUAD * group + q) ^ chip
-                outer, a, b = relative >> 2, (relative >> order[0]) & 1, (relative >> order[1]) & 1
-                send, keep = outs[2 * index], outs[2 * index + 1]
-
-                @pl.when(a == 1)
-                def _():
-                    send[b, outer, half] = value.astype(send.dtype)
-
-                @pl.when(a == 0)
-                def _():
-                    keep[b, outer, half] = value
+                outer = group ^ (chip >> 2)
+                target = pair[1 - ((near >> order[0]) & 1)]
+                target[(near >> order[1]) & 1, outer, 0 if split else half] = value.astype(target.dtype)
 
     for half in range(halves):
         for group in range(own.shape[2] // span):
@@ -142,10 +137,11 @@
         two = [project(spot, arrived, own[h : h + 1], other[h : h + 1], count_x, cuts, stages) for h in range(2)]
         return [jnp.concatenate(pair, axis=2) for pair in zip(*two)]
     shapes = []
-    for first, last, _ in cuts:
+    for first, last, orders in cuts:
         lines = count_x * (last - first) * block // LANES
-        for kind in (wire_type(0, stages), jnp.float32):
-            shapes.append(jax.ShapeDtypeStruct((2, groups, own.shape[0], lines, LANES), kind))
+        halves = 1 if len(orders) > 1 else own.shape[0]
+        for kind in (wire_type(0, stages), jnp.float32) * len(orders):
+            shapes.append(jax.ShapeDtypeStruct((2, groups, halves, lines, LANES), kind))
     inside = pl.BlockSpec(memory_space=pltpu.VMEM)
     scratch = jax.ShapeDtypeStruct((2, rows, QUAD * block), jnp.float32)
     held = sum(t.size * t.dtype.itemsize for t in [*arrived, *arrived, own, other, scratch, *shapes])
@@ -168,54 +164,68 @@
     )(spot, *arrived, own, other)
 
 
-def down_kernel(block, count, order, place_ref, keep_in, recv_in, own, other, send, keep, hidden):
+def down_kernel(block, count, order, place_ref, *refs):
+    terms, (own, other, send, keep, hidden) = refs[:-5], refs[-5:]
     chip, core = place_ref[0], place_ref[1]
     whole_tiles, rest = block // LANES, block % LANES
     fold = LANES // rest
 
+    chips = 4 * send.shape[1]
+    each = count // chips
+
+    def by_owner(value):
+        if chips > 4:
+            return value
+        blocks = [value[i * each : (i + 1) * each] for i in range(4)]
+        for bit in (1, 2):
+            flip = (chip & bit) != 0
+            blocks = [jnp.where(flip, blocks[i ^ bit], blocks[i]) for i in range(4)]
+        return jnp.concatenate(blocks)
+
     @pl.when(pl.program_id(0) == 0)
     def _():
-        gate = keep_in[0] + recv_in[0].astype(jnp.float32)
-        upper = keep_in[1] + recv_in[1].astype(jnp.float32)
+        gate = terms[0][0] + terms[1][0].astype(jnp.float32)
+        last = terms[-1].shape[0] - 1
+        upper = terms[-2][last] + terms[-1][last].astype(jnp.float32)
         value = gate / (1.0 + jnp.exp(-gate)) * upper
         tiles = jnp.concatenate(
             [value[piece * count : (piece + 1) * count] for piece in range(whole_tiles)], axis=1
         )
         shift = (chip & (QUAD - 1)) * rest
         turned = pltpu.roll(tiles, lax.rem(whole_tiles * LANES - shift, whole_tiles * LANES), 1)
+        turned = by_owner(turned)
         high = turned.astype(jnp.bfloat16)
         hidden[:count, : whole_tiles * LANES] = high
         hidden[count:, : whole_tiles * LANES] = (turned - high.astype(jnp.float32)).astype(jnp.bfloat16)
         packed = value[whole_tiles * count :]
         part = count // fold
-        for k in range(fold):
-            turned = pltpu.roll(packed, (LANES - k * rest) % LANES, 1) if k else packed
-            turned = turned[:, :rest]
-            high = turned.astype(jnp.bfloat16)
-            hidden[k * part : (k + 1) * part, whole_tiles * LANES :] = high
-            hidden[count + k * part : count + (k + 1) * part, whole_tiles * LANES :] = (
-                turned - high.astype(jnp.float32)
-            ).astype(jnp.bfloat16)
+        turned = [pltpu.roll(packed, (LANES - k * rest) % LANES, 1) if k else packed for k in range(fold)]
+        turned = by_owner(jnp.concatenate(turned))[:, :rest]
+        high = turned.astype(jnp.bfloat16)
+        hidden[:count, whole_tiles * LANES :] = high
+        hidden[count:, whole_tiles * LANES :] = (turned - high.astype(jnp.float32)).astype(jnp.bfloat16)
 
     low, high = hidden[:, : block // 2], hidden[:, block // 2 :]
     product = jnp.dot(
         jnp.where(core == 0, low, high), own[...], preferred_element_type=jnp.float32
     ) + jnp.dot(jnp.where(core == 0, high, low), other[...], preferred_element_type=jnp.float32)
     product = product[:count] + product[count:]
-    chips = 4 * send.shape[1]
-    each = count // chips
     for owner in range(chips):
-        place(owner ^ lax.rem(chip, chips), order, send, keep, product[owner * each : (owner + 1) * each])
-
-
-def down_project(spot, keep, recv, own, other, count, order, count_x, stages, span=(0, 1), wide=4096):
+        value = product[owner * each : (owner + 1) * each]
+        if chips > 4:
+            place(owner ^ lax.rem(chip, chips), order, send, keep, value)
+        else:
+            target = send if (owner >> order[0]) & 1 else keep
+            target[(owner >> order[1]) & 1, 0] = value.astype(target.dtype)
+
+
+def down_project(spot, terms, own, other, count, order, count_x, stages, span=(0, 1), wide=4096):
     block, features = 2 * own.shape[0], own.shape[1]
     part, parts = span
     features = features // parts
     wide = min(wide, features)
     groups = count_x // 2 // QUAD
     each = count // (count_x // 2)
-    whole = pl.BlockSpec(keep.shape, lambda c, s: (0, 0, 0))
     out = pl.BlockSpec((2, groups, each, wide), lambda c, s: (0, 0, 0, c))
     weights = pl.BlockSpec((block // 2, wide), lambda c, s: (0, part * (features // wide) + c))
     return pl.pallas_call(
@@ -228,8 +238,7 @@
             num_scalar_prefetch=1,
             grid=(features // wide,),
             in_specs=[
-                whole,
-                whole,
+                *[pl.BlockSpec(term.shape, lambda c, s: (0, 0, 0)) for term in terms],
                 weights,
                 weights,
             ],
@@ -242,7 +251,7 @@
         cost_estimate=pl.CostEstimate(
             flops=2 * count * block * features, bytes_accessed=2 * block * features, transcendentals=0
         ),
-    )(spot, keep, recv, own, other)
+    )(spot, *terms, own, other)
 
 
 def swap(value, bit):
@@ -259,7 +268,7 @@
 
 
 def halving(send, keep, order, count, stages, done):
-    recv = swap(after(send, done), order[0])
+    recv = swap(send if done is None else after(send, done), order[0])
     done = yield send
     for stage in range(1, count):
         acc = keep + after(recv, done).astype(jnp.float32)
@@ -278,14 +287,36 @@
     return lax.ppermute(value, ("gx", "gy"), [(2 * a + b, 2 * c + d) for (a, b), (c, d) in pairs])
 
 
+def together(ways):
+    done, ends = None, []
+    while len(ends) < len(ways):
+        sent = []
+        for way in ways:
+            try:
+                sent.append(way.send(done))
+            except StopIteration as end:
+                ends.append(end.value)
+        if sent:
+            done = yield sent
+    return ends
+
+
 def chunk_steps(spot, flags, parts, downs, count, orders, count_x, stages):
     first_core, owner = flags
     done = yield
-    keep, recv = yield from halving(parts[0], parts[1], orders[0], stages, stages, done)
-    send, keep = down_project(spot, keep, recv, *downs, count, orders[1], count_x, stages)
-    keep, recv = yield from halving(send, keep, orders[1], stages - 1, stages, None)
-    acc = keep + recv.astype(jnp.float32)
-    low, high = jnp.split(acc, 2, axis=1)
+    ways = [
+        halving(parts[2 * i], parts[2 * i + 1], order, stages, stages, done) for i, order in enumerate(orders[0])
+    ]
+    terms = yield from together(ways)
+    terms = [term for pair in terms for term in pair]
+    ways = []
+    for part, order in enumerate(orders[1]):
+        span = (part, len(orders[1]))
+        sent, kept = down_project(spot, terms, *downs, count, order, count_x, stages, span)
+        ways.append(halving(sent, kept, order, stages - 1, stages, None))
+    terms = yield from together(ways)
+    sums = [keep + recv.astype(jnp.float32) for keep, recv in terms]
+    low, high = jnp.split(sums[0], 2, axis=1) if len(sums) == 1 else sums
     mine, send = jnp.where(first_core, low, high), jnp.where(first_core, high, low)
     got = swap_cores(send)
     done = yield send
@@ -323,13 +354,14 @@
     if stages == 3 and each == 24:
         step, orders, turns = 8, ORDERS, TURNS
     else:
-        step, orders = each, [((0, 1), (0, 1))]
+        step, orders = each, [(((0, 1),), ((0, 1),))]
         turns = [0] * (2 * stages + 2)
     cuts = tuple((i * step, (i + 1) * step, order[0]) for i, order in enumerate(orders))
+    starts = [2 * sum(len(order[0]) for order in orders[:i]) for i in range(len(orders) + 1)]
     parts = project(spot, arrived, gate_up, other, count_x, cuts, stages)
     chunks = [
         chunk_steps(
-            spot, flags, parts[2 * i : 2 * i + 2], (down_weight, down_other), count_x * step, order, count_x, stages
+            spot, flags, parts[starts[i] : starts[i + 1]], (down_weight, down_other), count_x * step, order, count_x, stages
         )
         for i, order in enumerate(orders)
     ]

time: 119 us -> 109 us (0.916)
  waiting for transfers between devices: 54.1 us -> 44.3 us
  Pallas kernels: 19.5 us -> 16.5 us
  starting transfers between devices: 41.2 us -> 43.9 us
    ppermute x18 -> x27, waiting for transfers between devices: 50.4 us -> 40.5 us  [swap(): return lax.ppermute(value, 'gx', [(i, i ^ 1 << bit) for i in range(count)])]
    ppermute x18 -> x27, starting transfers between devices: 27 us -> 29.8 us  [swap(): return lax.ppermute(value, 'gx', [(i, i ^ 1 << bit) for i in range(count)])]
    pallas_call x1, Pallas kernels: 9.58 us -> 7.02 us  [project(): pl.pallas_call(functools.partial(project_kernel, block, cuts, len(arrived...]
    pallas_call x3 -> x6, Pallas kernels: 9.33 us -> 8.87 us  [down_project(): pl.pallas_call(functools.partial(down_kernel, block, count, order), out_s...]
  transfers between devices with their start and end apart: 27 -> 36, of which waited for: 14 -> 13; matrix products, arithmetic and copies ran while one was open for 1% -> 1% of each run, Pallas kernels for 16% -> 15%
where the time goes in v3:
time: 109 us
  waiting for transfers between devices  44.3 us (41%)
  starting transfers between devices  43.9 us (40%)
  Pallas kernels  16.5 us (15%)
  other arithmetic  2.15 us (2%)
  local copies, waits for them, and re-layouts  1.3 us (1%)
    ppermute x27, waiting for transfers between devices, swap(): return lax.ppermute(value, 'gx', [(i, i ^ 1 << bit) for i in range(count)])  40.5 us
    ppermute x27, starting transfers between devices, swap(): return lax.ppermute(value, 'gx', [(i, i ^ 1 << bit) for i in range(count)])  29.8 us
    pallas_call x6, Pallas kernels, down_project(): pl.pallas_call(functools.partial(down_kernel, block, count, order), out_s...  8.87 us
    ppermute x5, starting transfers between devices, swap_cores(): return lax.ppermute(value, 'gy', [(0, 1), (1, 0)])  7.92 us
    pallas_call x1, Pallas kernels, project(): pl.pallas_call(functools.partial(project_kernel, block, cuts, len(arrived...  7.02 us
    ppermute x4, starting transfers between devices, move(): lax.ppermute(value, ('gx', 'gy'), [(2 * a + b, 2 * c + d) for (a, b), (c,...  6.22 us
    ppermute x4, waiting for transfers between devices, move(): lax.ppermute(value, ('gx', 'gy'), [(2 * a + b, 2 * c + d) for (a, b), (c,...  3.74 us
  transfers between devices with their start and end apart: 36, of which 13 were waited for; matrix products, arithmetic and copies ran while one was open for 1% of the time, Pallas kernels for 15%

profile of v3, /device:TPU:0, one launch (start us, length us, event | category | flops | bytes accessed | tf_op | source)
XLA Modules:
  0.0 108.5 jit_solution(1657890128141327471)
XLA Ops:
  0.0 0.5 collective-permute-start.4
  0.5 0.1 pad_add_fusion.place_ref
  0.5 1.0 copy-done.1
  1.5 0.6 shard_map.37
  2.1 0.7 collective-permute-start
  2.8 2.5 %collective-permute-start.1 = (bf16[48,1024]{1,0:T(8,128)(2,1)S(1)}, bf16[48,1024]{1,0:T(8,128)(2,1)S(1)}, u32[]{:S(2)}, u32[]{:S(2)}) collective-permute-start(bf16[48,1024]{1,0:T(8,128)(2,1)S(1)} %get-tuple-element.72), channel_id=1, source_target_pairs={{0,2},{1,10},{2,4},{3,12},{4,6},{5,14},{6,0},{7,8},{8,3},{9,11},{1... | collective-permute-start | bytes 294920 | tf_op jit(solution)/shard_map/ppermute | solution.py:287
  5.3 1.6 %collective-permute-start.2 = (bf16[48,1024]{1,0:T(8,128)(2,1)S(1)}, bf16[48,1024]{1,0:T(8,128)(2,1)S(1)}, u32[]{:S(2)}, u32[]{:S(2)}) collective-permute-start(bf16[48,1024]{1,0:T(8,128)(2,1)S(1)} %get-tuple-element.73), channel_id=1, source_target_pairs={{0,4},{1,12},{2,6},{3,14},{4,0},{5,8},{6,2},{7,10},{8,5},{9,13},{1... | collective-permute-start | bytes 294920 | tf_op jit(solution)/shard_map/ppermute | solution.py:287
  6.9 1.4 %collective-permute-start.3 = (bf16[48,1024]{1,0:T(8,128)(2,1)S(1)}, bf16[48,1024]{1,0:T(8,128)(2,1)S(1)}, u32[]{:S(2)}, u32[]{:S(2)}) collective-permute-start(bf16[48,1024]{1,0:T(8,128)(2,1)S(1)} %get-tuple-element.74), channel_id=1, source_target_pairs={{0,6},{1,14},{2,0},{3,8},{4,2},{5,10},{6,4},{7,12},{8,7},{9,15},{1... | collective-permute-start | bytes 294920 | tf_op jit(solution)/shard_map/ppermute | solution.py:287
  8.3 0.6 collective-permute-done.1.refs_1_
  8.9 2.1 %collective-permute-done.2.refs_2_ = bf16[48,1024]{1,0:T(8,128)(2,1)S(1)} collective-permute-done((bf16[48,1024]{1,0:T(8,128)(2,1)S(1)}, bf16[48,1024]{1,0:T(8,128)(2,1)S(1)}, u32[]{:S(2)}, u32[]{:S(2)}) %collective-permute-start.2) | collective-permute-done | bytes 98336 | tf_op jit(solution)/shard_map/ppermute | solution.py:287
  11.0 1.1 %collective-permute-done.3.refs_3_ = bf16[48,1024]{1,0:T(8,128)(2,1)S(1)} collective-permute-done((bf16[48,1024]{1,0:T(8,128)(2,1)S(1)}, bf16[48,1024]{1,0:T(8,128)(2,1)S(1)}, u32[]{:S(2)}, u32[]{:S(2)}) %collective-permute-start.3) | collective-permute-done | bytes 98336 | tf_op jit(solution)/shard_map/ppermute | solution.py:287
  12.1 7.3 %collective-permute-start.12 = (bf16[208,8192]{1,0:T(8,128)(2,1)}, bf16[208,8192]{1,0:T(8,128)(2,1)S(1)}, u32[]{:S(2)}, u32[]{:S(2)}) collective-permute-start(bf16[208,8192]{1,0:T(8,128)(2,1)} %refs_4_.5), channel_id=1, source_target_pairs={{0,1},{1,0},{2,3},{3,2},{4,5},{5,4},{6,7},{7,6},{8,9},{9,8},{10,11... | collective-permute-start | bytes 10223624 | tf_op jit(solution)/shard_map/ppermute | solution.py:263
  19.3 7.0 %shard_map.38 = (bf16[2,2,2,208,128]{4,3,2,1,0:T(8,128)(2,1)S(1)}, f32[2,2,2,208,128]{4,3,2,1,0:T(8,128)S(1)}, bf16[2,2,2,208,128]{4,3,2,1,0:T(8,128)(2,1)S(1)},...) custom-call(s32[2]{0:T(128)S(1)} %pad_add_fusion.place_ref, ...), custom_call_target="tpu_custom_call" | custom-call | flops 1308622848 | bytes 6815744 | tf_op jit(solution)/shard_map/pallas_call | solution.py:148
  26.4 0.4 collective-permute-start.5
  26.7 1.4 %collective-permute-start.8 = (bf16[2,2,2,208,128]{4,3,2,1,0:T(8,128)(2,1)S(1)}, bf16[2,2,2,208,128]{4,3,2,1,0:T(8,128)(2,1)S(1)}, u32[]{:S(2)}, u32[]{:S(2)}) collective-permute-start(bf16[2,2,2,208,128]{4,3,2,1,0:T(8,128)(2,1)S(1)} %get-tuple-element.84), channel_id=1, source_target_pairs={{0,4},{2,6},{4,0},{6,2},{8,12},{10,14},{12,8},{14,10},{1,5},{3,7},... | collective-permute-start | bytes 1277960 | tf_op jit(solution)/shard_map/ppermute | solution.py:259
  28.1 10.0 %collective-permute-done.5 = bf16[2,2,2,208,128]{4,3,2,1,0:T(8,128)(2,1)S(1)} collective-permute-done((bf16[2,2,2,208,128]{4,3,2,1,0:T(8,128)(2,1)S(1)}, bf16[2,2,2,208,128]{4,3,2,1,0:T(8,128)(2,1)S(1)}, u32[]{:S(2)}, u32[]{:S(2)}) %collective-permute-start.5) | collective-permute-done | bytes 426016 | tf_op jit(solution)/shard_map/ppermute | solution.py:259
  38.2 0.1 convert_add_fusion.1
  38.3 0.1 collective-permute-start.6
  38.4 0.1 convert_add_fusion
  38.5 1.7 %collective-permute-start.10 = (bf16[2,2,208,128]{3,2,1,0:T(8,128)(2,1)S(1)}, bf16[2,2,208,128]{3,2,1,0:T(8,128)(2,1)S(1)}, u32[]{:S(2)}, u32[]{:S(2)}) collective-permute-start(bf16[2,2,208,128]{3,2,1,0:T(8,128)(2,1)S(1)} %fusion.9), channel_id=1, source_target_pairs={{0,2},{2,0},{4,6},{6,4},{8,10},{10,8},{12,14},{14,12},{1,3},{3,1},... | collective-permute-start | bytes 638984 | tf_op jit(solution)/shard_map/ppermute | solution.py:259
  40.2 0.7 collective-permute-start.11
  40.9 1.7 %collective-permute-start.9 = (bf16[2,2,1,208,128]{4,3,1,2,0:T(8,128)(2,1)S(1)}, bf16[2,2,1,208,128]{4,3,1,2,0:T(8,128)(2,1)S(1)}, u32[]{:S(2)}, u32[]{:S(2)}) collective-permute-start(bf16[2,2,1,208,128]{4,3,1,2,0:T(8,128)(2,1)S(1)} %bitcast.160), channel_id=1, source_target_pairs={{0,2},{2,0},{4,6},{6,4},{8,10},{10,8},{12,14},{14,12},{1,3},{3,1},... | collective-permute-start | bytes 638984 | tf_op jit(solution)/shard_map/ppermute | solution.py:259
  42.6 3.9 %collective-permute-done.6 = bf16[2,2,208,128]{3,2,1,0:T(8,128)(2,1)S(1)} collective-permute-done((bf16[2,2,208,128]{3,2,1,0:T(8,128)(2,1)S(1)}, bf16[2,2,208,128]{3,2,1,0:T(8,128)(2,1)S(1)}, u32[]{:S(2)}, u32[]{:S(2)}) %collective-permute-start.6) | collective-permute-done | bytes 213024 | tf_op jit(solution)/shard_map/ppermute | solution.py:259
  46.6 1.5 %collective-permute-start.7 = (bf16[1,2,208,128]{3,2,1,0:T(8,128)(2,1)S(1)}, bf16[1,2,208,128]{3,2,1,0:T(8,128)(2,1)S(1)}, u32[]{:S(2)}, u32[]{:S(2)}) collective-permute-start(bf16[1,2,208,128]{3,2,1,0:T(8,128)(2,1)S(1)} %slice.247), channel_id=1, source_target_pairs={{0,8},{2,10},{4,12},{6,14},{8,0},{10,2},{12,4},{14,6},{1,9},{3,11}... | collective-permute-start | bytes 319496 | tf_op jit(solution)/shard_map/ppermute | solution.py:259
  48.2 2.2 %collective-permute-start.14 = (bf16[1,2,208,128]{3,2,1,0:T(8,128)(2,1)S(1)}, bf16[1,2,208,128]{3,2,1,0:T(8,128)(2,1)S(1)}, u32[]{:S(2)}, u32[]{:S(2)}) collective-permute-start(bf16[1,2,208,128]{3,2,1,0:T(8,128)(2,1)S(1)} %slice.246), channel_id=1, source_target_pairs={{0,8},{2,10},{4,12},{6,14},{8,0},{10,2},{12,4},{14,6},{1,9},{3,11}... | collective-permute-start | bytes 319496 | tf_op jit(solution)/shard_map/ppermute | solution.py:259
  50.5 1.0 collective-permute-done.11
  51.6 0.2 collective-permute-start.16
  51.8 0.8 collective-permute-start.15
  52.7 3.8 %collective-permute-done.7 = bf16[1,2,208,128]{3,2,1,0:T(8,128)(2,1)S(1)} collective-permute-done((bf16[1,2,208,128]{3,2,1,0:T(8,128)(2,1)S(1)}, bf16[1,2,208,128]{3,2,1,0:T(8,128)(2,1)S(1)}, u32[]{:S(2)}, u32[]{:S(2)}) %collective-permute-start.7) | collective-permute-done | bytes 106528 | tf_op jit(solution)/shard_map/ppermute | solution.py:259
  56.5 1.5 %shard_map.40 = (bf16[2,1,16,4096]{3,2,1,0:T(8,128)(2,1)S(1)}, f32[2,1,16,4096]{3,2,1,0:T(8,128)S(1)}) custom-call(s32[2]{0:T(128)S(1)} %pad_add_fusion.place_ref, f32[2,208,128]{2,1,0:T(8,128)S(1)} %slice_bitcast_fusion.11.refs_0_, bf16[2,208,128]{2,1,0:T(8,128)(2,1)S(1)} %bitcast.153, bf16[208,8192]{1,0:T(8,128)(2,1)S(1)} %copy-done, ...), custom_call_target="tpu_custom_call" | custom-call | flops 218103808 | bytes 3407872 | tf_op jit(solution)/shard_map/pallas_call | solution.py:231
  57.9 0.1 collective-permute-start.20
  58.0 1.5 %shard_map.39 = (bf16[2,1,16,4096]{3,2,1,0:T(8,128)(2,1)S(1)}, f32[2,1,16,4096]{3,2,1,0:T(8,128)S(1)}) custom-call(s32[2]{0:T(128)S(1)} %pad_add_fusion.place_ref, f32[2,208,128]{2,1,0:T(8,128)S(1)} %slice_bitcast_fusion.11.refs_0_, bf16[2,208,128]{2,1,0:T(8,128)(2,1)S(1)} %bitcast.154, bf16[208,8192]{1,0:T(8,128)(2,1)S(1)} %copy-done, ...), custom_call_target="tpu_custom_call" | custom-call | flops 218103808 | bytes 3407872 | tf_op jit(solution)/shard_map/pallas_call | solution.py:231
  59.5 0.8 collective-permute-start.13
  60.4 2.9 %collective-permute-start.21 = (bf16[1,1,208,128]{3,2,1,0:T(8,128)(2,1)S(1)}, bf16[1,1,208,128]{3,2,1,0:T(8,128)(2,1)S(1)}, u32[]{:S(2)}, u32[]{:S(2)}) collective-permute-start(bf16[1,1,208,128]{3,2,1,0:T(8,128)(2,1)S(1)} %slice.248), channel_id=1, source_target_pairs={{0,8},{2,10},{4,12},{6,14},{8,0},{10,2},{12,4},{14,6},{1,9},{3,11}... | collective-permute-start | bytes 159752 | tf_op jit(solution)/shard_map/ppermute | solution.py:259
  63.3 0.1 collective-permute-start.19
  63.4 1.5 %shard_map.42 = (bf16[2,1,16,4096]{3,2,1,0:T(8,128)(2,1)S(1)}, f32[2,1,16,4096]{3,2,1,0:T(8,128)S(1)}) custom-call(s32[2]{0:T(128)S(1)} %pad_add_fusion.place_ref, f32[2,208,128]{2,1,0:T(8,128)S(1)} %slice_bitcast_fusion.10.refs_0_, bf16[2,208,128]{2,1,0:T(8,128)(2,1)S(1)} %bitcast.151, bf16[208,8192]{1,0:T(8,128)(2,1)S(1)} %copy-done, ...), custom_call_target="tpu_custom_call" | custom-call | flops 218103808 | bytes 3407872 | tf_op jit(solution)/shard_map/pallas_call | solution.py:231
  64.9 2.1 %collective-permute-start.22 = (bf16[2,1,16,4096]{3,2,1,0:T(8,128)(2,1)S(1)}, bf16[2,1,16,4096]{3,2,1,0:T(8,128)(2,1)S(1)}, u32[]{:S(2)}, u32[]{:S(2)}) collective-permute-start(bf16[2,1,16,4096]{3,2,1,0:T(8,128)(2,1)S(1)} %get-tuple-element.101), channel_id=1, source_target_pairs={{0,4},{2,6},{4,0},{6,2},{8,12},{10,14},{12,8},{14,10},{1,5},{3,7},... | collective-permute-start | bytes 786440 | tf_op jit(solution)/shard_map/ppermute | solution.py:259
  66.9 1.5 %shard_map.41 = (bf16[2,1,16,4096]{3,2,1,0:T(8,128)(2,1)S(1)}, f32[2,1,16,4096]{3,2,1,0:T(8,128)S(1)}) custom-call(s32[2]{0:T(128)S(1)} %pad_add_fusion.place_ref, f32[2,208,128]{2,1,0:T(8,128)S(1)} %slice_bitcast_fusion.10.refs_0_, bf16[2,208,128]{2,1,0:T(8,128)(2,1)S(1)} %bitcast.152, bf16[208,8192]{1,0:T(8,128)(2,1)S(1)} %copy-done, ...), custom_call_target="tpu_custom_call" | custom-call | flops 218103808 | bytes 3407872 | tf_op jit(solution)/shard_map/pallas_call | solution.py:231
  68.5 1.4 %collective-permute-start.18 = (bf16[2,1,16,4096]{3,2,1,0:T(8,128)(2,1)S(1)}, bf16[2,1,16,4096]{3,2,1,0:T(8,128)(2,1)S(1)}, u32[]{:S(2)}, u32[]{:S(2)}) collective-permute-start(bf16[2,1,16,4096]{3,2,1,0:T(8,128)(2,1)S(1)} %get-tuple-element.100), channel_id=1, source_target_pairs={{0,2},{2,0},{4,6},{6,4},{8,10},{10,8},{12,14},{14,12},{1,3},{3,1},... | collective-permute-start | bytes 786440 | tf_op jit(solution)/shard_map/ppermute | solution.py:259
  70.0 0.1 collective-permute-start.17
  70.1 0.8 collective-permute-start.23
  70.9 1.5 %shard_map.43 = (bf16[2,1,16,4096]{3,2,1,0:T(8,128)(2,1)S(1)}, f32[2,1,16,4096]{3,2,1,0:T(8,128)S(1)}) custom-call(s32[2]{0:T(128)S(1)} %pad_add_fusion.place_ref, f32[1,208,128]{2,1,0:T(8,128)S(1)} %slice_bitcast_fusion.13.refs_0_, bf16[1,208,128]{2,1,0:T(8,128)(2,1)S(1)} %bitcast.158, f32[1,208,128]{2,1,0:T(8,128)S(1)} %slice_bitcast_fusion.12.refs_2_, ...), custom_call_target="tpu_custom_call" | custom-call | flops 218103808 | bytes 3407872 | tf_op jit(solution)/shard_map/pallas_call | solution.py:231
  72.4 1.4 %collective-permute-start.29 = (bf16[2,1,16,4096]{3,2,1,0:T(8,128)(2,1)S(1)}, bf16[2,1,16,4096]{3,2,1,0:T(8,128)(2,1)S(1)}, u32[]{:S(2)}, u32[]{:S(2)}) collective-permute-start(bf16[2,1,16,4096]{3,2,1,0:T(8,128)(2,1)S(1)} %get-tuple-element.108), channel_id=1, source_target_pairs={{0,2},{2,0},{4,6},{6,4},{8,10},{10,8},{12,14},{14,12},{1,3},{3,1},... | collective-permute-start | bytes 786440 | tf_op jit(solution)/shard_map/ppermute | solution.py:259
  73.8 1.5 %shard_map.44 = (bf16[2,1,16,4096]{3,2,1,0:T(8,128)(2,1)S(1)}, f32[2,1,16,4096]{3,2,1,0:T(8,128)S(1)}) custom-call(s32[2]{0:T(128)S(1)} %pad_add_fusion.place_ref, f32[1,208,128]{2,1,0:T(8,128)S(1)} %slice_bitcast_fusion.13.refs_0_, bf16[1,208,128]{2,1,0:T(8,128)(2,1)S(1)} %bitcast.159, f32[1,208,128]{2,1,0:T(8,128)S(1)} %slice_bitcast_fusion.12.refs_2_, ...), custom_call_target="tpu_custom_call" | custom-call | flops 218103808 | bytes 3407872 | tf_op jit(solution)/shard_map/pallas_call | solution.py:231
  75.3 2.0 %collective-permute-start.30 = (bf16[2,1,16,4096]{3,2,1,0:T(8,128)(2,1)S(1)}, bf16[2,1,16,4096]{3,2,1,0:T(8,128)(2,1)S(1)}, u32[]{:S(2)}, u32[]{:S(2)}) collective-permute-start(bf16[2,1,16,4096]{3,2,1,0:T(8,128)(2,1)S(1)} %get-tuple-element.109), channel_id=1, source_target_pairs={{0,4},{2,6},{4,0},{6,2},{8,12},{10,14},{12,8},{14,10},{1,5},{3,7},... | collective-permute-start | bytes 786440 | tf_op jit(solution)/shard_map/ppermute | solution.py:259
  77.4 0.8 collective-permute-start.25
  78.2 1.1 collective-permute-start.26
  79.3 0.1 collective-permute-start.24
  79.4 3.4 %collective-permute-done.25 = bf16[1,16,4096]{2,1,0:T(8,128)(2,1)S(1)} collective-permute-done((bf16[1,16,4096]{2,1,0:T(8,128)(2,1)S(1)}, bf16[1,16,4096]{2,1,0:T(8,128)(2,1)S(1)}, u32[]{:S(2)}, u32[]{:S(2)}) %collective-permute-start.25) | collective-permute-done | bytes 131104 | tf_op jit(solution)/shard_map/ppermute | solution.py:259
  82.8 0.4 collective-permute-done.26
  83.2 0.1 fusion.15
  83.3 0.1 select_convert_fusion.2
  83.4 2.4 %collective-permute-start.27 = (bf16[16,4096]{1,0:T(8,128)(2,1)S(1)}, bf16[16,4096]{1,0:T(8,128)(2,1)S(1)}, u32[]{:S(2)}, u32[]{:S(2)}) collective-permute-start(bf16[16,4096]{1,0:T(8,128)(2,1)S(1)} %get-tuple-element.133), channel_id=1, source_target_pairs={{0,8},{2,10},{4,12},{6,14},{8,0},{10,2},{12,4},{14,6},{1,9},{3,11}... | collective-permute-start | bytes 393224 | tf_op jit(solution)/shard_map/ppermute | solution.py:259
  86.0 1.1 %collective-permute-start.32 = (bf16[1,16,4096]{2,1,0:T(8,128)(2,1)S(1)}, bf16[1,16,4096]{2,1,0:T(8,128)(2,1)S(1)}, u32[]{:S(2)}, u32[]{:S(2)}) collective-permute-start(bf16[1,16,4096]{2,1,0:T(8,128)(2,1)S(1)} %fusion.26), channel_id=1, source_target_pairs={{0,2},{2,0},{4,6},{6,4},{8,10},{10,8},{12,14},{14,12},{1,3},{3,1},... | collective-permute-start | bytes 393224 | tf_op jit(solution)/shard_map/ppermute | solution.py:259
  87.1 1.2 %collective-permute-start.33 = (bf16[1,16,4096]{2,1,0:T(8,128)(2,1)S(1)}, bf16[1,16,4096]{2,1,0:T(8,128)(2,1)S(1)}, u32[]{:S(2)}, u32[]{:S(2)}) collective-permute-start(bf16[1,16,4096]{2,1,0:T(8,128)(2,1)S(1)} %fusion.25), channel_id=1, source_target_pairs={{0,4},{2,6},{4,0},{6,2},{8,12},{10,14},{12,8},{14,10},{1,5},{3,7},... | collective-permute-start | bytes 393224 | tf_op jit(solution)/shard_map/ppermute | solution.py:259
  88.3 0.1 select_convert_fusion.1
  88.4 1.0 collective-permute-start.31
  89.4 4.2 %collective-permute-done.27 = bf16[16,4096]{1,0:T(8,128)(2,1)S(1)} collective-permute-done((bf16[16,4096]{1,0:T(8,128)(2,1)S(1)}, bf16[16,4096]{1,0:T(8,128)(2,1)S(1)}, u32[]{:S(2)}, u32[]{:S(2)}) %collective-permute-start.27) | collective-permute-done | bytes 131104 | tf_op jit(solution)/shard_map/ppermute | solution.py:259
  93.6 1.7 %collective-permute-done.33 = bf16[1,16,4096]{2,1,0:T(8,128)(2,1)S(1)} collective-permute-done((bf16[1,16,4096]{2,1,0:T(8,128)(2,1)S(1)}, bf16[1,16,4096]{2,1,0:T(8,128)(2,1)S(1)}, u32[]{:S(2)}, u32[]{:S(2)}) %collective-permute-start.33) | collective-permute-done | bytes 131104 | tf_op jit(solution)/shard_map/ppermute | solution.py:259
  95.3 0.1 collective-permute-start.34
  95.4 3.3 %collective-permute-done.31 = bf16[16,4096]{1,0:T(8,128)(2,1)S(1)} collective-permute-done((bf16[16,4096]{1,0:T(8,128)(2,1)S(1)}, bf16[16,4096]{1,0:T(8,128)(2,1)S(1)}, u32[]{:S(2)}, u32[]{:S(2)}) %collective-permute-start.31) | collective-permute-done | bytes 131104 | tf_op jit(solution)/shard_map/ppermute | solution.py:259
  98.8 0.1 collective-permute-start.35
  98.9 8.8 %collective-permute-done.35 = bf16[16,4096]{1,0:T(8,128)(2,1)S(1)} collective-permute-done((bf16[16,4096]{1,0:T(8,128)(2,1)S(1)}, bf16[16,4096]{1,0:T(8,128)(2,1)S(1)}, u32[]{:S(2)}, u32[]{:S(2)}) %collective-permute-start.35) | collective-permute-done | bytes 131104 | tf_op jit(solution)/shard_map/ppermute | solution.py:259
  107.7 0.8 pad_maximum_fusion
  (62 shorter events, 1.3 us)
Async XLA Ops:
  0.0 19.3 %collective-permute-start.4 = (bf16[2,512,3328]{2,1,0:T(8,128)(2,1)}, bf16[2,512,3328]{2,1,0:T(8,128)(2,1)}, u32[]{:S(2)}, u32[]{:S(2)}) collective-permute-start(bf16[2,512,3328]{2,1,0:T(8,128)(2,1)} %refs_4_.3), channel_id=1, source_target_pairs={{0,1},{1,0},{2,3},{3,2},{4,5},{5,4},{6,7},{7,6},{8,9},{9,8},{10,11... | collective-permute-start | bytes 20447240 | tf_op jit(solution)/shard_map/ppermute | solution.py:263
  0.5 1.0 copy-start.1
  2.1 6.2 %collective-permute-start = (bf16[48,1024]{1,0:T(8,128)(2,1)S(1)}, bf16[48,1024]{1,0:T(8,128)(2,1)S(1)}, u32[]{:S(2)}, u32[]{:S(2)}) collective-permute-start(bf16[48,1024]{1,0:T(8,128)(2,1)S(1)} %get-tuple-element.71), channel_id=1, source_target_pairs={{0,0},{1,8},{2,2},{3,10},{4,4},{5,12},{6,6},{7,14},{8,1},{9,9},{10... | collective-permute-start | bytes 294920 | tf_op jit(solution)/shard_map/ppermute | solution.py:287
  2.8 6.2 %collective-permute-start.1 = (bf16[48,1024]{1,0:T(8,128)(2,1)S(1)}, bf16[48,1024]{1,0:T(8,128)(2,1)S(1)}, u32[]{:S(2)}, u32[]{:S(2)}) collective-permute-start(bf16[48,1024]{1,0:T(8,128)(2,1)S(1)} %get-tuple-element.72), channel_id=1, source_target_pairs={{0,2},{1,10},{2,4},{3,12},{4,6},{5,14},{6,0},{7,8},{8,3},{9,11},{1... | collective-permute-start | bytes 294920 | tf_op jit(solution)/shard_map/ppermute | solution.py:287
  5.3 5.7 %collective-permute-start.2 = (bf16[48,1024]{1,0:T(8,128)(2,1)S(1)}, bf16[48,1024]{1,0:T(8,128)(2,1)S(1)}, u32[]{:S(2)}, u32[]{:S(2)}) collective-permute-start(bf16[48,1024]{1,0:T(8,128)(2,1)S(1)} %get-tuple-element.73), channel_id=1, source_target_pairs={{0,4},{1,12},{2,6},{3,14},{4,0},{5,8},{6,2},{7,10},{8,5},{9,13},{1... | collective-permute-start | bytes 294920 | tf_op jit(solution)/shard_map/ppermute | solution.py:287
  6.9 5.2 %collective-permute-start.3 = (bf16[48,1024]{1,0:T(8,128)(2,1)S(1)}, bf16[48,1024]{1,0:T(8,128)(2,1)S(1)}, u32[]{:S(2)}, u32[]{:S(2)}) collective-permute-start(bf16[48,1024]{1,0:T(8,128)(2,1)S(1)} %get-tuple-element.74), channel_id=1, source_target_pairs={{0,6},{1,14},{2,0},{3,8},{4,2},{5,10},{6,4},{7,12},{8,7},{9,15},{1... | collective-permute-start | bytes 294920 | tf_op jit(solution)/shard_map/ppermute | solution.py:287
  12.1 44.4 %collective-permute-start.12 = (bf16[208,8192]{1,0:T(8,128)(2,1)}, bf16[208,8192]{1,0:T(8,128)(2,1)S(1)}, u32[]{:S(2)}, u32[]{:S(2)}) collective-permute-start(bf16[208,8192]{1,0:T(8,128)(2,1)} %refs_4_.5), channel_id=1, source_target_pairs={{0,1},{1,0},{2,3},{3,2},{4,5},{5,4},{6,7},{7,6},{8,9},{9,8},{10,11... | collective-permute-start | bytes 10223624 | tf_op jit(solution)/shard_map/ppermute | solution.py:263
  26.4 30.1 %copy-start = (bf16[208,8192]{1,0:T(8,128)(2,1)S(1)}, bf16[208,8192]{1,0:T(8,128)(2,1)}, u32[]{:S(2)}) copy-start(bf16[208,8192]{1,0:T(8,128)(2,1)} %refs_4_.5) | copy-start | bytes 10223620
  26.4 11.8 %collective-permute-start.5 = (bf16[2,2,2,208,128]{4,3,2,1,0:T(8,128)(2,1)S(1)}, bf16[2,2,2,208,128]{4,3,2,1,0:T(8,128)(2,1)S(1)}, u32[]{:S(2)}, u32[]{:S(2)}) collective-permute-start(bf16[2,2,2,208,128]{4,3,2,1,0:T(8,128)(2,1)S(1)} %get-tuple-element.76), channel_id=1, source_target_pairs={{0,2},{2,0},{4,6},{6,4},{8,10},{10,8},{12,14},{14,12},{1,3},{3,1},... | collective-permute-start | bytes 1277960 | tf_op jit(solution)/shard_map/ppermute | solution.py:259
  26.7 11.6 %collective-permute-start.8 = (bf16[2,2,2,208,128]{4,3,2,1,0:T(8,128)(2,1)S(1)}, bf16[2,2,2,208,128]{4,3,2,1,0:T(8,128)(2,1)S(1)}, u32[]{:S(2)}, u32[]{:S(2)}) collective-permute-start(bf16[2,2,2,208,128]{4,3,2,1,0:T(8,128)(2,1)S(1)} %get-tuple-element.84), channel_id=1, source_target_pairs={{0,4},{2,6},{4,0},{6,2},{8,12},{10,14},{12,8},{14,10},{1,5},{3,7},... | collective-permute-start | bytes 1277960 | tf_op jit(solution)/shard_map/ppermute | solution.py:259
  38.3 8.3 %collective-permute-start.6 = (bf16[2,2,208,128]{3,2,1,0:T(8,128)(2,1)S(1)}, bf16[2,2,208,128]{3,2,1,0:T(8,128)(2,1)S(1)}, u32[]{:S(2)}, u32[]{:S(2)}) collective-permute-start(bf16[2,2,208,128]{3,2,1,0:T(8,128)(2,1)S(1)} %fusion.8), channel_id=1, source_target_pairs={{0,4},{2,6},{4,0},{6,2},{8,12},{10,14},{12,8},{14,10},{1,5},{3,7},... | collective-permute-start | bytes 638984 | tf_op jit(solution)/shard_map/ppermute | solution.py:259
  38.5 9.6 %collective-permute-start.10 = (bf16[2,2,208,128]{3,2,1,0:T(8,128)(2,1)S(1)}, bf16[2,2,208,128]{3,2,1,0:T(8,128)(2,1)S(1)}, u32[]{:S(2)}, u32[]{:S(2)}) collective-permute-start(bf16[2,2,208,128]{3,2,1,0:T(8,128)(2,1)S(1)} %fusion.9), channel_id=1, source_target_pairs={{0,2},{2,0},{4,6},{6,4},{8,10},{10,8},{12,14},{14,12},{1,3},{3,1},... | collective-permute-start | bytes 638984 | tf_op jit(solution)/shard_map/ppermute | solution.py:259
  40.2 11.2 %collective-permute-start.11 = (bf16[2,2,1,208,128]{4,3,1,2,0:T(8,128)(2,1)S(1)}, bf16[2,2,1,208,128]{4,3,1,2,0:T(8,128)(2,1)S(1)}, u32[]{:S(2)}, u32[]{:S(2)}) collective-permute-start(bf16[2,2,1,208,128]{4,3,1,2,0:T(8,128)(2,1)S(1)} %bitcast.161), channel_id=1, source_target_pairs={{0,4},{2,6},{4,0},{6,2},{8,12},{10,14},{12,8},{14,10},{1,5},{3,7},... | collective-permute-start | bytes 638984 | tf_op jit(solution)/shard_map/ppermute | solution.py:259
  40.9 10.5 %collective-permute-start.9 = (bf16[2,2,1,208,128]{4,3,1,2,0:T(8,128)(2,1)S(1)}, bf16[2,2,1,208,128]{4,3,1,2,0:T(8,128)(2,1)S(1)}, u32[]{:S(2)}, u32[]{:S(2)}) collective-permute-start(bf16[2,2,1,208,128]{4,3,1,2,0:T(8,128)(2,1)S(1)} %bitcast.160), channel_id=1, source_target_pairs={{0,2},{2,0},{4,6},{6,4},{8,10},{10,8},{12,14},{14,12},{1,3},{3,1},... | collective-permute-start | bytes 638984 | tf_op jit(solution)/shard_map/ppermute | solution.py:259
  46.6 9.8 %collective-permute-start.7 = (bf16[1,2,208,128]{3,2,1,0:T(8,128)(2,1)S(1)}, bf16[1,2,208,128]{3,2,1,0:T(8,128)(2,1)S(1)}, u32[]{:S(2)}, u32[]{:S(2)}) collective-permute-start(bf16[1,2,208,128]{3,2,1,0:T(8,128)(2,1)S(1)} %slice.247), channel_id=1, source_target_pairs={{0,8},{2,10},{4,12},{6,14},{8,0},{10,2},{12,4},{14,6},{1,9},{3,11}... | collective-permute-start | bytes 319496 | tf_op jit(solution)/shard_map/ppermute | solution.py:259
  48.2 15.1 %collective-permute-start.14 = (bf16[1,2,208,128]{3,2,1,0:T(8,128)(2,1)S(1)}, bf16[1,2,208,128]{3,2,1,0:T(8,128)(2,1)S(1)}, u32[]{:S(2)}, u32[]{:S(2)}) collective-permute-start(bf16[1,2,208,128]{3,2,1,0:T(8,128)(2,1)S(1)} %slice.246), channel_id=1, source_target_pairs={{0,8},{2,10},{4,12},{6,14},{8,0},{10,2},{12,4},{14,6},{1,9},{3,11}... | collective-permute-start | bytes 319496 | tf_op jit(solution)/shard_map/ppermute | solution.py:259
  51.6 8.7 %collective-permute-start.16 = (bf16[2,1,208,128]{3,2,1,0:T(8,128)(2,1)S(1)}, bf16[2,1,208,128]{3,2,1,0:T(8,128)(2,1)S(1)}, u32[]{:S(2)}, u32[]{:S(2)}) collective-permute-start(bf16[2,1,208,128]{3,2,1,0:T(8,128)(2,1)S(1)} %get-tuple-element.136), channel_id=1, source_target_pairs={{0,2},{2,0},{4,6},{6,4},{8,10},{10,8},{12,14},{14,12},{1,3},{3,1},... | collective-permute-start | bytes 319496 | tf_op jit(solution)/shard_map/ppermute | solution.py:259
  51.8 8.5 %collective-permute-start.15 = (bf16[2,1,208,128]{3,2,1,0:T(8,128)(2,1)S(1)}, bf16[2,1,208,128]{3,2,1,0:T(8,128)(2,1)S(1)}, u32[]{:S(2)}, u32[]{:S(2)}) collective-permute-start(bf16[2,1,208,128]{3,2,1,0:T(8,128)(2,1)S(1)} %get-tuple-element.135), channel_id=1, source_target_pairs={{0,4},{2,6},{4,0},{6,2},{8,12},{10,14},{12,8},{14,10},{1,5},{3,7},... | collective-permute-start | bytes 319496 | tf_op jit(solution)/shard_map/ppermute | solution.py:259
  57.9 10.5 %collective-permute-start.20 = (bf16[2,1,16,4096]{3,2,1,0:T(8,128)(2,1)S(1)}, bf16[2,1,16,4096]{3,2,1,0:T(8,128)(2,1)S(1)}, u32[]{:S(2)}, u32[]{:S(2)}) collective-permute-start(bf16[2,1,16,4096]{3,2,1,0:T(8,128)(2,1)S(1)} %get-tuple-element.96), channel_id=1, source_target_pairs={{0,4},{2,6},{4,0},{6,2},{8,12},{10,14},{12,8},{14,10},{1,5},{3,7},... | collective-permute-start | bytes 786440 | tf_op jit(solution)/shard_map/ppermute | solution.py:259
  59.5 10.4 %collective-permute-start.13 = (bf16[2,1,16,4096]{3,2,1,0:T(8,128)(2,1)S(1)}, bf16[2,1,16,4096]{3,2,1,0:T(8,128)(2,1)S(1)}, u32[]{:S(2)}, u32[]{:S(2)}) collective-permute-start(bf16[2,1,16,4096]{3,2,1,0:T(8,128)(2,1)S(1)} %get-tuple-element.95), channel_id=1, source_target_pairs={{0,2},{2,0},{4,6},{6,4},{8,10},{10,8},{12,14},{14,12},{1,3},{3,1},... | collective-permute-start | bytes 786440 | tf_op jit(solution)/shard_map/ppermute | solution.py:259
  60.4 9.7 %collective-permute-start.21 = (bf16[1,1,208,128]{3,2,1,0:T(8,128)(2,1)S(1)}, bf16[1,1,208,128]{3,2,1,0:T(8,128)(2,1)S(1)}, u32[]{:S(2)}, u32[]{:S(2)}) collective-permute-start(bf16[1,1,208,128]{3,2,1,0:T(8,128)(2,1)S(1)} %slice.248), channel_id=1, source_target_pairs={{0,8},{2,10},{4,12},{6,14},{8,0},{10,2},{12,4},{14,6},{1,9},{3,11}... | collective-permute-start | bytes 159752 | tf_op jit(solution)/shard_map/ppermute | solution.py:259
  63.3 7.6 %collective-permute-start.19 = (bf16[1,1,208,128]{3,2,1,0:T(8,128)(2,1)S(1)}, bf16[1,1,208,128]{3,2,1,0:T(8,128)(2,1)S(1)}, u32[]{:S(2)}, u32[]{:S(2)}) collective-permute-start(bf16[1,1,208,128]{3,2,1,0:T(8,128)(2,1)S(1)} %slice.249), channel_id=1, source_target_pairs={{0,8},{2,10},{4,12},{6,14},{8,0},{10,2},{12,4},{14,6},{1,9},{3,11}... | collective-permute-start | bytes 159752 | tf_op jit(solution)/shard_map/ppermute | solution.py:259
  64.9 10.4 %collective-permute-start.22 = (bf16[2,1,16,4096]{3,2,1,0:T(8,128)(2,1)S(1)}, bf16[2,1,16,4096]{3,2,1,0:T(8,128)(2,1)S(1)}, u32[]{:S(2)}, u32[]{:S(2)}) collective-permute-start(bf16[2,1,16,4096]{3,2,1,0:T(8,128)(2,1)S(1)} %get-tuple-element.101), channel_id=1, source_target_pairs={{0,4},{2,6},{4,0},{6,2},{8,12},{10,14},{12,8},{14,10},{1,5},{3,7},... | collective-permute-start | bytes 786440 | tf_op jit(solution)/shard_map/ppermute | solution.py:259
  68.5 8.9 %collective-permute-start.18 = (bf16[2,1,16,4096]{3,2,1,0:T(8,128)(2,1)S(1)}, bf16[2,1,16,4096]{3,2,1,0:T(8,128)(2,1)S(1)}, u32[]{:S(2)}, u32[]{:S(2)}) collective-permute-start(bf16[2,1,16,4096]{3,2,1,0:T(8,128)(2,1)S(1)} %get-tuple-element.100), channel_id=1, source_target_pairs={{0,2},{2,0},{4,6},{6,4},{8,10},{10,8},{12,14},{14,12},{1,3},{3,1},... | collective-permute-start | bytes 786440 | tf_op jit(solution)/shard_map/ppermute | solution.py:259
  70.0 8.2 %collective-permute-start.17 = (bf16[1,16,4096]{2,1,0:T(8,128)(2,1)S(1)}, bf16[1,16,4096]{2,1,0:T(8,128)(2,1)S(1)}, u32[]{:S(2)}, u32[]{:S(2)}) collective-permute-start(bf16[1,16,4096]{2,1,0:T(8,128)(2,1)S(1)} %fusion.21), channel_id=1, source_target_pairs={{0,4},{2,6},{4,0},{6,2},{8,12},{10,14},{12,8},{14,10},{1,5},{3,7},... | collective-permute-start | bytes 393224 | tf_op jit(solution)/shard_map/ppermute | solution.py:259
  70.1 9.2 %collective-permute-start.23 = (bf16[1,16,4096]{2,1,0:T(8,128)(2,1)S(1)}, bf16[1,16,4096]{2,1,0:T(8,128)(2,1)S(1)}, u32[]{:S(2)}, u32[]{:S(2)}) collective-permute-start(bf16[1,16,4096]{2,1,0:T(8,128)(2,1)S(1)} %fusion.22), channel_id=1, source_target_pairs={{0,2},{2,0},{4,6},{6,4},{8,10},{10,8},{12,14},{14,12},{1,3},{3,1},... | collective-permute-start | bytes 393224 | tf_op jit(solution)/shard_map/ppermute | solution.py:259
  72.4 13.5 %collective-permute-start.29 = (bf16[2,1,16,4096]{3,2,1,0:T(8,128)(2,1)S(1)}, bf16[2,1,16,4096]{3,2,1,0:T(8,128)(2,1)S(1)}, u32[]{:S(2)}, u32[]{:S(2)}) collective-permute-start(bf16[2,1,16,4096]{3,2,1,0:T(8,128)(2,1)S(1)} %get-tuple-element.108), channel_id=1, source_target_pairs={{0,2},{2,0},{4,6},{6,4},{8,10},{10,8},{12,14},{14,12},{1,3},{3,1},... | collective-permute-start | bytes 786440 | tf_op jit(solution)/shard_map/ppermute | solution.py:259
  75.3 10.7 %collective-permute-start.30 = (bf16[2,1,16,4096]{3,2,1,0:T(8,128)(2,1)S(1)}, bf16[2,1,16,4096]{3,2,1,0:T(8,128)(2,1)S(1)}, u32[]{:S(2)}, u32[]{:S(2)}) collective-permute-start(bf16[2,1,16,4096]{3,2,1,0:T(8,128)(2,1)S(1)} %get-tuple-element.109), channel_id=1, source_target_pairs={{0,4},{2,6},{4,0},{6,2},{8,12},{10,14},{12,8},{14,10},{1,5},{3,7},... | collective-permute-start | bytes 786440 | tf_op jit(solution)/shard_map/ppermute | solution.py:259
  77.4 5.4 %collective-permute-start.25 = (bf16[1,16,4096]{2,1,0:T(8,128)(2,1)S(1)}, bf16[1,16,4096]{2,1,0:T(8,128)(2,1)S(1)}, u32[]{:S(2)}, u32[]{:S(2)}) collective-permute-start(bf16[1,16,4096]{2,1,0:T(8,128)(2,1)S(1)} %fusion.24), channel_id=1, source_target_pairs={{0,2},{2,0},{4,6},{6,4},{8,10},{10,8},{12,14},{14,12},{1,3},{3,1},... | collective-permute-start | bytes 393224 | tf_op jit(solution)/shard_map/ppermute | solution.py:259
  78.2 5.0 %collective-permute-start.26 = (bf16[1,16,4096]{2,1,0:T(8,128)(2,1)S(1)}, bf16[1,16,4096]{2,1,0:T(8,128)(2,1)S(1)}, u32[]{:S(2)}, u32[]{:S(2)}) collective-permute-start(bf16[1,16,4096]{2,1,0:T(8,128)(2,1)S(1)} %fusion.23), channel_id=1, source_target_pairs={{0,4},{2,6},{4,0},{6,2},{8,12},{10,14},{12,8},{14,10},{1,5},{3,7},... | collective-permute-start | bytes 393224 | tf_op jit(solution)/shard_map/ppermute | solution.py:259
  79.3 4.0 %collective-permute-start.24 = (f32[16,4096]{1,0:T(8,128)S(1)}, f32[16,4096]{1,0:T(8,128)S(1)}, u32[]{:S(2)}, u32[]{:S(2)}) collective-permute-start(f32[16,4096]{1,0:T(8,128)S(1)} %fusion.12), channel_id=1, source_target_pairs={{0,1},{1,0},{2,3},{3,2},{4,5},{5,4},{6,7},{7,6},{8,9},{9,8},{10,11... | collective-permute-start | bytes 786440 | tf_op jit(solution)/shard_map/ppermute | solution.py:263
  83.3 5.1 %collective-permute-start.28 = (f32[16,4096]{1,0:T(8,128)S(1)}, f32[16,4096]{1,0:T(8,128)S(1)}, u32[]{:S(2)}, u32[]{:S(2)}) collective-permute-start(f32[16,4096]{1,0:T(8,128)S(1)} %fusion.15), channel_id=1, source_target_pairs={{0,1},{1,0},{2,3},{3,2},{4,5},{5,4},{6,7},{7,6},{8,9},{9,8},{10,11... | collective-permute-start | bytes 786440 | tf_op jit(solution)/shard_map/ppermute | solution.py:263
  83.4 10.2 %collective-permute-start.27 = (bf16[16,4096]{1,0:T(8,128)(2,1)S(1)}, bf16[16,4096]{1,0:T(8,128)(2,1)S(1)}, u32[]{:S(2)}, u32[]{:S(2)}) collective-permute-start(bf16[16,4096]{1,0:T(8,128)(2,1)S(1)} %get-tuple-element.133), channel_id=1, source_target_pairs={{0,8},{2,10},{4,12},{6,14},{8,0},{10,2},{12,4},{14,6},{1,9},{3,11}... | collective-permute-start | bytes 393224 | tf_op jit(solution)/shard_map/ppermute | solution.py:259
  86.0 7.6 %collective-permute-start.32 = (bf16[1,16,4096]{2,1,0:T(8,128)(2,1)S(1)}, bf16[1,16,4096]{2,1,0:T(8,128)(2,1)S(1)}, u32[]{:S(2)}, u32[]{:S(2)}) collective-permute-start(bf16[1,16,4096]{2,1,0:T(8,128)(2,1)S(1)} %fusion.26), channel_id=1, source_target_pairs={{0,2},{2,0},{4,6},{6,4},{8,10},{10,8},{12,14},{14,12},{1,3},{3,1},... | collective-permute-start | bytes 393224 | tf_op jit(solution)/shard_map/ppermute | solution.py:259
  87.1 8.1 %collective-permute-start.33 = (bf16[1,16,4096]{2,1,0:T(8,128)(2,1)S(1)}, bf16[1,16,4096]{2,1,0:T(8,128)(2,1)S(1)}, u32[]{:S(2)}, u32[]{:S(2)}) collective-permute-start(bf16[1,16,4096]{2,1,0:T(8,128)(2,1)S(1)} %fusion.25), channel_id=1, source_target_pairs={{0,4},{2,6},{4,0},{6,2},{8,12},{10,14},{12,8},{14,10},{1,5},{3,7},... | collective-permute-start | bytes 393224 | tf_op jit(solution)/shard_map/ppermute | solution.py:259
  88.4 10.3 %collective-permute-start.31 = (bf16[16,4096]{1,0:T(8,128)(2,1)S(1)}, bf16[16,4096]{1,0:T(8,128)(2,1)S(1)}, u32[]{:S(2)}, u32[]{:S(2)}) collective-permute-start(bf16[16,4096]{1,0:T(8,128)(2,1)S(1)} %get-tuple-element.131), channel_id=1, source_target_pairs={{0,8},{2,10},{4,12},{6,14},{8,0},{10,2},{12,4},{14,6},{1,9},{3,11}... | collective-permute-start | bytes 393224 | tf_op jit(solution)/shard_map/ppermute | solution.py:259
  95.3 3.4 %collective-permute-start.34 = (f32[16,4096]{1,0:T(8,128)S(1)}, f32[16,4096]{1,0:T(8,128)S(1)}, u32[]{:S(2)}, u32[]{:S(2)}) collective-permute-start(f32[16,4096]{1,0:T(8,128)S(1)} %fusion.17), channel_id=1, source_target_pairs={{0,1},{1,0},{2,3},{3,2},{4,5},{5,4},{6,7},{7,6},{8,9},{9,8},{10,11... | collective-permute-start | bytes 786440 | tf_op jit(solution)/shard_map/ppermute | solution.py:263
  98.8 8.9 %collective-permute-start.35 = (bf16[16,4096]{1,0:T(8,128)(2,1)S(1)}, bf16[16,4096]{1,0:T(8,128)(2,1)S(1)}, u32[]{:S(2)}, u32[]{:S(2)}) collective-permute-start(bf16[16,4096]{1,0:T(8,128)(2,1)S(1)} %get-tuple-element.129), channel_id=1, source_target_pairs={{0,8},{2,10},{4,12},{6,14},{8,0},{10,2},{12,4},{14,6},{1,9},{3,11}... | collective-permute-start | bytes 393224 | tf_op jit(solution)/shard_map/ppermute | solution.py:259

commit v4 on v3

--- a/solution.py
+++ b/solution.py
@@ -11,8 +11,8 @@
 QUAD = 4
 
 
-ORDERS = [(((0, 1),), ((0, 1), (1, 0))), (((1, 0),), ((0, 1), (1, 0))), (((0, 1), (1, 0)), ((0, 1), (1, 0)))]
-TURNS = [0, 1, 0, 1, 2, 0, 1, 2, 0, 2, 1, 0, 2, 1, 0, 1, 0, 2, 1, 0, 2, 1, 2, 2]
+ORDERS = [(((0, 1), (1, 0)), ((0, 1), (1, 0))), (((0, 1), (1, 0)), ((0, 1), (1, 0))), (((0, 1), (1, 0)), ((0, 1), (1, 0)))]
+TURNS = [0, 1, 0, 1, 2, 0, 1, 2, 0, 1, 2, 0, 1, 2, 0, 1, 0, 2, 1, 0, 2, 1, 2, 2]
 
 
 def wire_type(stage, stages):

time: 109 us -> 105 us (0.963)
  waiting for transfers between devices: 44.3 us -> 28.7 us
  starting transfers between devices: 43.9 us -> 55.7 us
    ppermute x27 -> x33, waiting for transfers between devices: 40.5 us -> 24 us  [swap(): return lax.ppermute(value, 'gx', [(i, i ^ 1 << bit) for i in range(count)])]
    ppermute x27 -> x33, starting transfers between devices: 29.8 us -> 44.1 us  [swap(): return lax.ppermute(value, 'gx', [(i, i ^ 1 << bit) for i in range(count)])]
    ppermute x5, starting transfers between devices: 7.92 us -> 5.39 us  [swap_cores(): return lax.ppermute(value, 'gy', [(0, 1), (1, 0)])]
  transfers between devices with their start and end apart: 36 -> 42, of which waited for: 13 -> 13; matrix products, arithmetic and copies ran while one was open for 1% -> 1% of each run, Pallas kernels for 15% -> 9%
where the time goes in v4:
time: 105 us
  starting transfers between devices  55.7 us (53%)
  waiting for transfers between devices  28.7 us (27%)
  Pallas kernels  16.4 us (16%)
  other arithmetic  2.12 us (2%)
  local copies, waits for them, and re-layouts  1.29 us (1%)
    ppermute x33, starting transfers between devices, swap(): return lax.ppermute(value, 'gx', [(i, i ^ 1 << bit) for i in range(count)])  44.1 us
    ppermute x33, waiting for transfers between devices, swap(): return lax.ppermute(value, 'gx', [(i, i ^ 1 << bit) for i in range(count)])  24 us
    pallas_call x6, Pallas kernels, down_project(): pl.pallas_call(functools.partial(down_kernel, block, count, order), out_s...  8.88 us
    pallas_call x1, Pallas kernels, project(): pl.pallas_call(functools.partial(project_kernel, block, cuts, len(arrived...  7 us
    ppermute x4, starting transfers between devices, move(): lax.ppermute(value, ('gx', 'gy'), [(2 * a + b, 2 * c + d) for (a, b), (c,...  6.22 us
    ppermute x5, starting transfers between devices, swap_cores(): return lax.ppermute(value, 'gy', [(0, 1), (1, 0)])  5.39 us
    ppermute x4, waiting for transfers between devices, move(): lax.ppermute(value, ('gx', 'gy'), [(2 * a + b, 2 * c + d) for (a, b), (c,...  3.74 us
  transfers between devices with their start and end apart: 42, of which 13 were waited for; matrix products, arithmetic and copies ran while one was open for 1% of the time, Pallas kernels for 9%

profile of v4, /device:TPU:0, one launch (start us, length us, event | category | flops | bytes accessed | tf_op | source)
XLA Modules:
  0.0 104.7 jit_solution(1229926474081359553)
XLA Ops:
  0.0 0.5 collective-permute-start.4
  0.5 0.1 pad_add_fusion.place_ref
  0.5 1.0 copy-done.1
  1.5 0.6 shard_map.37
  2.1 0.7 collective-permute-start
  2.8 2.5 %collective-permute-start.1 = (bf16[48,1024]{1,0:T(8,128)(2,1)S(1)}, bf16[48,1024]{1,0:T(8,128)(2,1)S(1)}, u32[]{:S(2)}, u32[]{:S(2)}) collective-permute-start(bf16[48,1024]{1,0:T(8,128)(2,1)S(1)} %get-tuple-element.83), channel_id=1, source_target_pairs={{0,2},{1,10},{2,4},{3,12},{4,6},{5,14},{6,0},{7,8},{8,3},{9,11},{1... | collective-permute-start | bytes 294920 | tf_op jit(solution)/shard_map/ppermute | solution.py:287
  5.3 1.6 %collective-permute-start.2 = (bf16[48,1024]{1,0:T(8,128)(2,1)S(1)}, bf16[48,1024]{1,0:T(8,128)(2,1)S(1)}, u32[]{:S(2)}, u32[]{:S(2)}) collective-permute-start(bf16[48,1024]{1,0:T(8,128)(2,1)S(1)} %get-tuple-element.84), channel_id=1, source_target_pairs={{0,4},{1,12},{2,6},{3,14},{4,0},{5,8},{6,2},{7,10},{8,5},{9,13},{1... | collective-permute-start | bytes 294920 | tf_op jit(solution)/shard_map/ppermute | solution.py:287
  6.9 1.4 %collective-permute-start.3 = (bf16[48,1024]{1,0:T(8,128)(2,1)S(1)}, bf16[48,1024]{1,0:T(8,128)(2,1)S(1)}, u32[]{:S(2)}, u32[]{:S(2)}) collective-permute-start(bf16[48,1024]{1,0:T(8,128)(2,1)S(1)} %get-tuple-element.85), channel_id=1, source_target_pairs={{0,6},{1,14},{2,0},{3,8},{4,2},{5,10},{6,4},{7,12},{8,7},{9,15},{1... | collective-permute-start | bytes 294920 | tf_op jit(solution)/shard_map/ppermute | solution.py:287
  8.3 0.6 collective-permute-done.1.refs_1_
  8.9 2.1 %collective-permute-done.2.refs_2_ = bf16[48,1024]{1,0:T(8,128)(2,1)S(1)} collective-permute-done((bf16[48,1024]{1,0:T(8,128)(2,1)S(1)}, bf16[48,1024]{1,0:T(8,128)(2,1)S(1)}, u32[]{:S(2)}, u32[]{:S(2)}) %collective-permute-start.2) | collective-permute-done | bytes 98336 | tf_op jit(solution)/shard_map/ppermute | solution.py:287
  11.0 1.1 %collective-permute-done.3.refs_3_ = bf16[48,1024]{1,0:T(8,128)(2,1)S(1)} collective-permute-done((bf16[48,1024]{1,0:T(8,128)(2,1)S(1)}, bf16[48,1024]{1,0:T(8,128)(2,1)S(1)}, u32[]{:S(2)}, u32[]{:S(2)}) %collective-permute-start.3) | collective-permute-done | bytes 98336 | tf_op jit(solution)/shard_map/ppermute | solution.py:287
  12.1 7.0 %shard_map.38 = (bf16[2,2,1,208,128]{4,3,2,1,0:T(8,128)(2,1)S(1)}, f32[2,2,1,208,128]{4,3,2,1,0:T(8,128)S(1)}, bf16[2,2,1,208,128]{4,3,2,1,0:T(8,128)(2,1)S(1)},...) custom-call(s32[2]{0:T(128)S(1)} %pad_add_fusion.place_ref, ...), custom_call_target="tpu_custom_call" | custom-call | flops 1308622848 | bytes 6815744 | tf_op jit(solution)/shard_map/pallas_call | solution.py:148
  19.1 2.3 %collective-permute-start.9 = (bf16[2,2,1,208,128]{4,3,1,2,0:T(8,128)(2,1)S(1)}, bf16[2,2,1,208,128]{4,3,1,2,0:T(8,128)(2,1)S(1)}, u32[]{:S(2)}, u32[]{:S(2)}) collective-permute-start(bf16[2,2,1,208,128]{4,3,1,2,0:T(8,128)(2,1)S(1)} %bitcast.207), channel_id=1, source_target_pairs={{0,4},{2,6},{4,0},{6,2},{8,12},{10,14},{12,8},{14,10},{1,5},{3,7},... | collective-permute-start | bytes 638984 | tf_op jit(solution)/shard_map/ppermute | solution.py:259
  21.3 1.9 %collective-permute-start.5 = (bf16[2,2,1,208,128]{4,3,1,2,0:T(8,128)(2,1)S(1)}, bf16[2,2,1,208,128]{4,3,1,2,0:T(8,128)(2,1)S(1)}, u32[]{:S(2)}, u32[]{:S(2)}) collective-permute-start(bf16[2,2,1,208,128]{4,3,1,2,0:T(8,128)(2,1)S(1)} %bitcast.206), channel_id=1, source_target_pairs={{0,2},{2,0},{4,6},{6,4},{8,10},{10,8},{12,14},{14,12},{1,3},{3,1},... | collective-permute-start | bytes 638984 | tf_op jit(solution)/shard_map/ppermute | solution.py:259
  23.2 4.3 %collective-permute-start.17 = (bf16[208,8192]{1,0:T(8,128)(2,1)S(1)}, bf16[208,8192]{1,0:T(8,128)(2,1)S(1)}, u32[]{:S(2)}, u32[]{:S(2)}) collective-permute-start(bf16[208,8192]{1,0:T(8,128)(2,1)S(1)} %copy-done), channel_id=1, source_target_pairs={{0,1},{1,0},{2,3},{3,2},{4,5},{5,4},{6,7},{7,6},{8,9},{9,8},{10,11... | collective-permute-start | bytes 10223624 | tf_op jit(solution)/shard_map/ppermute | solution.py:263
  27.5 0.7 collective-permute-start.10
  28.2 1.7 %collective-permute-start.8 = (bf16[2,2,1,208,128]{4,3,1,2,0:T(8,128)(2,1)S(1)}, bf16[2,2,1,208,128]{4,3,1,2,0:T(8,128)(2,1)S(1)}, u32[]{:S(2)}, u32[]{:S(2)}) collective-permute-start(bf16[2,2,1,208,128]{4,3,1,2,0:T(8,128)(2,1)S(1)} %bitcast.204), channel_id=1, source_target_pairs={{0,2},{2,0},{4,6},{6,4},{8,10},{10,8},{12,14},{14,12},{1,3},{3,1},... | collective-permute-start | bytes 638984 | tf_op jit(solution)/shard_map/ppermute | solution.py:259
  30.0 0.4 collective-permute-start.13
  30.4 1.3 %collective-permute-start.6 = (bf16[2,1,208,128]{3,2,1,0:T(8,128)(2,1)S(1)}, bf16[2,1,208,128]{3,2,1,0:T(8,128)(2,1)S(1)}, u32[]{:S(2)}, u32[]{:S(2)}) collective-permute-start(bf16[2,1,208,128]{3,2,1,0:T(8,128)(2,1)S(1)} %get-tuple-element.157), channel_id=1, source_target_pairs={{0,4},{2,6},{4,0},{6,2},{8,12},{10,14},{12,8},{14,10},{1,5},{3,7},... | collective-permute-start | bytes 319496 | tf_op jit(solution)/shard_map/ppermute | solution.py:259
  31.7 3.9 %collective-permute-done.10 = bf16[2,2,1,208,128]{4,3,1,2,0:T(8,128)(2,1)S(1)} collective-permute-done((bf16[2,2,1,208,128]{4,3,1,2,0:T(8,128)(2,1)S(1)}, bf16[2,2,1,208,128]{4,3,1,2,0:T(8,128)(2,1)S(1)}, u32[]{:S(2)}, u32[]{:S(2)}) %collective-permute-start.10) | collective-permute-done | bytes 213024 | tf_op jit(solution)/shard_map/ppermute | solution.py:259
  35.7 0.6 collective-permute-done.8
  36.4 1.8 %collective-permute-start.14 = (bf16[2,1,208,128]{3,2,1,0:T(8,128)(2,1)S(1)}, bf16[2,1,208,128]{3,2,1,0:T(8,128)(2,1)S(1)}, u32[]{:S(2)}, u32[]{:S(2)}) collective-permute-start(bf16[2,1,208,128]{3,2,1,0:T(8,128)(2,1)S(1)} %fusion.30), channel_id=1, source_target_pairs={{0,2},{2,0},{4,6},{6,4},{8,10},{10,8},{12,14},{14,12},{1,3},{3,1},... | collective-permute-start | bytes 319496 | tf_op jit(solution)/shard_map/ppermute | solution.py:259
  38.2 0.4 collective-permute-start.12
  38.6 1.7 %collective-permute-start.15 = (bf16[2,2,1,208,128]{4,3,1,2,0:T(8,128)(2,1)S(1)}, bf16[2,2,1,208,128]{4,3,1,2,0:T(8,128)(2,1)S(1)}, u32[]{:S(2)}, u32[]{:S(2)}) collective-permute-start(bf16[2,2,1,208,128]{4,3,1,2,0:T(8,128)(2,1)S(1)} %bitcast.203), channel_id=1, source_target_pairs={{0,4},{2,6},{4,0},{6,2},{8,12},{10,14},{12,8},{14,10},{1,5},{3,7},... | collective-permute-start | bytes 638984 | tf_op jit(solution)/shard_map/ppermute | solution.py:259
  40.3 0.3 collective-permute-start.11
  40.6 0.6 collective-permute-done.14
  41.2 6.0 %collective-permute-start.16 = (bf16[1,1,208,128]{3,2,1,0:T(8,128)(2,1)S(1)}, bf16[1,1,208,128]{3,2,1,0:T(8,128)(2,1)S(1)}, u32[]{:S(2)}, u32[]{:S(2)}) collective-permute-start(bf16[1,1,208,128]{3,2,1,0:T(8,128)(2,1)S(1)} %slice.310), channel_id=1, source_target_pairs={{0,8},{2,10},{4,12},{6,14},{8,0},{10,2},{12,4},{14,6},{1,9},{3,11}... | collective-permute-start | bytes 159752 | tf_op jit(solution)/shard_map/ppermute | solution.py:259
  47.4 3.0 %collective-permute-start.21 = (bf16[1,1,208,128]{3,2,1,0:T(8,128)(2,1)S(1)}, bf16[1,1,208,128]{3,2,1,0:T(8,128)(2,1)S(1)}, u32[]{:S(2)}, u32[]{:S(2)}) collective-permute-start(bf16[1,1,208,128]{3,2,1,0:T(8,128)(2,1)S(1)} %slice.308), channel_id=1, source_target_pairs={{0,8},{2,10},{4,12},{6,14},{8,0},{10,2},{12,4},{14,6},{1,9},{3,11}... | collective-permute-start | bytes 159752 | tf_op jit(solution)/shard_map/ppermute | solution.py:259
  50.4 0.1 collective-permute-start.20
  50.6 1.9 %collective-permute-start.22 = (bf16[2,1,208,128]{3,2,1,0:T(8,128)(2,1)S(1)}, bf16[2,1,208,128]{3,2,1,0:T(8,128)(2,1)S(1)}, u32[]{:S(2)}, u32[]{:S(2)}) collective-permute-start(bf16[2,1,208,128]{3,2,1,0:T(8,128)(2,1)S(1)} %fusion.32), channel_id=1, source_target_pairs={{0,2},{2,0},{4,6},{6,4},{8,10},{10,8},{12,14},{14,12},{1,3},{3,1},... | collective-permute-start | bytes 319496 | tf_op jit(solution)/shard_map/ppermute | solution.py:259
  52.6 0.8 collective-permute-done.7
  53.3 0.1 collective-permute-start.19
  53.4 1.5 %shard_map.40 = (bf16[2,1,16,4096]{3,2,1,0:T(8,128)(2,1)S(1)}, f32[2,1,16,4096]{3,2,1,0:T(8,128)S(1)}) custom-call(s32[2]{0:T(128)S(1)} %pad_add_fusion.place_ref, f32[1,208,128]{2,1,0:T(8,128)S(1)} %slice_bitcast_fusion.17.refs_0_, bf16[1,208,128]{2,1,0:T(8,128)(2,1)S(1)} %bitcast.198, f32[1,208,128]{2,1,0:T(8,128)S(1)} %slice_bitcast_fusion.16.refs_2_, ...), custom_call_target="tpu_custom_call" | custom-call | flops 218103808 | bytes 3407872 | tf_op jit(solution)/shard_map/pallas_call | solution.py:231
  54.9 2.0 %collective-permute-start.26 = (bf16[2,1,16,4096]{3,2,1,0:T(8,128)(2,1)S(1)}, bf16[2,1,16,4096]{3,2,1,0:T(8,128)(2,1)S(1)}, u32[]{:S(2)}, u32[]{:S(2)}) collective-permute-start(bf16[2,1,16,4096]{3,2,1,0:T(8,128)(2,1)S(1)} %get-tuple-element.117), channel_id=1, source_target_pairs={{0,4},{2,6},{4,0},{6,2},{8,12},{10,14},{12,8},{14,10},{1,5},{3,7},... | collective-permute-start | bytes 786440 | tf_op jit(solution)/shard_map/ppermute | solution.py:259
  56.9 1.5 %shard_map.39 = (bf16[2,1,16,4096]{3,2,1,0:T(8,128)(2,1)S(1)}, f32[2,1,16,4096]{3,2,1,0:T(8,128)S(1)}) custom-call(s32[2]{0:T(128)S(1)} %pad_add_fusion.place_ref, f32[1,208,128]{2,1,0:T(8,128)S(1)} %slice_bitcast_fusion.17.refs_0_, bf16[1,208,128]{2,1,0:T(8,128)(2,1)S(1)} %bitcast.199, f32[1,208,128]{2,1,0:T(8,128)S(1)} %slice_bitcast_fusion.16.refs_2_, ...), custom_call_target="tpu_custom_call" | custom-call | flops 218103808 | bytes 3407872 | tf_op jit(solution)/shard_map/pallas_call | solution.py:231
  58.4 1.0 collective-permute-start.18
  59.5 1.5 %shard_map.42 = (bf16[2,1,16,4096]{3,2,1,0:T(8,128)(2,1)S(1)}, f32[2,1,16,4096]{3,2,1,0:T(8,128)S(1)}) custom-call(s32[2]{0:T(128)S(1)} %pad_add_fusion.place_ref, f32[1,208,128]{2,1,0:T(8,128)S(1)} %slice_bitcast_fusion.15.refs_0_, bf16[1,208,128]{2,1,0:T(8,128)(2,1)S(1)} %bitcast.200, f32[1,208,128]{2,1,0:T(8,128)S(1)} %slice_bitcast_fusion.14.refs_2_, ...), custom_call_target="tpu_custom_call" | custom-call | flops 218103808 | bytes 3407872 | tf_op jit(solution)/shard_map/pallas_call | solution.py:231
  61.0 0.2 collective-permute-start.27
  61.2 1.5 %shard_map.41 = (bf16[2,1,16,4096]{3,2,1,0:T(8,128)(2,1)S(1)}, f32[2,1,16,4096]{3,2,1,0:T(8,128)S(1)}) custom-call(s32[2]{0:T(128)S(1)} %pad_add_fusion.place_ref, f32[1,208,128]{2,1,0:T(8,128)S(1)} %slice_bitcast_fusion.15.refs_0_, bf16[1,208,128]{2,1,0:T(8,128)(2,1)S(1)} %bitcast.201, f32[1,208,128]{2,1,0:T(8,128)S(1)} %slice_bitcast_fusion.14.refs_2_, ...), custom_call_target="tpu_custom_call" | custom-call | flops 218103808 | bytes 3407872 | tf_op jit(solution)/shard_map/pallas_call | solution.py:231
  62.7 1.1 %collective-permute-start.25 = (bf16[2,1,16,4096]{3,2,1,0:T(8,128)(2,1)S(1)}, bf16[2,1,16,4096]{3,2,1,0:T(8,128)(2,1)S(1)}, u32[]{:S(2)}, u32[]{:S(2)}) collective-permute-start(bf16[2,1,16,4096]{3,2,1,0:T(8,128)(2,1)S(1)} %get-tuple-element.120), channel_id=1, source_target_pairs={{0,2},{2,0},{4,6},{6,4},{8,10},{10,8},{12,14},{14,12},{1,3},{3,1},... | collective-permute-start | bytes 786440 | tf_op jit(solution)/shard_map/ppermute | solution.py:259
  63.9 2.6 %collective-permute-start.28 = (bf16[1,1,208,128]{3,2,1,0:T(8,128)(2,1)S(1)}, bf16[1,1,208,128]{3,2,1,0:T(8,128)(2,1)S(1)}, u32[]{:S(2)}, u32[]{:S(2)}) collective-permute-start(bf16[1,1,208,128]{3,2,1,0:T(8,128)(2,1)S(1)} %slice.306), channel_id=1, source_target_pairs={{0,8},{2,10},{4,12},{6,14},{8,0},{10,2},{12,4},{14,6},{1,9},{3,11}... | collective-permute-start | bytes 159752 | tf_op jit(solution)/shard_map/ppermute | solution.py:259
  66.5 0.4 collective-permute-start.24
  67.1 2.4 %collective-permute-start.23 = (bf16[1,16,4096]{2,1,0:T(8,128)(2,1)S(1)}, bf16[1,16,4096]{2,1,0:T(8,128)(2,1)S(1)}, u32[]{:S(2)}, u32[]{:S(2)}) collective-permute-start(bf16[1,16,4096]{2,1,0:T(8,128)(2,1)S(1)} %fusion.21), channel_id=1, source_target_pairs={{0,4},{2,6},{4,0},{6,2},{8,12},{10,14},{12,8},{14,10},{1,5},{3,7},... | collective-permute-start | bytes 393224 | tf_op jit(solution)/shard_map/ppermute | solution.py:259
  69.6 1.6 %collective-permute-done.27 = bf16[2,1,16,4096]{3,2,1,0:T(8,128)(2,1)S(1)} collective-permute-done((bf16[2,1,16,4096]{3,2,1,0:T(8,128)(2,1)S(1)}, bf16[2,1,16,4096]{3,2,1,0:T(8,128)(2,1)S(1)}, u32[]{:S(2)}, u32[]{:S(2)}) %collective-permute-start.27) | collective-permute-done | bytes 262176 | tf_op jit(solution)/shard_map/ppermute | solution.py:259
  71.1 1.0 collective-permute-start.29
  72.3 1.1 %collective-permute-start.31 = (bf16[1,16,4096]{2,1,0:T(8,128)(2,1)S(1)}, bf16[1,16,4096]{2,1,0:T(8,128)(2,1)S(1)}, u32[]{:S(2)}, u32[]{:S(2)}) collective-permute-start(bf16[1,16,4096]{2,1,0:T(8,128)(2,1)S(1)} %fusion.24), channel_id=1, source_target_pairs={{0,2},{2,0},{4,6},{6,4},{8,10},{10,8},{12,14},{14,12},{1,3},{3,1},... | collective-permute-start | bytes 393224 | tf_op jit(solution)/shard_map/ppermute | solution.py:259
  73.4 0.9 collective-permute-start.32
  74.3 1.5 %shard_map.43 = (bf16[2,1,16,4096]{3,2,1,0:T(8,128)(2,1)S(1)}, f32[2,1,16,4096]{3,2,1,0:T(8,128)S(1)}) custom-call(s32[2]{0:T(128)S(1)} %pad_add_fusion.place_ref, f32[1,208,128]{2,1,0:T(8,128)S(1)} %slice_bitcast_fusion.13.refs_0_, bf16[1,208,128]{2,1,0:T(8,128)(2,1)S(1)} %bitcast.196, f32[1,208,128]{2,1,0:T(8,128)S(1)} %slice_bitcast_fusion.12.refs_2_, ...), custom_call_target="tpu_custom_call" | custom-call | flops 218103808 | bytes 3407872 | tf_op jit(solution)/shard_map/pallas_call | solution.py:231
  75.8 1.7 %collective-permute-start.35 = (bf16[2,1,16,4096]{3,2,1,0:T(8,128)(2,1)S(1)}, bf16[2,1,16,4096]{3,2,1,0:T(8,128)(2,1)S(1)}, u32[]{:S(2)}, u32[]{:S(2)}) collective-permute-start(bf16[2,1,16,4096]{3,2,1,0:T(8,128)(2,1)S(1)} %get-tuple-element.133), channel_id=1, source_target_pairs={{0,2},{2,0},{4,6},{6,4},{8,10},{10,8},{12,14},{14,12},{1,3},{3,1},... | collective-permute-start | bytes 786440 | tf_op jit(solution)/shard_map/ppermute | solution.py:259
  77.5 1.5 %shard_map.44 = (bf16[2,1,16,4096]{3,2,1,0:T(8,128)(2,1)S(1)}, f32[2,1,16,4096]{3,2,1,0:T(8,128)S(1)}) custom-call(s32[2]{0:T(128)S(1)} %pad_add_fusion.place_ref, f32[1,208,128]{2,1,0:T(8,128)S(1)} %slice_bitcast_fusion.13.refs_0_, bf16[1,208,128]{2,1,0:T(8,128)(2,1)S(1)} %bitcast.197, f32[1,208,128]{2,1,0:T(8,128)S(1)} %slice_bitcast_fusion.12.refs_2_, ...), custom_call_target="tpu_custom_call" | custom-call | flops 218103808 | bytes 3407872 | tf_op jit(solution)/shard_map/pallas_call | solution.py:231
  79.0 0.5 collective-permute-start.36
  79.7 0.5 collective-permute-start.34
  80.3 0.9 collective-permute-done.30
  81.2 1.3 %collective-permute-start.33 = (bf16[16,4096]{1,0:T(8,128)(2,1)S(1)}, bf16[16,4096]{1,0:T(8,128)(2,1)S(1)}, u32[]{:S(2)}, u32[]{:S(2)}) collective-permute-start(bf16[16,4096]{1,0:T(8,128)(2,1)S(1)} %get-tuple-element.155), channel_id=1, source_target_pairs={{0,8},{2,10},{4,12},{6,14},{8,0},{10,2},{12,4},{14,6},{1,9},{3,11}... | collective-permute-start | bytes 393224 | tf_op jit(solution)/shard_map/ppermute | solution.py:259
  82.6 4.0 %collective-permute-done.36 = bf16[2,1,16,4096]{3,2,1,0:T(8,128)(2,1)S(1)} collective-permute-done((bf16[2,1,16,4096]{3,2,1,0:T(8,128)(2,1)S(1)}, bf16[2,1,16,4096]{3,2,1,0:T(8,128)(2,1)S(1)}, u32[]{:S(2)}, u32[]{:S(2)}) %collective-permute-start.36) | collective-permute-done | bytes 262176 | tf_op jit(solution)/shard_map/ppermute | solution.py:259
  86.8 0.4 collective-permute-start.39
  87.2 0.1 select_convert_fusion.1
  87.3 3.0 %collective-permute-start.37 = (bf16[16,4096]{1,0:T(8,128)(2,1)S(1)}, bf16[16,4096]{1,0:T(8,128)(2,1)S(1)}, u32[]{:S(2)}, u32[]{:S(2)}) collective-permute-start(bf16[16,4096]{1,0:T(8,128)(2,1)S(1)} %get-tuple-element.153), channel_id=1, source_target_pairs={{0,8},{2,10},{4,12},{6,14},{8,0},{10,2},{12,4},{14,6},{1,9},{3,11}... | collective-permute-start | bytes 393224 | tf_op jit(solution)/shard_map/ppermute | solution.py:259
  90.4 2.5 %collective-permute-done.33 = bf16[16,4096]{1,0:T(8,128)(2,1)S(1)} collective-permute-done((bf16[16,4096]{1,0:T(8,128)(2,1)S(1)}, bf16[16,4096]{1,0:T(8,128)(2,1)S(1)}, u32[]{:S(2)}, u32[]{:S(2)}) %collective-permute-start.33) | collective-permute-done | bytes 131104 | tf_op jit(solution)/shard_map/ppermute | solution.py:259
  93.0 3.2 %collective-permute-done.37 = bf16[16,4096]{1,0:T(8,128)(2,1)S(1)} collective-permute-done((bf16[16,4096]{1,0:T(8,128)(2,1)S(1)}, bf16[16,4096]{1,0:T(8,128)(2,1)S(1)}, u32[]{:S(2)}, u32[]{:S(2)}) %collective-permute-start.37) | collective-permute-done | bytes 131104 | tf_op jit(solution)/shard_map/ppermute | solution.py:259
  96.2 0.1 select_convert_fusion
  96.3 0.7 collective-permute-start.41
  97.0 6.9 %collective-permute-done.41 = bf16[16,4096]{1,0:T(8,128)(2,1)S(1)} collective-permute-done((bf16[16,4096]{1,0:T(8,128)(2,1)S(1)}, bf16[16,4096]{1,0:T(8,128)(2,1)S(1)}, u32[]{:S(2)}, u32[]{:S(2)}) %collective-permute-start.41) | collective-permute-done | bytes 131104 | tf_op jit(solution)/shard_map/ppermute | solution.py:259
  103.9 0.8 pad_maximum_fusion
  (84 shorter events, 1.8 us)
Async XLA Ops:
  0.0 12.1 %collective-permute-start.4 = (bf16[2,512,3328]{2,1,0:T(8,128)(2,1)}, bf16[2,512,3328]{2,1,0:T(8,128)(2,1)}, u32[]{:S(2)}, u32[]{:S(2)}) collective-permute-start(bf16[2,512,3328]{2,1,0:T(8,128)(2,1)} %refs_4_.7), channel_id=1, source_target_pairs={{0,1},{1,0},{2,3},{3,2},{4,5},{5,4},{6,7},{7,6},{8,9},{9,8},{10,11... | collective-permute-start | bytes 20447240 | tf_op jit(solution)/shard_map/ppermute | solution.py:263
  0.5 1.0 copy-start.1
  2.1 6.2 %collective-permute-start = (bf16[48,1024]{1,0:T(8,128)(2,1)S(1)}, bf16[48,1024]{1,0:T(8,128)(2,1)S(1)}, u32[]{:S(2)}, u32[]{:S(2)}) collective-permute-start(bf16[48,1024]{1,0:T(8,128)(2,1)S(1)} %get-tuple-element.82), channel_id=1, source_target_pairs={{0,0},{1,8},{2,2},{3,10},{4,4},{5,12},{6,6},{7,14},{8,1},{9,9},{10... | collective-permute-start | bytes 294920 | tf_op jit(solution)/shard_map/ppermute | solution.py:287
  2.8 6.2 %collective-permute-start.1 = (bf16[48,1024]{1,0:T(8,128)(2,1)S(1)}, bf16[48,1024]{1,0:T(8,128)(2,1)S(1)}, u32[]{:S(2)}, u32[]{:S(2)}) collective-permute-start(bf16[48,1024]{1,0:T(8,128)(2,1)S(1)} %get-tuple-element.83), channel_id=1, source_target_pairs={{0,2},{1,10},{2,4},{3,12},{4,6},{5,14},{6,0},{7,8},{8,3},{9,11},{1... | collective-permute-start | bytes 294920 | tf_op jit(solution)/shard_map/ppermute | solution.py:287
  5.3 5.7 %collective-permute-start.2 = (bf16[48,1024]{1,0:T(8,128)(2,1)S(1)}, bf16[48,1024]{1,0:T(8,128)(2,1)S(1)}, u32[]{:S(2)}, u32[]{:S(2)}) collective-permute-start(bf16[48,1024]{1,0:T(8,128)(2,1)S(1)} %get-tuple-element.84), channel_id=1, source_target_pairs={{0,4},{1,12},{2,6},{3,14},{4,0},{5,8},{6,2},{7,10},{8,5},{9,13},{1... | collective-permute-start | bytes 294920 | tf_op jit(solution)/shard_map/ppermute | solution.py:287
  6.9 16.3 %copy-start = (bf16[208,8192]{1,0:T(8,128)(2,1)S(1)}, bf16[208,8192]{1,0:T(8,128)(2,1)}, u32[]{:S(2)}) copy-start(bf16[208,8192]{1,0:T(8,128)(2,1)} %refs_4_.13) | copy-start | bytes 10223620
  6.9 5.2 %collective-permute-start.3 = (bf16[48,1024]{1,0:T(8,128)(2,1)S(1)}, bf16[48,1024]{1,0:T(8,128)(2,1)S(1)}, u32[]{:S(2)}, u32[]{:S(2)}) collective-permute-start(bf16[48,1024]{1,0:T(8,128)(2,1)S(1)} %get-tuple-element.85), channel_id=1, source_target_pairs={{0,6},{1,14},{2,0},{3,8},{4,2},{5,10},{6,4},{7,12},{8,7},{9,15},{1... | collective-permute-start | bytes 294920 | tf_op jit(solution)/shard_map/ppermute | solution.py:287
  19.1 10.8 %collective-permute-start.9 = (bf16[2,2,1,208,128]{4,3,1,2,0:T(8,128)(2,1)S(1)}, bf16[2,2,1,208,128]{4,3,1,2,0:T(8,128)(2,1)S(1)}, u32[]{:S(2)}, u32[]{:S(2)}) collective-permute-start(bf16[2,2,1,208,128]{4,3,1,2,0:T(8,128)(2,1)S(1)} %bitcast.207), channel_id=1, source_target_pairs={{0,4},{2,6},{4,0},{6,2},{8,12},{10,14},{12,8},{14,10},{1,5},{3,7},... | collective-permute-start | bytes 638984 | tf_op jit(solution)/shard_map/ppermute | solution.py:259
  21.3 8.6 %collective-permute-start.5 = (bf16[2,2,1,208,128]{4,3,1,2,0:T(8,128)(2,1)S(1)}, bf16[2,2,1,208,128]{4,3,1,2,0:T(8,128)(2,1)S(1)}, u32[]{:S(2)}, u32[]{:S(2)}) collective-permute-start(bf16[2,2,1,208,128]{4,3,1,2,0:T(8,128)(2,1)S(1)} %bitcast.206), channel_id=1, source_target_pairs={{0,2},{2,0},{4,6},{6,4},{8,10},{10,8},{12,14},{14,12},{1,3},{3,1},... | collective-permute-start | bytes 638984 | tf_op jit(solution)/shard_map/ppermute | solution.py:259
  23.2 30.2 %collective-permute-start.17 = (bf16[208,8192]{1,0:T(8,128)(2,1)S(1)}, bf16[208,8192]{1,0:T(8,128)(2,1)S(1)}, u32[]{:S(2)}, u32[]{:S(2)}) collective-permute-start(bf16[208,8192]{1,0:T(8,128)(2,1)S(1)} %copy-done), channel_id=1, source_target_pairs={{0,1},{1,0},{2,3},{3,2},{4,5},{5,4},{6,7},{7,6},{8,9},{9,8},{10,11... | collective-permute-start | bytes 10223624 | tf_op jit(solution)/shard_map/ppermute | solution.py:263
  27.5 8.2 %collective-permute-start.10 = (bf16[2,2,1,208,128]{4,3,1,2,0:T(8,128)(2,1)S(1)}, bf16[2,2,1,208,128]{4,3,1,2,0:T(8,128)(2,1)S(1)}, u32[]{:S(2)}, u32[]{:S(2)}) collective-permute-start(bf16[2,2,1,208,128]{4,3,1,2,0:T(8,128)(2,1)S(1)} %bitcast.205), channel_id=1, source_target_pairs={{0,4},{2,6},{4,0},{6,2},{8,12},{10,14},{12,8},{14,10},{1,5},{3,7},... | collective-permute-start | bytes 638984 | tf_op jit(solution)/shard_map/ppermute | solution.py:259
  28.2 8.2 %collective-permute-start.8 = (bf16[2,2,1,208,128]{4,3,1,2,0:T(8,128)(2,1)S(1)}, bf16[2,2,1,208,128]{4,3,1,2,0:T(8,128)(2,1)S(1)}, u32[]{:S(2)}, u32[]{:S(2)}) collective-permute-start(bf16[2,2,1,208,128]{4,3,1,2,0:T(8,128)(2,1)S(1)} %bitcast.204), channel_id=1, source_target_pairs={{0,2},{2,0},{4,6},{6,4},{8,10},{10,8},{12,14},{14,12},{1,3},{3,1},... | collective-permute-start | bytes 638984 | tf_op jit(solution)/shard_map/ppermute | solution.py:259
  30.0 8.6 %collective-permute-start.13 = (bf16[2,1,208,128]{3,2,1,0:T(8,128)(2,1)S(1)}, bf16[2,1,208,128]{3,2,1,0:T(8,128)(2,1)S(1)}, u32[]{:S(2)}, u32[]{:S(2)}) collective-permute-start(bf16[2,1,208,128]{3,2,1,0:T(8,128)(2,1)S(1)} %get-tuple-element.158), channel_id=1, source_target_pairs={{0,2},{2,0},{4,6},{6,4},{8,10},{10,8},{12,14},{14,12},{1,3},{3,1},... | collective-permute-start | bytes 319496 | tf_op jit(solution)/shard_map/ppermute | solution.py:259
  30.4 9.9 %collective-permute-start.6 = (bf16[2,1,208,128]{3,2,1,0:T(8,128)(2,1)S(1)}, bf16[2,1,208,128]{3,2,1,0:T(8,128)(2,1)S(1)}, u32[]{:S(2)}, u32[]{:S(2)}) collective-permute-start(bf16[2,1,208,128]{3,2,1,0:T(8,128)(2,1)S(1)} %get-tuple-element.157), channel_id=1, source_target_pairs={{0,4},{2,6},{4,0},{6,2},{8,12},{10,14},{12,8},{14,10},{1,5},{3,7},... | collective-permute-start | bytes 319496 | tf_op jit(solution)/shard_map/ppermute | solution.py:259
  36.4 4.8 %collective-permute-start.14 = (bf16[2,1,208,128]{3,2,1,0:T(8,128)(2,1)S(1)}, bf16[2,1,208,128]{3,2,1,0:T(8,128)(2,1)S(1)}, u32[]{:S(2)}, u32[]{:S(2)}) collective-permute-start(bf16[2,1,208,128]{3,2,1,0:T(8,128)(2,1)S(1)} %fusion.30), channel_id=1, source_target_pairs={{0,2},{2,0},{4,6},{6,4},{8,10},{10,8},{12,14},{14,12},{1,3},{3,1},... | collective-permute-start | bytes 319496 | tf_op jit(solution)/shard_map/ppermute | solution.py:259
  38.2 9.0 %collective-permute-start.12 = (bf16[2,1,208,128]{3,2,1,0:T(8,128)(2,1)S(1)}, bf16[2,1,208,128]{3,2,1,0:T(8,128)(2,1)S(1)}, u32[]{:S(2)}, u32[]{:S(2)}) collective-permute-start(bf16[2,1,208,128]{3,2,1,0:T(8,128)(2,1)S(1)} %fusion.29), channel_id=1, source_target_pairs={{0,4},{2,6},{4,0},{6,2},{8,12},{10,14},{12,8},{14,10},{1,5},{3,7},... | collective-permute-start | bytes 319496 | tf_op jit(solution)/shard_map/ppermute | solution.py:259
  38.6 8.9 %collective-permute-start.15 = (bf16[2,2,1,208,128]{4,3,1,2,0:T(8,128)(2,1)S(1)}, bf16[2,2,1,208,128]{4,3,1,2,0:T(8,128)(2,1)S(1)}, u32[]{:S(2)}, u32[]{:S(2)}) collective-permute-start(bf16[2,2,1,208,128]{4,3,1,2,0:T(8,128)(2,1)S(1)} %bitcast.203), channel_id=1, source_target_pairs={{0,4},{2,6},{4,0},{6,2},{8,12},{10,14},{12,8},{14,10},{1,5},{3,7},... | collective-permute-start | bytes 638984 | tf_op jit(solution)/shard_map/ppermute | solution.py:259
  40.3 10.2 %collective-permute-start.11 = (bf16[2,2,1,208,128]{4,3,1,2,0:T(8,128)(2,1)S(1)}, bf16[2,2,1,208,128]{4,3,1,2,0:T(8,128)(2,1)S(1)}, u32[]{:S(2)}, u32[]{:S(2)}) collective-permute-start(bf16[2,2,1,208,128]{4,3,1,2,0:T(8,128)(2,1)S(1)} %bitcast.202), channel_id=1, source_target_pairs={{0,2},{2,0},{4,6},{6,4},{8,10},{10,8},{12,14},{14,12},{1,3},{3,1},... | collective-permute-start | bytes 638984 | tf_op jit(solution)/shard_map/ppermute | solution.py:259
  41.2 9.4 %collective-permute-start.16 = (bf16[1,1,208,128]{3,2,1,0:T(8,128)(2,1)S(1)}, bf16[1,1,208,128]{3,2,1,0:T(8,128)(2,1)S(1)}, u32[]{:S(2)}, u32[]{:S(2)}) collective-permute-start(bf16[1,1,208,128]{3,2,1,0:T(8,128)(2,1)S(1)} %slice.310), channel_id=1, source_target_pairs={{0,8},{2,10},{4,12},{6,14},{8,0},{10,2},{12,4},{14,6},{1,9},{3,11}... | collective-permute-start | bytes 159752 | tf_op jit(solution)/shard_map/ppermute | solution.py:259
  47.2 6.1 %collective-permute-start.7 = (bf16[1,1,208,128]{3,2,1,0:T(8,128)(2,1)S(1)}, bf16[1,1,208,128]{3,2,1,0:T(8,128)(2,1)S(1)}, u32[]{:S(2)}, u32[]{:S(2)}) collective-permute-start(bf16[1,1,208,128]{3,2,1,0:T(8,128)(2,1)S(1)} %slice.311), channel_id=1, source_target_pairs={{0,8},{2,10},{4,12},{6,14},{8,0},{10,2},{12,4},{14,6},{1,9},{3,11}... | collective-permute-start | bytes 159752 | tf_op jit(solution)/shard_map/ppermute | solution.py:259
  47.4 11.0 %collective-permute-start.21 = (bf16[1,1,208,128]{3,2,1,0:T(8,128)(2,1)S(1)}, bf16[1,1,208,128]{3,2,1,0:T(8,128)(2,1)S(1)}, u32[]{:S(2)}, u32[]{:S(2)}) collective-permute-start(bf16[1,1,208,128]{3,2,1,0:T(8,128)(2,1)S(1)} %slice.308), channel_id=1, source_target_pairs={{0,8},{2,10},{4,12},{6,14},{8,0},{10,2},{12,4},{14,6},{1,9},{3,11}... | collective-permute-start | bytes 159752 | tf_op jit(solution)/shard_map/ppermute | solution.py:259
  50.4 9.1 %collective-permute-start.20 = (bf16[1,1,208,128]{3,2,1,0:T(8,128)(2,1)S(1)}, bf16[1,1,208,128]{3,2,1,0:T(8,128)(2,1)S(1)}, u32[]{:S(2)}, u32[]{:S(2)}) collective-permute-start(bf16[1,1,208,128]{3,2,1,0:T(8,128)(2,1)S(1)} %slice.309), channel_id=1, source_target_pairs={{0,8},{2,10},{4,12},{6,14},{8,0},{10,2},{12,4},{14,6},{1,9},{3,11}... | collective-permute-start | bytes 159752 | tf_op jit(solution)/shard_map/ppermute | solution.py:259
  50.6 12.0 %collective-permute-start.22 = (bf16[2,1,208,128]{3,2,1,0:T(8,128)(2,1)S(1)}, bf16[2,1,208,128]{3,2,1,0:T(8,128)(2,1)S(1)}, u32[]{:S(2)}, u32[]{:S(2)}) collective-permute-start(bf16[2,1,208,128]{3,2,1,0:T(8,128)(2,1)S(1)} %fusion.32), channel_id=1, source_target_pairs={{0,2},{2,0},{4,6},{6,4},{8,10},{10,8},{12,14},{14,12},{1,3},{3,1},... | collective-permute-start | bytes 319496 | tf_op jit(solution)/shard_map/ppermute | solution.py:259
  53.3 10.4 %collective-permute-start.19 = (bf16[2,1,208,128]{3,2,1,0:T(8,128)(2,1)S(1)}, bf16[2,1,208,128]{3,2,1,0:T(8,128)(2,1)S(1)}, u32[]{:S(2)}, u32[]{:S(2)}) collective-permute-start(bf16[2,1,208,128]{3,2,1,0:T(8,128)(2,1)S(1)} %fusion.31), channel_id=1, source_target_pairs={{0,4},{2,6},{4,0},{6,2},{8,12},{10,14},{12,8},{14,10},{1,5},{3,7},... | collective-permute-start | bytes 319496 | tf_op jit(solution)/shard_map/ppermute | solution.py:259
  54.9 11.6 %collective-permute-start.26 = (bf16[2,1,16,4096]{3,2,1,0:T(8,128)(2,1)S(1)}, bf16[2,1,16,4096]{3,2,1,0:T(8,128)(2,1)S(1)}, u32[]{:S(2)}, u32[]{:S(2)}) collective-permute-start(bf16[2,1,16,4096]{3,2,1,0:T(8,128)(2,1)S(1)} %get-tuple-element.117), channel_id=1, source_target_pairs={{0,4},{2,6},{4,0},{6,2},{8,12},{10,14},{12,8},{14,10},{1,5},{3,7},... | collective-permute-start | bytes 786440 | tf_op jit(solution)/shard_map/ppermute | solution.py:259
  58.4 8.6 %collective-permute-start.18 = (bf16[2,1,16,4096]{3,2,1,0:T(8,128)(2,1)S(1)}, bf16[2,1,16,4096]{3,2,1,0:T(8,128)(2,1)S(1)}, u32[]{:S(2)}, u32[]{:S(2)}) collective-permute-start(bf16[2,1,16,4096]{3,2,1,0:T(8,128)(2,1)S(1)} %get-tuple-element.116), channel_id=1, source_target_pairs={{0,2},{2,0},{4,6},{6,4},{8,10},{10,8},{12,14},{14,12},{1,3},{3,1},... | collective-permute-start | bytes 786440 | tf_op jit(solution)/shard_map/ppermute | solution.py:259
  61.0 10.1 %collective-permute-start.27 = (bf16[2,1,16,4096]{3,2,1,0:T(8,128)(2,1)S(1)}, bf16[2,1,16,4096]{3,2,1,0:T(8,128)(2,1)S(1)}, u32[]{:S(2)}, u32[]{:S(2)}) collective-permute-start(bf16[2,1,16,4096]{3,2,1,0:T(8,128)(2,1)S(1)} %get-tuple-element.121), channel_id=1, source_target_pairs={{0,4},{2,6},{4,0},{6,2},{8,12},{10,14},{12,8},{14,10},{1,5},{3,7},... | collective-permute-start | bytes 786440 | tf_op jit(solution)/shard_map/ppermute | solution.py:259
  62.7 9.5 %collective-permute-start.25 = (bf16[2,1,16,4096]{3,2,1,0:T(8,128)(2,1)S(1)}, bf16[2,1,16,4096]{3,2,1,0:T(8,128)(2,1)S(1)}, u32[]{:S(2)}, u32[]{:S(2)}) collective-permute-start(bf16[2,1,16,4096]{3,2,1,0:T(8,128)(2,1)S(1)} %get-tuple-element.120), channel_id=1, source_target_pairs={{0,2},{2,0},{4,6},{6,4},{8,10},{10,8},{12,14},{14,12},{1,3},{3,1},... | collective-permute-start | bytes 786440 | tf_op jit(solution)/shard_map/ppermute | solution.py:259
  63.9 9.5 %collective-permute-start.28 = (bf16[1,1,208,128]{3,2,1,0:T(8,128)(2,1)S(1)}, bf16[1,1,208,128]{3,2,1,0:T(8,128)(2,1)S(1)}, u32[]{:S(2)}, u32[]{:S(2)}) collective-permute-start(bf16[1,1,208,128]{3,2,1,0:T(8,128)(2,1)S(1)} %slice.306), channel_id=1, source_target_pairs={{0,8},{2,10},{4,12},{6,14},{8,0},{10,2},{12,4},{14,6},{1,9},{3,11}... | collective-permute-start | bytes 159752 | tf_op jit(solution)/shard_map/ppermute | solution.py:259
  66.5 7.8 %collective-permute-start.24 = (bf16[1,1,208,128]{3,2,1,0:T(8,128)(2,1)S(1)}, bf16[1,1,208,128]{3,2,1,0:T(8,128)(2,1)S(1)}, u32[]{:S(2)}, u32[]{:S(2)}) collective-permute-start(bf16[1,1,208,128]{3,2,1,0:T(8,128)(2,1)S(1)} %slice.307), channel_id=1, source_target_pairs={{0,8},{2,10},{4,12},{6,14},{8,0},{10,2},{12,4},{14,6},{1,9},{3,11}... | collective-permute-start | bytes 159752 | tf_op jit(solution)/shard_map/ppermute | solution.py:259
  67.1 11.9 %collective-permute-start.23 = (bf16[1,16,4096]{2,1,0:T(8,128)(2,1)S(1)}, bf16[1,16,4096]{2,1,0:T(8,128)(2,1)S(1)}, u32[]{:S(2)}, u32[]{:S(2)}) collective-permute-start(bf16[1,16,4096]{2,1,0:T(8,128)(2,1)S(1)} %fusion.21), channel_id=1, source_target_pairs={{0,4},{2,6},{4,0},{6,2},{8,12},{10,14},{12,8},{14,10},{1,5},{3,7},... | collective-permute-start | bytes 393224 | tf_op jit(solution)/shard_map/ppermute | solution.py:259
  71.1 8.4 %collective-permute-start.29 = (bf16[1,16,4096]{2,1,0:T(8,128)(2,1)S(1)}, bf16[1,16,4096]{2,1,0:T(8,128)(2,1)S(1)}, u32[]{:S(2)}, u32[]{:S(2)}) collective-permute-start(bf16[1,16,4096]{2,1,0:T(8,128)(2,1)S(1)} %fusion.22), channel_id=1, source_target_pairs={{0,2},{2,0},{4,6},{6,4},{8,10},{10,8},{12,14},{14,12},{1,3},{3,1},... | collective-permute-start | bytes 393224 | tf_op jit(solution)/shard_map/ppermute | solution.py:259
  72.3 7.4 %collective-permute-start.31 = (bf16[1,16,4096]{2,1,0:T(8,128)(2,1)S(1)}, bf16[1,16,4096]{2,1,0:T(8,128)(2,1)S(1)}, u32[]{:S(2)}, u32[]{:S(2)}) collective-permute-start(bf16[1,16,4096]{2,1,0:T(8,128)(2,1)S(1)} %fusion.24), channel_id=1, source_target_pairs={{0,2},{2,0},{4,6},{6,4},{8,10},{10,8},{12,14},{14,12},{1,3},{3,1},... | collective-permute-start | bytes 393224 | tf_op jit(solution)/shard_map/ppermute | solution.py:259
  73.4 6.3 %collective-permute-start.32 = (bf16[1,16,4096]{2,1,0:T(8,128)(2,1)S(1)}, bf16[1,16,4096]{2,1,0:T(8,128)(2,1)S(1)}, u32[]{:S(2)}, u32[]{:S(2)}) collective-permute-start(bf16[1,16,4096]{2,1,0:T(8,128)(2,1)S(1)} %fusion.23), channel_id=1, source_target_pairs={{0,4},{2,6},{4,0},{6,2},{8,12},{10,14},{12,8},{14,10},{1,5},{3,7},... | collective-permute-start | bytes 393224 | tf_op jit(solution)/shard_map/ppermute | solution.py:259
  75.8 6.7 %collective-permute-start.35 = (bf16[2,1,16,4096]{3,2,1,0:T(8,128)(2,1)S(1)}, bf16[2,1,16,4096]{3,2,1,0:T(8,128)(2,1)S(1)}, u32[]{:S(2)}, u32[]{:S(2)}) collective-permute-start(bf16[2,1,16,4096]{3,2,1,0:T(8,128)(2,1)S(1)} %get-tuple-element.133), channel_id=1, source_target_pairs={{0,2},{2,0},{4,6},{6,4},{8,10},{10,8},{12,14},{14,12},{1,3},{3,1},... | collective-permute-start | bytes 786440 | tf_op jit(solution)/shard_map/ppermute | solution.py:259
  79.0 7.6 %collective-permute-start.36 = (bf16[2,1,16,4096]{3,2,1,0:T(8,128)(2,1)S(1)}, bf16[2,1,16,4096]{3,2,1,0:T(8,128)(2,1)S(1)}, u32[]{:S(2)}, u32[]{:S(2)}) collective-permute-start(bf16[2,1,16,4096]{3,2,1,0:T(8,128)(2,1)S(1)} %get-tuple-element.134), channel_id=1, source_target_pairs={{0,4},{2,6},{4,0},{6,2},{8,12},{10,14},{12,8},{14,10},{1,5},{3,7},... | collective-permute-start | bytes 786440 | tf_op jit(solution)/shard_map/ppermute | solution.py:259
  79.6 1.6 %collective-permute-start.30 = (f32[16,4096]{1,0:T(8,128)S(1)}, f32[16,4096]{1,0:T(8,128)S(1)}, u32[]{:S(2)}, u32[]{:S(2)}) collective-permute-start(f32[16,4096]{1,0:T(8,128)S(1)} %fusion.12), channel_id=1, source_target_pairs={{0,1},{1,0},{2,3},{3,2},{4,5},{5,4},{6,7},{7,6},{8,9},{9,8},{10,11... | collective-permute-start | bytes 786440 | tf_op jit(solution)/shard_map/ppermute | solution.py:263
  79.7 7.5 %collective-permute-start.34 = (f32[16,4096]{1,0:T(8,128)S(1)}, f32[16,4096]{1,0:T(8,128)S(1)}, u32[]{:S(2)}, u32[]{:S(2)}) collective-permute-start(f32[16,4096]{1,0:T(8,128)S(1)} %fusion.15), channel_id=1, source_target_pairs={{0,1},{1,0},{2,3},{3,2},{4,5},{5,4},{6,7},{7,6},{8,9},{9,8},{10,11... | collective-permute-start | bytes 786440 | tf_op jit(solution)/shard_map/ppermute | solution.py:263
  81.2 11.6 %collective-permute-start.33 = (bf16[16,4096]{1,0:T(8,128)(2,1)S(1)}, bf16[16,4096]{1,0:T(8,128)(2,1)S(1)}, u32[]{:S(2)}, u32[]{:S(2)}) collective-permute-start(bf16[16,4096]{1,0:T(8,128)(2,1)S(1)} %get-tuple-element.155), channel_id=1, source_target_pairs={{0,8},{2,10},{4,12},{6,14},{8,0},{10,2},{12,4},{14,6},{1,9},{3,11}... | collective-permute-start | bytes 393224 | tf_op jit(solution)/shard_map/ppermute | solution.py:259
  86.7 6.1 %collective-permute-start.38 = (bf16[1,16,4096]{2,1,0:T(8,128)(2,1)S(1)}, bf16[1,16,4096]{2,1,0:T(8,128)(2,1)S(1)}, u32[]{:S(2)}, u32[]{:S(2)}) collective-permute-start(bf16[1,16,4096]{2,1,0:T(8,128)(2,1)S(1)} %fusion.26), channel_id=1, source_target_pairs={{0,2},{2,0},{4,6},{6,4},{8,10},{10,8},{12,14},{14,12},{1,3},{3,1},... | collective-permute-start | bytes 393224 | tf_op jit(solution)/shard_map/ppermute | solution.py:259
  86.8 6.0 %collective-permute-start.39 = (bf16[1,16,4096]{2,1,0:T(8,128)(2,1)S(1)}, bf16[1,16,4096]{2,1,0:T(8,128)(2,1)S(1)}, u32[]{:S(2)}, u32[]{:S(2)}) collective-permute-start(bf16[1,16,4096]{2,1,0:T(8,128)(2,1)S(1)} %fusion.25), channel_id=1, source_target_pairs={{0,4},{2,6},{4,0},{6,2},{8,12},{10,14},{12,8},{14,10},{1,5},{3,7},... | collective-permute-start | bytes 393224 | tf_op jit(solution)/shard_map/ppermute | solution.py:259
  87.3 8.9 %collective-permute-start.37 = (bf16[16,4096]{1,0:T(8,128)(2,1)S(1)}, bf16[16,4096]{1,0:T(8,128)(2,1)S(1)}, u32[]{:S(2)}, u32[]{:S(2)}) collective-permute-start(bf16[16,4096]{1,0:T(8,128)(2,1)S(1)} %get-tuple-element.153), channel_id=1, source_target_pairs={{0,8},{2,10},{4,12},{6,14},{8,0},{10,2},{12,4},{14,6},{1,9},{3,11}... | collective-permute-start | bytes 393224 | tf_op jit(solution)/shard_map/ppermute | solution.py:259
  92.9 3.3 %collective-permute-start.40 = (f32[16,4096]{1,0:T(8,128)S(1)}, f32[16,4096]{1,0:T(8,128)S(1)}, u32[]{:S(2)}, u32[]{:S(2)}) collective-permute-start(f32[16,4096]{1,0:T(8,128)S(1)} %fusion.17), channel_id=1, source_target_pairs={{0,1},{1,0},{2,3},{3,2},{4,5},{5,4},{6,7},{7,6},{8,9},{9,8},{10,11... | collective-permute-start | bytes 786440 | tf_op jit(solution)/shard_map/ppermute | solution.py:263
  96.3 7.6 %collective-permute-start.41 = (bf16[16,4096]{1,0:T(8,128)(2,1)S(1)}, bf16[16,4096]{1,0:T(8,128)(2,1)S(1)}, u32[]{:S(2)}, u32[]{:S(2)}) collective-permute-start(bf16[16,4096]{1,0:T(8,128)(2,1)S(1)} %get-tuple-element.151), channel_id=1, source_target_pairs={{0,8},{2,10},{4,12},{6,14},{8,0},{10,2},{12,4},{14,6},{1,9},{3,11}... | collective-permute-start | bytes 393224 | tf_op jit(solution)/shard_map/ppermute | solution.py:259

commit v5 on v4

--- a/solution.py
+++ b/solution.py
@@ -12,7 +12,7 @@
 
 
 ORDERS = [(((0, 1), (1, 0)), ((0, 1), (1, 0))), (((0, 1), (1, 0)), ((0, 1), (1, 0))), (((0, 1), (1, 0)), ((0, 1), (1, 0)))]
-TURNS = [0, 1, 0, 1, 2, 0, 1, 2, 0, 1, 2, 0, 1, 2, 0, 1, 0, 2, 1, 0, 2, 1, 2, 2]
+TURNS = [0, 1, 0, 1, 2, 0, 1, 2, 0, 1, 2, 0, 1, 2, 0, 0, 1, 2, 0, 1, 2, 1, 2, 2]
 
 
 def wire_type(stage, stages):

time: 105 us -> 110 us (1.048)
  waiting for transfers between devices: 28.7 us -> 34.6 us
    ppermute x33, waiting for transfers between devices: 24 us -> 30.7 us  [swap(): return lax.ppermute(value, 'gx', [(i, i ^ 1 << bit) for i in range(count)])]
  transfers between devices with their start and end apart: 42 -> 42, of which waited for: 13 -> 18; matrix products, arithmetic and copies ran while one was open for 1% -> 1% of each run, Pallas kernels for 9% -> 9%
where the time goes in v5:
time: 110 us
  starting transfers between devices  54.7 us (50%)
  waiting for transfers between devices  34.6 us (31%)
  Pallas kernels  16.5 us (15%)
  other arithmetic  2.05 us (2%)
  local copies, waits for them, and re-layouts  1.29 us (1%)
    ppermute x33, starting transfers between devices, swap(): return lax.ppermute(value, 'gx', [(i, i ^ 1 << bit) for i in range(count)])  43.5 us
    ppermute x33, waiting for transfers between devices, swap(): return lax.ppermute(value, 'gx', [(i, i ^ 1 << bit) for i in range(count)])  30.7 us
    pallas_call x6, Pallas kernels, down_project(): pl.pallas_call(functools.partial(down_kernel, block, count, order), out_s...  8.89 us
    pallas_call x1, Pallas kernels, project(): pl.pallas_call(functools.partial(project_kernel, block, cuts, len(arrived...  7 us
    ppermute x4, starting transfers between devices, move(): lax.ppermute(value, ('gx', 'gy'), [(2 * a + b, 2 * c + d) for (a, b), (c,...  6.22 us
    ppermute x5, starting transfers between devices, swap_cores(): return lax.ppermute(value, 'gy', [(0, 1), (1, 0)])  4.92 us
    ppermute x4, waiting for transfers between devices, move(): lax.ppermute(value, ('gx', 'gy'), [(2 * a + b, 2 * c + d) for (a, b), (c,...  3.74 us
  transfers between devices with their start and end apart: 42, of which 18 were waited for; matrix products, arithmetic and copies ran while one was open for 1% of the time, Pallas kernels for 9%

profile of v5, /device:TPU:0, one launch (start us, length us, event | category | flops | bytes accessed | tf_op | source)
XLA Modules:
  0.0 109.5 jit_solution(15134686668496762943)
XLA Ops:
  0.0 0.5 collective-permute-start.4
  0.5 1.0 copy-done.1
  1.5 0.6 shard_map.37
  2.1 0.7 collective-permute-start
  2.8 2.5 %collective-permute-start.1 = (bf16[48,1024]{1,0:T(8,128)(2,1)S(1)}, bf16[48,1024]{1,0:T(8,128)(2,1)S(1)}, u32[]{:S(2)}, u32[]{:S(2)}) collective-permute-start(bf16[48,1024]{1,0:T(8,128)(2,1)S(1)} %get-tuple-element.83), channel_id=1, source_target_pairs={{0,2},{1,10},{2,4},{3,12},{4,6},{5,14},{6,0},{7,8},{8,3},{9,11},{1... | collective-permute-start | bytes 294920 | tf_op jit(solution)/shard_map/ppermute | solution.py:287
  5.3 1.6 %collective-permute-start.2 = (bf16[48,1024]{1,0:T(8,128)(2,1)S(1)}, bf16[48,1024]{1,0:T(8,128)(2,1)S(1)}, u32[]{:S(2)}, u32[]{:S(2)}) collective-permute-start(bf16[48,1024]{1,0:T(8,128)(2,1)S(1)} %get-tuple-element.84), channel_id=1, source_target_pairs={{0,4},{1,12},{2,6},{3,14},{4,0},{5,8},{6,2},{7,10},{8,5},{9,13},{1... | collective-permute-start | bytes 294920 | tf_op jit(solution)/shard_map/ppermute | solution.py:287
  6.9 1.4 %collective-permute-start.3 = (bf16[48,1024]{1,0:T(8,128)(2,1)S(1)}, bf16[48,1024]{1,0:T(8,128)(2,1)S(1)}, u32[]{:S(2)}, u32[]{:S(2)}) collective-permute-start(bf16[48,1024]{1,0:T(8,128)(2,1)S(1)} %get-tuple-element.85), channel_id=1, source_target_pairs={{0,6},{1,14},{2,0},{3,8},{4,2},{5,10},{6,4},{7,12},{8,7},{9,15},{1... | collective-permute-start | bytes 294920 | tf_op jit(solution)/shard_map/ppermute | solution.py:287
  8.3 0.6 collective-permute-done.1.refs_1_
  8.9 2.1 %collective-permute-done.2.refs_2_ = bf16[48,1024]{1,0:T(8,128)(2,1)S(1)} collective-permute-done((bf16[48,1024]{1,0:T(8,128)(2,1)S(1)}, bf16[48,1024]{1,0:T(8,128)(2,1)S(1)}, u32[]{:S(2)}, u32[]{:S(2)}) %collective-permute-start.2) | collective-permute-done | bytes 98336 | tf_op jit(solution)/shard_map/ppermute | solution.py:287
  11.0 1.1 collective-permute-done.3.refs_3_
  12.1 7.0 %shard_map.38 = (bf16[2,2,1,208,128]{4,3,2,1,0:T(8,128)(2,1)S(1)}, f32[2,2,1,208,128]{4,3,2,1,0:T(8,128)S(1)}, bf16[2,2,1,208,128]{4,3,2,1,0:T(8,128)(2,1)S(1)},...) custom-call(s32[2]{0:T(128)S(1)} %pad_add_fusion.place_ref, ...), custom_call_target="tpu_custom_call" | custom-call | flops 1308622848 | bytes 6815744 | tf_op jit(solution)/shard_map/pallas_call | solution.py:148
  19.1 2.3 %collective-permute-start.9 = (bf16[2,2,1,208,128]{4,3,1,2,0:T(8,128)(2,1)S(1)}, bf16[2,2,1,208,128]{4,3,1,2,0:T(8,128)(2,1)S(1)}, u32[]{:S(2)}, u32[]{:S(2)}) collective-permute-start(bf16[2,2,1,208,128]{4,3,1,2,0:T(8,128)(2,1)S(1)} %bitcast.207), channel_id=1, source_target_pairs={{0,4},{2,6},{4,0},{6,2},{8,12},{10,14},{12,8},{14,10},{1,5},{3,7},... | collective-permute-start | bytes 638984 | tf_op jit(solution)/shard_map/ppermute | solution.py:259
  21.3 1.9 %collective-permute-start.5 = (bf16[2,2,1,208,128]{4,3,1,2,0:T(8,128)(2,1)S(1)}, bf16[2,2,1,208,128]{4,3,1,2,0:T(8,128)(2,1)S(1)}, u32[]{:S(2)}, u32[]{:S(2)}) collective-permute-start(bf16[2,2,1,208,128]{4,3,1,2,0:T(8,128)(2,1)S(1)} %bitcast.206), channel_id=1, source_target_pairs={{0,2},{2,0},{4,6},{6,4},{8,10},{10,8},{12,14},{14,12},{1,3},{3,1},... | collective-permute-start | bytes 638984 | tf_op jit(solution)/shard_map/ppermute | solution.py:259
  23.2 4.3 %collective-permute-start.17 = (bf16[208,8192]{1,0:T(8,128)(2,1)S(1)}, bf16[208,8192]{1,0:T(8,128)(2,1)S(1)}, u32[]{:S(2)}, u32[]{:S(2)}) collective-permute-start(bf16[208,8192]{1,0:T(8,128)(2,1)S(1)} %copy-done), channel_id=1, source_target_pairs={{0,1},{1,0},{2,3},{3,2},{4,5},{5,4},{6,7},{7,6},{8,9},{9,8},{10,11... | collective-permute-start | bytes 10223624 | tf_op jit(solution)/shard_map/ppermute | solution.py:263
  27.5 0.7 collective-permute-start.10
  28.2 1.7 %collective-permute-start.8 = (bf16[2,2,1,208,128]{4,3,1,2,0:T(8,128)(2,1)S(1)}, bf16[2,2,1,208,128]{4,3,1,2,0:T(8,128)(2,1)S(1)}, u32[]{:S(2)}, u32[]{:S(2)}) collective-permute-start(bf16[2,2,1,208,128]{4,3,1,2,0:T(8,128)(2,1)S(1)} %bitcast.204), channel_id=1, source_target_pairs={{0,2},{2,0},{4,6},{6,4},{8,10},{10,8},{12,14},{14,12},{1,3},{3,1},... | collective-permute-start | bytes 638984 | tf_op jit(solution)/shard_map/ppermute | solution.py:259
  30.0 0.4 collective-permute-start.13
  30.4 1.3 %collective-permute-start.6 = (bf16[2,1,208,128]{3,2,1,0:T(8,128)(2,1)S(1)}, bf16[2,1,208,128]{3,2,1,0:T(8,128)(2,1)S(1)}, u32[]{:S(2)}, u32[]{:S(2)}) collective-permute-start(bf16[2,1,208,128]{3,2,1,0:T(8,128)(2,1)S(1)} %get-tuple-element.157), channel_id=1, source_target_pairs={{0,4},{2,6},{4,0},{6,2},{8,12},{10,14},{12,8},{14,10},{1,5},{3,7},... | collective-permute-start | bytes 319496 | tf_op jit(solution)/shard_map/ppermute | solution.py:259
  31.7 3.9 %collective-permute-done.10 = bf16[2,2,1,208,128]{4,3,1,2,0:T(8,128)(2,1)S(1)} collective-permute-done((bf16[2,2,1,208,128]{4,3,1,2,0:T(8,128)(2,1)S(1)}, bf16[2,2,1,208,128]{4,3,1,2,0:T(8,128)(2,1)S(1)}, u32[]{:S(2)}, u32[]{:S(2)}) %collective-permute-start.10) | collective-permute-done | bytes 213024 | tf_op jit(solution)/shard_map/ppermute | solution.py:259
  35.7 0.6 collective-permute-done.8
  36.4 1.8 %collective-permute-start.14 = (bf16[2,1,208,128]{3,2,1,0:T(8,128)(2,1)S(1)}, bf16[2,1,208,128]{3,2,1,0:T(8,128)(2,1)S(1)}, u32[]{:S(2)}, u32[]{:S(2)}) collective-permute-start(bf16[2,1,208,128]{3,2,1,0:T(8,128)(2,1)S(1)} %fusion.30), channel_id=1, source_target_pairs={{0,2},{2,0},{4,6},{6,4},{8,10},{10,8},{12,14},{14,12},{1,3},{3,1},... | collective-permute-start | bytes 319496 | tf_op jit(solution)/shard_map/ppermute | solution.py:259
  38.2 0.4 collective-permute-start.12
  38.6 1.7 %collective-permute-start.15 = (bf16[2,2,1,208,128]{4,3,1,2,0:T(8,128)(2,1)S(1)}, bf16[2,2,1,208,128]{4,3,1,2,0:T(8,128)(2,1)S(1)}, u32[]{:S(2)}, u32[]{:S(2)}) collective-permute-start(bf16[2,2,1,208,128]{4,3,1,2,0:T(8,128)(2,1)S(1)} %bitcast.203), channel_id=1, source_target_pairs={{0,4},{2,6},{4,0},{6,2},{8,12},{10,14},{12,8},{14,10},{1,5},{3,7},... | collective-permute-start | bytes 638984 | tf_op jit(solution)/shard_map/ppermute | solution.py:259
  40.3 0.3 collective-permute-start.11
  40.6 0.6 collective-permute-done.14
  41.2 6.0 %collective-permute-start.16 = (bf16[1,1,208,128]{3,2,1,0:T(8,128)(2,1)S(1)}, bf16[1,1,208,128]{3,2,1,0:T(8,128)(2,1)S(1)}, u32[]{:S(2)}, u32[]{:S(2)}) collective-permute-start(bf16[1,1,208,128]{3,2,1,0:T(8,128)(2,1)S(1)} %slice.310), channel_id=1, source_target_pairs={{0,8},{2,10},{4,12},{6,14},{8,0},{10,2},{12,4},{14,6},{1,9},{3,11}... | collective-permute-start | bytes 159752 | tf_op jit(solution)/shard_map/ppermute | solution.py:259
  47.4 3.0 %collective-permute-start.21 = (bf16[1,1,208,128]{3,2,1,0:T(8,128)(2,1)S(1)}, bf16[1,1,208,128]{3,2,1,0:T(8,128)(2,1)S(1)}, u32[]{:S(2)}, u32[]{:S(2)}) collective-permute-start(bf16[1,1,208,128]{3,2,1,0:T(8,128)(2,1)S(1)} %slice.308), channel_id=1, source_target_pairs={{0,8},{2,10},{4,12},{6,14},{8,0},{10,2},{12,4},{14,6},{1,9},{3,11}... | collective-permute-start | bytes 159752 | tf_op jit(solution)/shard_map/ppermute | solution.py:259
  50.4 0.1 collective-permute-start.20
  50.6 1.9 %collective-permute-start.22 = (bf16[2,1,208,128]{3,2,1,0:T(8,128)(2,1)S(1)}, bf16[2,1,208,128]{3,2,1,0:T(8,128)(2,1)S(1)}, u32[]{:S(2)}, u32[]{:S(2)}) collective-permute-start(bf16[2,1,208,128]{3,2,1,0:T(8,128)(2,1)S(1)} %fusion.32), channel_id=1, source_target_pairs={{0,2},{2,0},{4,6},{6,4},{8,10},{10,8},{12,14},{14,12},{1,3},{3,1},... | collective-permute-start | bytes 319496 | tf_op jit(solution)/shard_map/ppermute | solution.py:259
  52.6 0.8 collective-permute-done.7
  53.3 0.1 collective-permute-start.19
  53.4 1.5 %shard_map.40 = (bf16[2,1,16,4096]{3,2,1,0:T(8,128)(2,1)S(1)}, f32[2,1,16,4096]{3,2,1,0:T(8,128)S(1)}) custom-call(s32[2]{0:T(128)S(1)} %pad_add_fusion.place_ref, f32[1,208,128]{2,1,0:T(8,128)S(1)} %slice_bitcast_fusion.17.refs_0_, bf16[1,208,128]{2,1,0:T(8,128)(2,1)S(1)} %bitcast.194, f32[1,208,128]{2,1,0:T(8,128)S(1)} %slice_bitcast_fusion.16.refs_2_, ...), custom_call_target="tpu_custom_call" | custom-call | flops 218103808 | bytes 3407872 | tf_op jit(solution)/shard_map/pallas_call | solution.py:231
  54.9 2.0 %collective-permute-start.26 = (bf16[2,1,16,4096]{3,2,1,0:T(8,128)(2,1)S(1)}, bf16[2,1,16,4096]{3,2,1,0:T(8,128)(2,1)S(1)}, u32[]{:S(2)}, u32[]{:S(2)}) collective-permute-start(bf16[2,1,16,4096]{3,2,1,0:T(8,128)(2,1)S(1)} %get-tuple-element.117), channel_id=1, source_target_pairs={{0,4},{2,6},{4,0},{6,2},{8,12},{10,14},{12,8},{14,10},{1,5},{3,7},... | collective-permute-start | bytes 786440 | tf_op jit(solution)/shard_map/ppermute | solution.py:259
  56.9 1.5 %shard_map.39 = (bf16[2,1,16,4096]{3,2,1,0:T(8,128)(2,1)S(1)}, f32[2,1,16,4096]{3,2,1,0:T(8,128)S(1)}) custom-call(s32[2]{0:T(128)S(1)} %pad_add_fusion.place_ref, f32[1,208,128]{2,1,0:T(8,128)S(1)} %slice_bitcast_fusion.17.refs_0_, bf16[1,208,128]{2,1,0:T(8,128)(2,1)S(1)} %bitcast.195, f32[1,208,128]{2,1,0:T(8,128)S(1)} %slice_bitcast_fusion.16.refs_2_, ...), custom_call_target="tpu_custom_call" | custom-call | flops 218103808 | bytes 3407872 | tf_op jit(solution)/shard_map/pallas_call | solution.py:231
  58.4 1.0 collective-permute-start.18
  59.5 1.5 %shard_map.42 = (bf16[2,1,16,4096]{3,2,1,0:T(8,128)(2,1)S(1)}, f32[2,1,16,4096]{3,2,1,0:T(8,128)S(1)}) custom-call(s32[2]{0:T(128)S(1)} %pad_add_fusion.place_ref, f32[1,208,128]{2,1,0:T(8,128)S(1)} %slice_bitcast_fusion.15.refs_0_, bf16[1,208,128]{2,1,0:T(8,128)(2,1)S(1)} %bitcast.196, f32[1,208,128]{2,1,0:T(8,128)S(1)} %slice_bitcast_fusion.14.refs_2_, ...), custom_call_target="tpu_custom_call" | custom-call | flops 218103808 | bytes 3407872 | tf_op jit(solution)/shard_map/pallas_call | solution.py:231
  61.0 0.2 collective-permute-start.27
  61.2 1.5 %shard_map.41 = (bf16[2,1,16,4096]{3,2,1,0:T(8,128)(2,1)S(1)}, f32[2,1,16,4096]{3,2,1,0:T(8,128)S(1)}) custom-call(s32[2]{0:T(128)S(1)} %pad_add_fusion.place_ref, f32[1,208,128]{2,1,0:T(8,128)S(1)} %slice_bitcast_fusion.15.refs_0_, bf16[1,208,128]{2,1,0:T(8,128)(2,1)S(1)} %bitcast.197, f32[1,208,128]{2,1,0:T(8,128)S(1)} %slice_bitcast_fusion.14.refs_2_, ...), custom_call_target="tpu_custom_call" | custom-call | flops 218103808 | bytes 3407872 | tf_op jit(solution)/shard_map/pallas_call | solution.py:231
  62.7 1.1 %collective-permute-start.25 = (bf16[2,1,16,4096]{3,2,1,0:T(8,128)(2,1)S(1)}, bf16[2,1,16,4096]{3,2,1,0:T(8,128)(2,1)S(1)}, u32[]{:S(2)}, u32[]{:S(2)}) collective-permute-start(bf16[2,1,16,4096]{3,2,1,0:T(8,128)(2,1)S(1)} %get-tuple-element.120), channel_id=1, source_target_pairs={{0,2},{2,0},{4,6},{6,4},{8,10},{10,8},{12,14},{14,12},{1,3},{3,1},... | collective-permute-start | bytes 786440 | tf_op jit(solution)/shard_map/ppermute | solution.py:259
  63.9 2.6 %collective-permute-start.28 = (bf16[1,1,208,128]{3,2,1,0:T(8,128)(2,1)S(1)}, bf16[1,1,208,128]{3,2,1,0:T(8,128)(2,1)S(1)}, u32[]{:S(2)}, u32[]{:S(2)}) collective-permute-start(bf16[1,1,208,128]{3,2,1,0:T(8,128)(2,1)S(1)} %slice.306), channel_id=1, source_target_pairs={{0,8},{2,10},{4,12},{6,14},{8,0},{10,2},{12,4},{14,6},{1,9},{3,11}... | collective-permute-start | bytes 159752 | tf_op jit(solution)/shard_map/ppermute | solution.py:259
  66.5 0.4 collective-permute-start.24
  67.1 2.4 %collective-permute-start.23 = (bf16[1,16,4096]{2,1,0:T(8,128)(2,1)S(1)}, bf16[1,16,4096]{2,1,0:T(8,128)(2,1)S(1)}, u32[]{:S(2)}, u32[]{:S(2)}) collective-permute-start(bf16[1,16,4096]{2,1,0:T(8,128)(2,1)S(1)} %fusion.21), channel_id=1, source_target_pairs={{0,4},{2,6},{4,0},{6,2},{8,12},{10,14},{12,8},{14,10},{1,5},{3,7},... | collective-permute-start | bytes 393224 | tf_op jit(solution)/shard_map/ppermute | solution.py:259
  69.6 0.9 collective-permute-done.27
  70.5 1.0 collective-permute-start.29
  71.7 1.5 %shard_map.43 = (bf16[2,1,16,4096]{3,2,1,0:T(8,128)(2,1)S(1)}, f32[2,1,16,4096]{3,2,1,0:T(8,128)S(1)}) custom-call(s32[2]{0:T(128)S(1)} %pad_add_fusion.place_ref, f32[1,208,128]{2,1,0:T(8,128)S(1)} %slice_bitcast_fusion.13.refs_0_, bf16[1,208,128]{2,1,0:T(8,128)(2,1)S(1)} %bitcast.200, f32[1,208,128]{2,1,0:T(8,128)S(1)} %slice_bitcast_fusion.12.refs_2_, ...), custom_call_target="tpu_custom_call" | custom-call | flops 218103808 | bytes 3407872 | tf_op jit(solution)/shard_map/pallas_call | solution.py:231
  73.2 1.5 %shard_map.44 = (bf16[2,1,16,4096]{3,2,1,0:T(8,128)(2,1)S(1)}, f32[2,1,16,4096]{3,2,1,0:T(8,128)S(1)}) custom-call(s32[2]{0:T(128)S(1)} %pad_add_fusion.place_ref, f32[1,208,128]{2,1,0:T(8,128)S(1)} %slice_bitcast_fusion.13.refs_0_, bf16[1,208,128]{2,1,0:T(8,128)(2,1)S(1)} %bitcast.201, f32[1,208,128]{2,1,0:T(8,128)S(1)} %slice_bitcast_fusion.12.refs_2_, ...), custom_call_target="tpu_custom_call" | custom-call | flops 218103808 | bytes 3407872 | tf_op jit(solution)/shard_map/pallas_call | solution.py:231
  74.7 0.8 collective-permute-done.29
  75.6 1.1 collective-permute-start.33
  76.6 0.2 collective-permute-start.34
  76.9 1.3 %collective-permute-start.32 = (bf16[2,1,16,4096]{3,2,1,0:T(8,128)(2,1)S(1)}, bf16[2,1,16,4096]{3,2,1,0:T(8,128)(2,1)S(1)}, u32[]{:S(2)}, u32[]{:S(2)}) collective-permute-start(bf16[2,1,16,4096]{3,2,1,0:T(8,128)(2,1)S(1)} %get-tuple-element.133), channel_id=1, source_target_pairs={{0,2},{2,0},{4,6},{6,4},{8,10},{10,8},{12,14},{14,12},{1,3},{3,1},... | collective-permute-start | bytes 786440 | tf_op jit(solution)/shard_map/ppermute | solution.py:259
  78.2 1.5 %collective-permute-start.35 = (bf16[2,1,16,4096]{3,2,1,0:T(8,128)(2,1)S(1)}, bf16[2,1,16,4096]{3,2,1,0:T(8,128)(2,1)S(1)}, u32[]{:S(2)}, u32[]{:S(2)}) collective-permute-start(bf16[2,1,16,4096]{3,2,1,0:T(8,128)(2,1)S(1)} %get-tuple-element.134), channel_id=1, source_target_pairs={{0,4},{2,6},{4,0},{6,2},{8,12},{10,14},{12,8},{14,10},{1,5},{3,7},... | collective-permute-start | bytes 786440 | tf_op jit(solution)/shard_map/ppermute | solution.py:259
  79.8 0.8 collective-permute-start.31
  80.6 1.3 %collective-permute-done.33 = bf16[1,16,4096]{2,1,0:T(8,128)(2,1)S(1)} collective-permute-done((bf16[1,16,4096]{2,1,0:T(8,128)(2,1)S(1)}, bf16[1,16,4096]{2,1,0:T(8,128)(2,1)S(1)}, u32[]{:S(2)}, u32[]{:S(2)}) %collective-permute-start.33) | collective-permute-done | bytes 131104 | tf_op jit(solution)/shard_map/ppermute | solution.py:259
  81.9 3.9 %collective-permute-done.34 = bf16[1,16,4096]{2,1,0:T(8,128)(2,1)S(1)} collective-permute-done((bf16[1,16,4096]{2,1,0:T(8,128)(2,1)S(1)}, bf16[1,16,4096]{2,1,0:T(8,128)(2,1)S(1)}, u32[]{:S(2)}, u32[]{:S(2)}) %collective-permute-start.34) | collective-permute-done | bytes 131104 | tf_op jit(solution)/shard_map/ppermute | solution.py:259
  85.9 1.2 %collective-permute-done.32 = bf16[2,1,16,4096]{3,2,1,0:T(8,128)(2,1)S(1)} collective-permute-done((bf16[2,1,16,4096]{3,2,1,0:T(8,128)(2,1)S(1)}, bf16[2,1,16,4096]{3,2,1,0:T(8,128)(2,1)S(1)}, u32[]{:S(2)}, u32[]{:S(2)}) %collective-permute-start.32) | collective-permute-done | bytes 262176 | tf_op jit(solution)/shard_map/ppermute | solution.py:259
  87.2 3.5 %collective-permute-done.35 = bf16[2,1,16,4096]{3,2,1,0:T(8,128)(2,1)S(1)} collective-permute-done((bf16[2,1,16,4096]{3,2,1,0:T(8,128)(2,1)S(1)}, bf16[2,1,16,4096]{3,2,1,0:T(8,128)(2,1)S(1)}, u32[]{:S(2)}, u32[]{:S(2)}) %collective-permute-start.35) | collective-permute-done | bytes 262176 | tf_op jit(solution)/shard_map/ppermute | solution.py:259
  90.7 1.1 collective-permute-start.38
  91.9 2.8 %collective-permute-start.37 = (bf16[16,4096]{1,0:T(8,128)(2,1)S(1)}, bf16[16,4096]{1,0:T(8,128)(2,1)S(1)}, u32[]{:S(2)}, u32[]{:S(2)}) collective-permute-start(bf16[16,4096]{1,0:T(8,128)(2,1)S(1)} %get-tuple-element.153), channel_id=1, source_target_pairs={{0,8},{2,10},{4,12},{6,14},{8,0},{10,2},{12,4},{14,6},{1,9},{3,11}... | collective-permute-start | bytes 393224 | tf_op jit(solution)/shard_map/ppermute | solution.py:259
  94.7 1.0 collective-permute-done.38
  95.8 2.9 %collective-permute-done.39 = bf16[1,16,4096]{2,1,0:T(8,128)(2,1)S(1)} collective-permute-done((bf16[1,16,4096]{2,1,0:T(8,128)(2,1)S(1)}, bf16[1,16,4096]{2,1,0:T(8,128)(2,1)S(1)}, u32[]{:S(2)}, u32[]{:S(2)}) %collective-permute-start.39) | collective-permute-done | bytes 131104 | tf_op jit(solution)/shard_map/ppermute | solution.py:259
  98.9 1.4 %collective-permute-done.37 = bf16[16,4096]{1,0:T(8,128)(2,1)S(1)} collective-permute-done((bf16[16,4096]{1,0:T(8,128)(2,1)S(1)}, bf16[16,4096]{1,0:T(8,128)(2,1)S(1)}, u32[]{:S(2)}, u32[]{:S(2)}) %collective-permute-start.37) | collective-permute-done | bytes 131104 | tf_op jit(solution)/shard_map/ppermute | solution.py:259
  100.4 0.3 collective-permute-start.41
  100.8 8.0 %collective-permute-done.41 = bf16[16,4096]{1,0:T(8,128)(2,1)S(1)} collective-permute-done((bf16[16,4096]{1,0:T(8,128)(2,1)S(1)}, bf16[16,4096]{1,0:T(8,128)(2,1)S(1)}, u32[]{:S(2)}, u32[]{:S(2)}) %collective-permute-start.41) | collective-permute-done | bytes 131104 | tf_op jit(solution)/shard_map/ppermute | solution.py:259
  108.8 0.8 pad_maximum_fusion
  (84 shorter events, 2.0 us)
Async XLA Ops:
  0.0 12.1 %collective-permute-start.4 = (bf16[2,512,3328]{2,1,0:T(8,128)(2,1)}, bf16[2,512,3328]{2,1,0:T(8,128)(2,1)}, u32[]{:S(2)}, u32[]{:S(2)}) collective-permute-start(bf16[2,512,3328]{2,1,0:T(8,128)(2,1)} %refs_4_.7), channel_id=1, source_target_pairs={{0,1},{1,0},{2,3},{3,2},{4,5},{5,4},{6,7},{7,6},{8,9},{9,8},{10,11... | collective-permute-start | bytes 20447240 | tf_op jit(solution)/shard_map/ppermute | solution.py:263
  0.5 1.0 copy-start.1
  2.1 6.2 %collective-permute-start = (bf16[48,1024]{1,0:T(8,128)(2,1)S(1)}, bf16[48,1024]{1,0:T(8,128)(2,1)S(1)}, u32[]{:S(2)}, u32[]{:S(2)}) collective-permute-start(bf16[48,1024]{1,0:T(8,128)(2,1)S(1)} %get-tuple-element.82), channel_id=1, source_target_pairs={{0,0},{1,8},{2,2},{3,10},{4,4},{5,12},{6,6},{7,14},{8,1},{9,9},{10... | collective-permute-start | bytes 294920 | tf_op jit(solution)/shard_map/ppermute | solution.py:287
  2.8 6.2 %collective-permute-start.1 = (bf16[48,1024]{1,0:T(8,128)(2,1)S(1)}, bf16[48,1024]{1,0:T(8,128)(2,1)S(1)}, u32[]{:S(2)}, u32[]{:S(2)}) collective-permute-start(bf16[48,1024]{1,0:T(8,128)(2,1)S(1)} %get-tuple-element.83), channel_id=1, source_target_pairs={{0,2},{1,10},{2,4},{3,12},{4,6},{5,14},{6,0},{7,8},{8,3},{9,11},{1... | collective-permute-start | bytes 294920 | tf_op jit(solution)/shard_map/ppermute | solution.py:287
  5.3 5.7 %collective-permute-start.2 = (bf16[48,1024]{1,0:T(8,128)(2,1)S(1)}, bf16[48,1024]{1,0:T(8,128)(2,1)S(1)}, u32[]{:S(2)}, u32[]{:S(2)}) collective-permute-start(bf16[48,1024]{1,0:T(8,128)(2,1)S(1)} %get-tuple-element.84), channel_id=1, source_target_pairs={{0,4},{1,12},{2,6},{3,14},{4,0},{5,8},{6,2},{7,10},{8,5},{9,13},{1... | collective-permute-start | bytes 294920 | tf_op jit(solution)/shard_map/ppermute | solution.py:287
  6.9 16.3 %copy-start = (bf16[208,8192]{1,0:T(8,128)(2,1)S(1)}, bf16[208,8192]{1,0:T(8,128)(2,1)}, u32[]{:S(2)}) copy-start(bf16[208,8192]{1,0:T(8,128)(2,1)} %refs_4_.13) | copy-start | bytes 10223620
  6.9 5.2 %collective-permute-start.3 = (bf16[48,1024]{1,0:T(8,128)(2,1)S(1)}, bf16[48,1024]{1,0:T(8,128)(2,1)S(1)}, u32[]{:S(2)}, u32[]{:S(2)}) collective-permute-start(bf16[48,1024]{1,0:T(8,128)(2,1)S(1)} %get-tuple-element.85), channel_id=1, source_target_pairs={{0,6},{1,14},{2,0},{3,8},{4,2},{5,10},{6,4},{7,12},{8,7},{9,15},{1... | collective-permute-start | bytes 294920 | tf_op jit(solution)/shard_map/ppermute | solution.py:287
  19.1 10.8 %collective-permute-start.9 = (bf16[2,2,1,208,128]{4,3,1,2,0:T(8,128)(2,1)S(1)}, bf16[2,2,1,208,128]{4,3,1,2,0:T(8,128)(2,1)S(1)}, u32[]{:S(2)}, u32[]{:S(2)}) collective-permute-start(bf16[2,2,1,208,128]{4,3,1,2,0:T(8,128)(2,1)S(1)} %bitcast.207), channel_id=1, source_target_pairs={{0,4},{2,6},{4,0},{6,2},{8,12},{10,14},{12,8},{14,10},{1,5},{3,7},... | collective-permute-start | bytes 638984 | tf_op jit(solution)/shard_map/ppermute | solution.py:259
  21.3 8.6 %collective-permute-start.5 = (bf16[2,2,1,208,128]{4,3,1,2,0:T(8,128)(2,1)S(1)}, bf16[2,2,1,208,128]{4,3,1,2,0:T(8,128)(2,1)S(1)}, u32[]{:S(2)}, u32[]{:S(2)}) collective-permute-start(bf16[2,2,1,208,128]{4,3,1,2,0:T(8,128)(2,1)S(1)} %bitcast.206), channel_id=1, source_target_pairs={{0,2},{2,0},{4,6},{6,4},{8,10},{10,8},{12,14},{14,12},{1,3},{3,1},... | collective-permute-start | bytes 638984 | tf_op jit(solution)/shard_map/ppermute | solution.py:259
  23.2 30.2 %collective-permute-start.17 = (bf16[208,8192]{1,0:T(8,128)(2,1)S(1)}, bf16[208,8192]{1,0:T(8,128)(2,1)S(1)}, u32[]{:S(2)}, u32[]{:S(2)}) collective-permute-start(bf16[208,8192]{1,0:T(8,128)(2,1)S(1)} %copy-done), channel_id=1, source_target_pairs={{0,1},{1,0},{2,3},{3,2},{4,5},{5,4},{6,7},{7,6},{8,9},{9,8},{10,11... | collective-permute-start | bytes 10223624 | tf_op jit(solution)/shard_map/ppermute | solution.py:263
  27.5 8.2 %collective-permute-start.10 = (bf16[2,2,1,208,128]{4,3,1,2,0:T(8,128)(2,1)S(1)}, bf16[2,2,1,208,128]{4,3,1,2,0:T(8,128)(2,1)S(1)}, u32[]{:S(2)}, u32[]{:S(2)}) collective-permute-start(bf16[2,2,1,208,128]{4,3,1,2,0:T(8,128)(2,1)S(1)} %bitcast.205), channel_id=1, source_target_pairs={{0,4},{2,6},{4,0},{6,2},{8,12},{10,14},{12,8},{14,10},{1,5},{3,7},... | collective-permute-start | bytes 638984 | tf_op jit(solution)/shard_map/ppermute | solution.py:259
  28.2 8.2 %collective-permute-start.8 = (bf16[2,2,1,208,128]{4,3,1,2,0:T(8,128)(2,1)S(1)}, bf16[2,2,1,208,128]{4,3,1,2,0:T(8,128)(2,1)S(1)}, u32[]{:S(2)}, u32[]{:S(2)}) collective-permute-start(bf16[2,2,1,208,128]{4,3,1,2,0:T(8,128)(2,1)S(1)} %bitcast.204), channel_id=1, source_target_pairs={{0,2},{2,0},{4,6},{6,4},{8,10},{10,8},{12,14},{14,12},{1,3},{3,1},... | collective-permute-start | bytes 638984 | tf_op jit(solution)/shard_map/ppermute | solution.py:259
  30.0 8.6 %collective-permute-start.13 = (bf16[2,1,208,128]{3,2,1,0:T(8,128)(2,1)S(1)}, bf16[2,1,208,128]{3,2,1,0:T(8,128)(2,1)S(1)}, u32[]{:S(2)}, u32[]{:S(2)}) collective-permute-start(bf16[2,1,208,128]{3,2,1,0:T(8,128)(2,1)S(1)} %get-tuple-element.158), channel_id=1, source_target_pairs={{0,2},{2,0},{4,6},{6,4},{8,10},{10,8},{12,14},{14,12},{1,3},{3,1},... | collective-permute-start | bytes 319496 | tf_op jit(solution)/shard_map/ppermute | solution.py:259
  30.4 9.9 %collective-permute-start.6 = (bf16[2,1,208,128]{3,2,1,0:T(8,128)(2,1)S(1)}, bf16[2,1,208,128]{3,2,1,0:T(8,128)(2,1)S(1)}, u32[]{:S(2)}, u32[]{:S(2)}) collective-permute-start(bf16[2,1,208,128]{3,2,1,0:T(8,128)(2,1)S(1)} %get-tuple-element.157), channel_id=1, source_target_pairs={{0,4},{2,6},{4,0},{6,2},{8,12},{10,14},{12,8},{14,10},{1,5},{3,7},... | collective-permute-start | bytes 319496 | tf_op jit(solution)/shard_map/ppermute | solution.py:259
  36.4 4.8 %collective-permute-start.14 = (bf16[2,1,208,128]{3,2,1,0:T(8,128)(2,1)S(1)}, bf16[2,1,208,128]{3,2,1,0:T(8,128)(2,1)S(1)}, u32[]{:S(2)}, u32[]{:S(2)}) collective-permute-start(bf16[2,1,208,128]{3,2,1,0:T(8,128)(2,1)S(1)} %fusion.30), channel_id=1, source_target_pairs={{0,2},{2,0},{4,6},{6,4},{8,10},{10,8},{12,14},{14,12},{1,3},{3,1},... | collective-permute-start | bytes 319496 | tf_op jit(solution)/shard_map/ppermute | solution.py:259
  38.2 9.0 %collective-permute-start.12 = (bf16[2,1,208,128]{3,2,1,0:T(8,128)(2,1)S(1)}, bf16[2,1,208,128]{3,2,1,0:T(8,128)(2,1)S(1)}, u32[]{:S(2)}, u32[]{:S(2)}) collective-permute-start(bf16[2,1,208,128]{3,2,1,0:T(8,128)(2,1)S(1)} %fusion.29), channel_id=1, source_target_pairs={{0,4},{2,6},{4,0},{6,2},{8,12},{10,14},{12,8},{14,10},{1,5},{3,7},... | collective-permute-start | bytes 319496 | tf_op jit(solution)/shard_map/ppermute | solution.py:259
  38.6 8.9 %collective-permute-start.15 = (bf16[2,2,1,208,128]{4,3,1,2,0:T(8,128)(2,1)S(1)}, bf16[2,2,1,208,128]{4,3,1,2,0:T(8,128)(2,1)S(1)}, u32[]{:S(2)}, u32[]{:S(2)}) collective-permute-start(bf16[2,2,1,208,128]{4,3,1,2,0:T(8,128)(2,1)S(1)} %bitcast.203), channel_id=1, source_target_pairs={{0,4},{2,6},{4,0},{6,2},{8,12},{10,14},{12,8},{14,10},{1,5},{3,7},... | collective-permute-start | bytes 638984 | tf_op jit(solution)/shard_map/ppermute | solution.py:259
  40.3 10.2 %collective-permute-start.11 = (bf16[2,2,1,208,128]{4,3,1,2,0:T(8,128)(2,1)S(1)}, bf16[2,2,1,208,128]{4,3,1,2,0:T(8,128)(2,1)S(1)}, u32[]{:S(2)}, u32[]{:S(2)}) collective-permute-start(bf16[2,2,1,208,128]{4,3,1,2,0:T(8,128)(2,1)S(1)} %bitcast.202), channel_id=1, source_target_pairs={{0,2},{2,0},{4,6},{6,4},{8,10},{10,8},{12,14},{14,12},{1,3},{3,1},... | collective-permute-start | bytes 638984 | tf_op jit(solution)/shard_map/ppermute | solution.py:259
  41.2 9.4 %collective-permute-start.16 = (bf16[1,1,208,128]{3,2,1,0:T(8,128)(2,1)S(1)}, bf16[1,1,208,128]{3,2,1,0:T(8,128)(2,1)S(1)}, u32[]{:S(2)}, u32[]{:S(2)}) collective-permute-start(bf16[1,1,208,128]{3,2,1,0:T(8,128)(2,1)S(1)} %slice.310), channel_id=1, source_target_pairs={{0,8},{2,10},{4,12},{6,14},{8,0},{10,2},{12,4},{14,6},{1,9},{3,11}... | collective-permute-start | bytes 159752 | tf_op jit(solution)/shard_map/ppermute | solution.py:259
  47.2 6.1 %collective-permute-start.7 = (bf16[1,1,208,128]{3,2,1,0:T(8,128)(2,1)S(1)}, bf16[1,1,208,128]{3,2,1,0:T(8,128)(2,1)S(1)}, u32[]{:S(2)}, u32[]{:S(2)}) collective-permute-start(bf16[1,1,208,128]{3,2,1,0:T(8,128)(2,1)S(1)} %slice.311), channel_id=1, source_target_pairs={{0,8},{2,10},{4,12},{6,14},{8,0},{10,2},{12,4},{14,6},{1,9},{3,11}... | collective-permute-start | bytes 159752 | tf_op jit(solution)/shard_map/ppermute | solution.py:259
  47.4 11.0 %collective-permute-start.21 = (bf16[1,1,208,128]{3,2,1,0:T(8,128)(2,1)S(1)}, bf16[1,1,208,128]{3,2,1,0:T(8,128)(2,1)S(1)}, u32[]{:S(2)}, u32[]{:S(2)}) collective-permute-start(bf16[1,1,208,128]{3,2,1,0:T(8,128)(2,1)S(1)} %slice.308), channel_id=1, source_target_pairs={{0,8},{2,10},{4,12},{6,14},{8,0},{10,2},{12,4},{14,6},{1,9},{3,11}... | collective-permute-start | bytes 159752 | tf_op jit(solution)/shard_map/ppermute | solution.py:259
  50.4 9.1 %collective-permute-start.20 = (bf16[1,1,208,128]{3,2,1,0:T(8,128)(2,1)S(1)}, bf16[1,1,208,128]{3,2,1,0:T(8,128)(2,1)S(1)}, u32[]{:S(2)}, u32[]{:S(2)}) collective-permute-start(bf16[1,1,208,128]{3,2,1,0:T(8,128)(2,1)S(1)} %slice.309), channel_id=1, source_target_pairs={{0,8},{2,10},{4,12},{6,14},{8,0},{10,2},{12,4},{14,6},{1,9},{3,11}... | collective-permute-start | bytes 159752 | tf_op jit(solution)/shard_map/ppermute | solution.py:259
  50.6 12.0 %collective-permute-start.22 = (bf16[2,1,208,128]{3,2,1,0:T(8,128)(2,1)S(1)}, bf16[2,1,208,128]{3,2,1,0:T(8,128)(2,1)S(1)}, u32[]{:S(2)}, u32[]{:S(2)}) collective-permute-start(bf16[2,1,208,128]{3,2,1,0:T(8,128)(2,1)S(1)} %fusion.32), channel_id=1, source_target_pairs={{0,2},{2,0},{4,6},{6,4},{8,10},{10,8},{12,14},{14,12},{1,3},{3,1},... | collective-permute-start | bytes 319496 | tf_op jit(solution)/shard_map/ppermute | solution.py:259
  53.3 10.4 %collective-permute-start.19 = (bf16[2,1,208,128]{3,2,1,0:T(8,128)(2,1)S(1)}, bf16[2,1,208,128]{3,2,1,0:T(8,128)(2,1)S(1)}, u32[]{:S(2)}, u32[]{:S(2)}) collective-permute-start(bf16[2,1,208,128]{3,2,1,0:T(8,128)(2,1)S(1)} %fusion.31), channel_id=1, source_target_pairs={{0,4},{2,6},{4,0},{6,2},{8,12},{10,14},{12,8},{14,10},{1,5},{3,7},... | collective-permute-start | bytes 319496 | tf_op jit(solution)/shard_map/ppermute | solution.py:259
  54.9 11.6 %collective-permute-start.26 = (bf16[2,1,16,4096]{3,2,1,0:T(8,128)(2,1)S(1)}, bf16[2,1,16,4096]{3,2,1,0:T(8,128)(2,1)S(1)}, u32[]{:S(2)}, u32[]{:S(2)}) collective-permute-start(bf16[2,1,16,4096]{3,2,1,0:T(8,128)(2,1)S(1)} %get-tuple-element.117), channel_id=1, source_target_pairs={{0,4},{2,6},{4,0},{6,2},{8,12},{10,14},{12,8},{14,10},{1,5},{3,7},... | collective-permute-start | bytes 786440 | tf_op jit(solution)/shard_map/ppermute | solution.py:259
  58.4 8.6 %collective-permute-start.18 = (bf16[2,1,16,4096]{3,2,1,0:T(8,128)(2,1)S(1)}, bf16[2,1,16,4096]{3,2,1,0:T(8,128)(2,1)S(1)}, u32[]{:S(2)}, u32[]{:S(2)}) collective-permute-start(bf16[2,1,16,4096]{3,2,1,0:T(8,128)(2,1)S(1)} %get-tuple-element.116), channel_id=1, source_target_pairs={{0,2},{2,0},{4,6},{6,4},{8,10},{10,8},{12,14},{14,12},{1,3},{3,1},... | collective-permute-start | bytes 786440 | tf_op jit(solution)/shard_map/ppermute | solution.py:259
  61.0 9.5 %collective-permute-start.27 = (bf16[2,1,16,4096]{3,2,1,0:T(8,128)(2,1)S(1)}, bf16[2,1,16,4096]{3,2,1,0:T(8,128)(2,1)S(1)}, u32[]{:S(2)}, u32[]{:S(2)}) collective-permute-start(bf16[2,1,16,4096]{3,2,1,0:T(8,128)(2,1)S(1)} %get-tuple-element.121), channel_id=1, source_target_pairs={{0,4},{2,6},{4,0},{6,2},{8,12},{10,14},{12,8},{14,10},{1,5},{3,7},... | collective-permute-start | bytes 786440 | tf_op jit(solution)/shard_map/ppermute | solution.py:259
  62.7 8.9 %collective-permute-start.25 = (bf16[2,1,16,4096]{3,2,1,0:T(8,128)(2,1)S(1)}, bf16[2,1,16,4096]{3,2,1,0:T(8,128)(2,1)S(1)}, u32[]{:S(2)}, u32[]{:S(2)}) collective-permute-start(bf16[2,1,16,4096]{3,2,1,0:T(8,128)(2,1)S(1)} %get-tuple-element.120), channel_id=1, source_target_pairs={{0,2},{2,0},{4,6},{6,4},{8,10},{10,8},{12,14},{14,12},{1,3},{3,1},... | collective-permute-start | bytes 786440 | tf_op jit(solution)/shard_map/ppermute | solution.py:259
  63.9 7.8 %collective-permute-start.28 = (bf16[1,1,208,128]{3,2,1,0:T(8,128)(2,1)S(1)}, bf16[1,1,208,128]{3,2,1,0:T(8,128)(2,1)S(1)}, u32[]{:S(2)}, u32[]{:S(2)}) collective-permute-start(bf16[1,1,208,128]{3,2,1,0:T(8,128)(2,1)S(1)} %slice.306), channel_id=1, source_target_pairs={{0,8},{2,10},{4,12},{6,14},{8,0},{10,2},{12,4},{14,6},{1,9},{3,11}... | collective-permute-start | bytes 159752 | tf_op jit(solution)/shard_map/ppermute | solution.py:259
  66.5 5.2 %collective-permute-start.24 = (bf16[1,1,208,128]{3,2,1,0:T(8,128)(2,1)S(1)}, bf16[1,1,208,128]{3,2,1,0:T(8,128)(2,1)S(1)}, u32[]{:S(2)}, u32[]{:S(2)}) collective-permute-start(bf16[1,1,208,128]{3,2,1,0:T(8,128)(2,1)S(1)} %slice.307), channel_id=1, source_target_pairs={{0,8},{2,10},{4,12},{6,14},{8,0},{10,2},{12,4},{14,6},{1,9},{3,11}... | collective-permute-start | bytes 159752 | tf_op jit(solution)/shard_map/ppermute | solution.py:259
  67.1 7.5 %collective-permute-start.23 = (bf16[1,16,4096]{2,1,0:T(8,128)(2,1)S(1)}, bf16[1,16,4096]{2,1,0:T(8,128)(2,1)S(1)}, u32[]{:S(2)}, u32[]{:S(2)}) collective-permute-start(bf16[1,16,4096]{2,1,0:T(8,128)(2,1)S(1)} %fusion.21), channel_id=1, source_target_pairs={{0,4},{2,6},{4,0},{6,2},{8,12},{10,14},{12,8},{14,10},{1,5},{3,7},... | collective-permute-start | bytes 393224 | tf_op jit(solution)/shard_map/ppermute | solution.py:259
  70.5 5.0 %collective-permute-start.29 = (bf16[1,16,4096]{2,1,0:T(8,128)(2,1)S(1)}, bf16[1,16,4096]{2,1,0:T(8,128)(2,1)S(1)}, u32[]{:S(2)}, u32[]{:S(2)}) collective-permute-start(bf16[1,16,4096]{2,1,0:T(8,128)(2,1)S(1)} %fusion.22), channel_id=1, source_target_pairs={{0,2},{2,0},{4,6},{6,4},{8,10},{10,8},{12,14},{14,12},{1,3},{3,1},... | collective-permute-start | bytes 393224 | tf_op jit(solution)/shard_map/ppermute | solution.py:259
  75.5 4.2 %collective-permute-start.30 = (f32[16,4096]{1,0:T(8,128)S(1)}, f32[16,4096]{1,0:T(8,128)S(1)}, u32[]{:S(2)}, u32[]{:S(2)}) collective-permute-start(f32[16,4096]{1,0:T(8,128)S(1)} %fusion.12), channel_id=1, source_target_pairs={{0,1},{1,0},{2,3},{3,2},{4,5},{5,4},{6,7},{7,6},{8,9},{9,8},{10,11... | collective-permute-start | bytes 786440 | tf_op jit(solution)/shard_map/ppermute | solution.py:263
  75.6 6.4 %collective-permute-start.33 = (bf16[1,16,4096]{2,1,0:T(8,128)(2,1)S(1)}, bf16[1,16,4096]{2,1,0:T(8,128)(2,1)S(1)}, u32[]{:S(2)}, u32[]{:S(2)}) collective-permute-start(bf16[1,16,4096]{2,1,0:T(8,128)(2,1)S(1)} %fusion.24), channel_id=1, source_target_pairs={{0,2},{2,0},{4,6},{6,4},{8,10},{10,8},{12,14},{14,12},{1,3},{3,1},... | collective-permute-start | bytes 393224 | tf_op jit(solution)/shard_map/ppermute | solution.py:259
  76.6 9.2 %collective-permute-start.34 = (bf16[1,16,4096]{2,1,0:T(8,128)(2,1)S(1)}, bf16[1,16,4096]{2,1,0:T(8,128)(2,1)S(1)}, u32[]{:S(2)}, u32[]{:S(2)}) collective-permute-start(bf16[1,16,4096]{2,1,0:T(8,128)(2,1)S(1)} %fusion.23), channel_id=1, source_target_pairs={{0,4},{2,6},{4,0},{6,2},{8,12},{10,14},{12,8},{14,10},{1,5},{3,7},... | collective-permute-start | bytes 393224 | tf_op jit(solution)/shard_map/ppermute | solution.py:259
  76.9 10.2 %collective-permute-start.32 = (bf16[2,1,16,4096]{3,2,1,0:T(8,128)(2,1)S(1)}, bf16[2,1,16,4096]{3,2,1,0:T(8,128)(2,1)S(1)}, u32[]{:S(2)}, u32[]{:S(2)}) collective-permute-start(bf16[2,1,16,4096]{3,2,1,0:T(8,128)(2,1)S(1)} %get-tuple-element.133), channel_id=1, source_target_pairs={{0,2},{2,0},{4,6},{6,4},{8,10},{10,8},{12,14},{14,12},{1,3},{3,1},... | collective-permute-start | bytes 786440 | tf_op jit(solution)/shard_map/ppermute | solution.py:259
  78.2 12.4 %collective-permute-start.35 = (bf16[2,1,16,4096]{3,2,1,0:T(8,128)(2,1)S(1)}, bf16[2,1,16,4096]{3,2,1,0:T(8,128)(2,1)S(1)}, u32[]{:S(2)}, u32[]{:S(2)}) collective-permute-start(bf16[2,1,16,4096]{3,2,1,0:T(8,128)(2,1)S(1)} %get-tuple-element.134), channel_id=1, source_target_pairs={{0,4},{2,6},{4,0},{6,2},{8,12},{10,14},{12,8},{14,10},{1,5},{3,7},... | collective-permute-start | bytes 786440 | tf_op jit(solution)/shard_map/ppermute | solution.py:259
  79.8 12.0 %collective-permute-start.31 = (bf16[16,4096]{1,0:T(8,128)(2,1)S(1)}, bf16[16,4096]{1,0:T(8,128)(2,1)S(1)}, u32[]{:S(2)}, u32[]{:S(2)}) collective-permute-start(bf16[16,4096]{1,0:T(8,128)(2,1)S(1)} %get-tuple-element.155), channel_id=1, source_target_pairs={{0,8},{2,10},{4,12},{6,14},{8,0},{10,2},{12,4},{14,6},{1,9},{3,11}... | collective-permute-start | bytes 393224 | tf_op jit(solution)/shard_map/ppermute | solution.py:259
  85.9 6.0 %collective-permute-start.36 = (f32[16,4096]{1,0:T(8,128)S(1)}, f32[16,4096]{1,0:T(8,128)S(1)}, u32[]{:S(2)}, u32[]{:S(2)}) collective-permute-start(f32[16,4096]{1,0:T(8,128)S(1)} %fusion.15), channel_id=1, source_target_pairs={{0,1},{1,0},{2,3},{3,2},{4,5},{5,4},{6,7},{7,6},{8,9},{9,8},{10,11... | collective-permute-start | bytes 786440 | tf_op jit(solution)/shard_map/ppermute | solution.py:263
  90.7 5.0 %collective-permute-start.38 = (bf16[1,16,4096]{2,1,0:T(8,128)(2,1)S(1)}, bf16[1,16,4096]{2,1,0:T(8,128)(2,1)S(1)}, u32[]{:S(2)}, u32[]{:S(2)}) collective-permute-start(bf16[1,16,4096]{2,1,0:T(8,128)(2,1)S(1)} %fusion.26), channel_id=1, source_target_pairs={{0,2},{2,0},{4,6},{6,4},{8,10},{10,8},{12,14},{14,12},{1,3},{3,1},... | collective-permute-start | bytes 393224 | tf_op jit(solution)/shard_map/ppermute | solution.py:259
  91.8 6.9 %collective-permute-start.39 = (bf16[1,16,4096]{2,1,0:T(8,128)(2,1)S(1)}, bf16[1,16,4096]{2,1,0:T(8,128)(2,1)S(1)}, u32[]{:S(2)}, u32[]{:S(2)}) collective-permute-start(bf16[1,16,4096]{2,1,0:T(8,128)(2,1)S(1)} %fusion.25), channel_id=1, source_target_pairs={{0,4},{2,6},{4,0},{6,2},{8,12},{10,14},{12,8},{14,10},{1,5},{3,7},... | collective-permute-start | bytes 393224 | tf_op jit(solution)/shard_map/ppermute | solution.py:259
  91.9 8.4 %collective-permute-start.37 = (bf16[16,4096]{1,0:T(8,128)(2,1)S(1)}, bf16[16,4096]{1,0:T(8,128)(2,1)S(1)}, u32[]{:S(2)}, u32[]{:S(2)}) collective-permute-start(bf16[16,4096]{1,0:T(8,128)(2,1)S(1)} %get-tuple-element.153), channel_id=1, source_target_pairs={{0,8},{2,10},{4,12},{6,14},{8,0},{10,2},{12,4},{14,6},{1,9},{3,11}... | collective-permute-start | bytes 393224 | tf_op jit(solution)/shard_map/ppermute | solution.py:259
  98.7 1.6 %collective-permute-start.40 = (f32[16,4096]{1,0:T(8,128)S(1)}, f32[16,4096]{1,0:T(8,128)S(1)}, u32[]{:S(2)}, u32[]{:S(2)}) collective-permute-start(f32[16,4096]{1,0:T(8,128)S(1)} %fusion.17), channel_id=1, source_target_pairs={{0,1},{1,0},{2,3},{3,2},{4,5},{5,4},{6,7},{7,6},{8,9},{9,8},{10,11... | collective-permute-start | bytes 786440 | tf_op jit(solution)/shard_map/ppermute | solution.py:263
  100.4 8.3 %collective-permute-start.41 = (bf16[16,4096]{1,0:T(8,128)(2,1)S(1)}, bf16[16,4096]{1,0:T(8,128)(2,1)S(1)}, u32[]{:S(2)}, u32[]{:S(2)}) collective-permute-start(bf16[16,4096]{1,0:T(8,128)(2,1)S(1)} %get-tuple-element.151), channel_id=1, source_target_pairs={{0,8},{2,10},{4,12},{6,14},{8,0},{10,2},{12,4},{14,6},{1,9},{3,11}... | collective-permute-start | bytes 393224 | tf_op jit(solution)/shard_map/ppermute | solution.py:259
